TPU v7x, 128 devices: a whole 4x4x4 slice. The times are simulated.
128 devices in a mesh: gx: 4 (over z), gy: 4 (over x), gz: 8 (over y, core).
Axes of the slice: x: 4, y: 4, z: 4, core: 2. Of those that a mesh axis runs over, the one named last changes fastest.
Arguments:
- field: float32 [4, 256, 512, 1024], P(None, 'gx', 'gz', 'gy'), may hold values from -6 to 6
- basis_two: float32 [1024, 64], P('gy'), may hold values from -0.1875 to 0.1875
- basis_three: float32 [512, 64], P('gz'), may hold values from -0.25 to 0.25
Outputs:
- projected: float32 [256, 16384], P('gx', ('gy', 'gz'))
- gram: float32 [256, 256], P('gx')
All inputs are finite; a program needn't handle non-finite values.
Results may differ from a plain program's by a relative error of at most 0.000071.
Values sent between devices are 32-bit elements; how exact they have to be, the bound alone decides.
No kernel may reach another device: no remote copies, remote signals or barrier semaphores. Data moves between devices by JAX's collectives and lax.ppermute only.
A program may use at most 128 MiB of HBM per device.

v0:
```python
import jax
import jax.numpy as jnp
from jax import lax
from jax.sharding import PartitionSpec as P

V = 4
R = 64


def body(field, basis_two, basis_three):
    highest = lax.Precision.HIGHEST
    rows = field.shape[1]
    first = jnp.einsum("vacb,bs->vacs", field, basis_two, precision=highest)
    core = jnp.einsum("vacs,ct->avst", first, basis_three, precision=highest)
    core = core.reshape(rows, -1)
    projected = lax.psum_scatter(core, ("gy", "gz"), scatter_dimension=1, tiled=True)
    partial_gram = jnp.dot(
        projected,
        lax.all_gather(projected, "gx", axis=0, tiled=True).T,
        precision=highest,
        preferred_element_type=jnp.float32,
    )
    gram = lax.psum(partial_gram, ("gy", "gz")) / jnp.float32(V * R * R)
    return (projected, gram)


def solution(mesh):
    placed = (P(None, "gx", "gz", "gy"), P("gy", None), P("gz", None))
    return jax.shard_map(
        body,
        mesh=mesh,
        in_specs=placed,
        out_specs=(P("gx", ("gy", "gz")), P("gx", None)),
        check_vma=False,
    )
```

profile of v0, /device:TPU:0, one launch (start us, length us, event | category | flops | bytes accessed | tf_op | source)
XLA Modules:
  0.0 256.1 jit_solution(17271692683134027216)
XLA Ops:
  7.2 0.0 copy-start
  7.2 0.0 copy-start.1
  7.2 0.0 reduce-scatter.2.cloned.1.call-start
  7.2 0.8 copy-done
  8.0 26.7 %fusion = f32[4,64,64,64]{2,3,1,0:T(8,128)S(1)} fusion(f32[4,64,64,256]{3,2,1,0:T(8,128)} %param.3, f32[256,64]{0,1:T(8,128)S(1)} %copy-done), kind=kOutput, calls=%fused_computation.1 | convolution fusion | flops 3221225472 | bytes 21037056 | tf_op jit(solution)/shard_map/vacb,bs->vacs/dot_general | solution.py:13
  34.7 0.0 copy-done.1
  34.7 7.8 %convolution_bitcast_fusion = f32[64,4,64,64]{3,2,0,1:T(8,128)S(1)} fusion(f32[4,64,64,64]{2,3,1,0:T(8,128)S(1)} %fusion, f32[64,64]{1,0:T(8,128)S(1)} %copy-done.1), kind=kOutput, calls=%fused_computation | convolution fusion | flops 805306368 | bytes 8404992 | tf_op jit(solution)/shard_map/vacs,ct->avst/dot_general | solution.py:14
  42.5 4.1 %copy.5 = f32[64,4,64,64]{3,2,1,0:T(8,128)} copy(f32[64,4,64,64]{3,2,0,1:T(8,128)S(1)} %convolution_bitcast_fusion) | data formatting | bytes 8388608 | tf_op jit(solution)/shard_map/vacs,ct->avst/transpose | solution.py:14
  46.6 6.9 %reshape.7 = f32[64,16384]{1,0:T(8,128)} reshape(f32[64,4,64,64]{3,2,1,0:T(8,128)} %copy.5) | data formatting | bytes 8388608 | tf_op jit(solution)/shard_map/reshape | solution.py:15
  53.5 0.0 reduce-scatter.2.cloned.1.call-update
  53.5 0.0 all-reduce.2.cloned.1.call-start
  53.5 84.5 %reduce-scatter.2.cloned.1.call-done = f32[64,512]{1,0:T(8,128)} async-done(((f32[64,16384]{1,0:T(8,128)}), f32[64,512]{1,0:T(8,128)}) %reduce-scatter.2.cloned.1.call-update) | async-done | bytes 131088 | tf_op jit(solution)/shard_map/reduce_scatter | solution.py:16
  138.0 14.1 %all_gather.3 = f32[256,512]{1,0:T(8,128)S(1)} all-gather(f32[64,512]{1,0:T(8,128)} %reduce-scatter.2.cloned.1.call-done), channel_id=1, replica_groups=mesh['gx'=4,'gy'=4,'gz'=8] {'gx'}, dimensions={0}, use_global_device_ids=true | all-gather | bytes 655360 | tf_op jit(solution)/shard_map/all_gather | solution.py:19
  152.1 2.1 fusion.3
  154.3 0.0 all-reduce.2.cloned.1.call-update
  154.3 93.4 %all-reduce.2.cloned.1.call-done = f32[64,256]{1,0:T(8,128)} async-done(((f32[64,256]{1,0:T(8,128)}), f32[64,256]{1,0:T(8,128)}) %all-reduce.2.cloned.1.call-update) | async-done | bytes 65552 | tf_op jit(solution)/shard_map/psum | solution.py:23
  247.7 1.5 broadcast_multiply_fusion
Async XLA Ops:
  7.2 0.8 copy-start
  7.2 27.5 %copy-start.1 = (f32[64,64]{1,0:T(8,128)S(1)}, f32[64,64]{1,0:T(8,128)}, u32[]{:S(2)}) copy-start(f32[64,64]{1,0:T(8,128)} %param.5) | copy-start | bytes 49156
  7.2 130.8 %reduce-scatter.2.cloned.1.call-start = ((), (), s32[]{:S(2)}) async-start(), calls=%async_computation.1 | async-start | bytes 4325376 | tf_op jit(solution)/shard_map/reduce_scatter | solution.py:16
  53.5 194.3 %all-reduce.2.cloned.1.call-start = ((), (), s32[]{:S(2)}) async-start(), calls=%async_computation.2 | async-start | bytes 131072 | tf_op jit(solution)/shard_map/psum | solution.py:23
Sparse Core Ops, SparseCore 0:
  53.6 84.3 reduce-scatter.1
  154.4 93.2 all-reduce.1
where the time goes:
time: 257 us; the launch traced here: 256 us
  waiting for transfers between devices  178 us (69%)
  matrix products  36.6 us (14%)
  blocking collectives  14.1 us (5%)
  between operations  14.1 us (5%)
  local copies, waits for them, and re-layouts  11.8 us (5%)
    psum x1, waiting for transfers between devices, body(): gram = lax.psum(partial_gram, ('gy', 'gz')) / jnp.float32(V * R * R)  93.4 us
    reduce_scatter x1, waiting for transfers between devices, body(): lax.psum_scatter(core, ('gy', 'gz'), scatter_dimension=1, tiled=True)  84.5 us
    dot_general x1, matrix products, body(): first = jnp.einsum('vacb,bs->vacs', field, basis_two, precision=highest)  26.7 us
    all_gather x1, blocking collectives, body(): lax.all_gather(projected, 'gx', axis=0, tiled=True)  14.1 us
    dot_general x1, matrix products, body(): core = jnp.einsum('vacs,ct->avst', first, basis_three, precision=highest)  7.78 us
    reshape x1, local copies, waits for them, and re-layouts, body(): core = core.reshape(rows, -1)  6.89 us
  transfers between devices with their start and end apart: 2, of which 2 were waited for; matrix products, arithmetic and copies ran while one was open for 0% of the time, Pallas kernels for 0%

commit v1 on v0

v1 whole, which is shorter than its diff:
```python
import functools

import jax
import jax.numpy as jnp
from jax import lax
from jax.experimental import pallas as pl
from jax.experimental.pallas import tpu as pltpu
from jax.sharding import PartitionSpec as P

V = 4
R = 64
AXES = ("gx", "gy", "gz")
F32, BF16 = jnp.float32, jnp.bfloat16
STEP = 8


def split(x):
    hi = x.astype(BF16)
    return hi, (x - hi.astype(F32)).astype(BF16)


def dot(a, b, contract):
    return lax.dot_general(a, b, ((contract[:1], contract[1:]), ((), ())), preferred_element_type=F32)


def project_kernel(where, field, b2t, b3, mine, theirs, rows, w2, w3):
    @pl.when((pl.program_id(0) == 0) & (pl.program_id(1) == 0))
    def _():
        y, c = where[1], where[2]
        for other in range(2):
            for off in range(4):
                start = (lax.rem(y + off, 4) * 2 + lax.rem(c + other, 2)) * 8
                rows[pl.ds((other * 4 + off) * 8, 8), :] = b2t[pl.ds(pl.multiple_of(start, 8), 8), :]
        hi, lo = split(rows[...])
        w2[0:64, :] = hi
        w2[64:128, :] = lo
        wide = jnp.concatenate([b3[...]] * 4, axis=1)
        tall = jnp.concatenate([wide] * 4, axis=0)
        same = lax.broadcasted_iota(jnp.int32, (256, 256), 0) // 64 == lax.broadcasted_iota(jnp.int32, (256, 256), 1) // 64
        hi, lo = split(jnp.where(same, tall, 0.0))
        w3[0] = hi
        w3[1] = lo

    for q in range(STEP // 2):
        k = 2 * q
        x = jnp.concatenate([field[0, 0, k], field[0, 1, k], field[0, 0, k + 1], field[0, 1, k + 1]], axis=0)
        hi, lo = split(x)
        both = dot(w2[...], hi, (1, 1))
        first = both[:64] + both[64:] + dot(w2[0:64, :], lo, (1, 1))
        hi, lo = split(first)
        both = dot(jnp.concatenate([hi, lo], axis=0), w3[0], (1, 0))
        core = both[:64] + both[64:] + dot(hi, w3[1], (1, 0))
        lanes = slice(q * 256, (q + 1) * 256)
        mine[0, :, :, lanes] = core[:32].reshape(4, 8, 256)
        theirs[0, :, :, lanes] = core[32:].reshape(4, 8, 256)


def project(where, field, b2t, b3):
    steps = 32 // STEP
    part = jax.ShapeDtypeStruct((4, 4, 8, 4096), F32)
    part_spec = pl.BlockSpec((1, 4, 8, STEP * 128), lambda d, j, w: (d, 0, 0, j))
    return pl.pallas_call(
        project_kernel,
        out_shape=(part, part),
        grid_spec=pltpu.PrefetchScalarGridSpec(
            num_scalar_prefetch=1,
            grid=(4, steps),
            in_specs=[
                pl.BlockSpec((1, 2, STEP, 64, 256), lambda d, j, w: (lax.rem(w[0] + d, 4), 0, j, 0, 0)),
                pl.BlockSpec((64, 256), lambda d, j, w: (0, 0)),
                pl.BlockSpec((64, 64), lambda d, j, w: (0, 0)),
            ],
            out_specs=(part_spec, part_spec),
            scratch_shapes=[
                pltpu.VMEM((64, 256), F32),
                pltpu.VMEM((128, 256), BF16),
                pltpu.VMEM((2, 256, 256), BF16),
            ],
        ),
        compiler_params=pltpu.CompilerParams(vmem_limit_bytes=32 * 2**20),
        name="project",
    )(where, field, b2t, b3)


def add_kernel(where, *refs):
    for g in range(4):
        refs[8 + g][0] = refs[g][0, 0] + refs[4 + g][0, 0]


def add_groups(where, mine, received):
    def group(g):
        def index(h, w):
            swap = w[2]
            return (g + (h - g) * swap, h + (g - h) * swap, 0, 0)

        return pl.BlockSpec((1, 1, 8, 4096), index)

    return pl.pallas_call(
        add_kernel,
        out_shape=[jax.ShapeDtypeStruct((4, 8, 4096), F32)] * 4,
        grid_spec=pltpu.PrefetchScalarGridSpec(
            num_scalar_prefetch=1,
            grid=(4,),
            in_specs=[group(g) for g in range(4)] * 2,
            out_specs=[pl.BlockSpec((1, 8, 4096), lambda h, w: (h, 0, 0))] * 4,
        ),
        compiler_params=pltpu.CompilerParams(vmem_limit_bytes=32 * 2**20),
        name="add_cores",
    )(where, *([mine] * 4 + [received] * 4))


def sum_kernel(a, b, c, d, *outs):
    for h in range(4):
        outs[h][...] = (a[h] + b[h]) + (c[h] + d[h])


def sum_groups(parts):
    return pl.pallas_call(
        sum_kernel,
        out_shape=[jax.ShapeDtypeStruct((8, 4096), F32)] * 4,
        compiler_params=pltpu.CompilerParams(vmem_limit_bytes=32 * 2**20),
        name="sum_first_axis",
    )(*parts)


def finish_kernel(a, b, c, d, out, rows):
    total = (a[...] + b[...]) + (c[...] + d[...])
    for k in range(32):
        rows[:, k, :] = total[:, k * 128 : (k + 1) * 128]
    low = lax.broadcasted_iota(jnp.int32, (32, 128), 1) < 64
    for j in range(4):
        even, odd = rows[2 * j], rows[2 * j + 1]
        out[0:32, j * 128 : (j + 1) * 128] = jnp.where(low, even, pltpu.roll(odd, 64, 1))
        out[32:64, j * 128 : (j + 1) * 128] = jnp.where(low, pltpu.roll(even, 64, 1), odd)


def finish(parts):
    return pl.pallas_call(
        finish_kernel,
        out_shape=jax.ShapeDtypeStruct((64, 512), F32),
        scratch_shapes=[pltpu.VMEM((8, 32, 128), F32)],
        name="sum_second_axis",
    )(*parts)


def gram_kernel(z, a, b, c, d, out, cols):
    for off, ref in enumerate((a, b, c, d)):
        start = pl.multiple_of(lax.rem(z[0] + off, 4) * 64, 64)
        cols[pl.ds(start, 64), :] = ref[...]
    hi, lo = split(a[...])
    chi, clo = split(cols[...])
    both = dot(jnp.concatenate([hi, lo], axis=0), chi, (1, 1))
    out[...] = (both[:64] + both[64:] + dot(hi, clo, (1, 1))) * (1.0 / (V * R * R))


def gram_part(z, parts):
    return pl.pallas_call(
        gram_kernel,
        out_shape=jax.ShapeDtypeStruct((64, 256), F32),
        in_specs=[pl.BlockSpec(memory_space=pltpu.SMEM)] + [pl.BlockSpec(memory_space=pltpu.VMEM)] * 4,
        scratch_shapes=[pltpu.VMEM((256, 512), F32)],
        name="gram",
    )(z, *parts)


def pairs(target):
    out = []
    for z in range(4):
        for x in range(4):
            for y in range(4):
                for c in range(2):
                    tz, tx, ty, tc = target(z, x, y, c)
                    out.append((((z * 4 + x) * 4 + y) * 2 + c, (((tz % 4) * 4 + tx % 4) * 4 + ty % 4) * 2 + tc))
    return out


def send(x, target):
    return lax.ppermute(x, AXES, pairs(target))


def first_axis(off):
    return lambda z, x, y, c: (z, x + off * (1 - c), y + off * c, c)


def second_axis(off):
    return lambda z, x, y, c: (z, x + off * c, y + off * (1 - c), c)


def other_core(z, x, y, c):
    return (z, x, y, 1 - c)


def exchange(parts, axis):
    late = {off: send(parts[off], axis(off)) for off in (2, 1, 3)}
    return [parts[0], late[1], late[2], late[3]]


def total(x, axis):
    return sum(exchange([x] * 4, axis))


def body(field, basis_two, basis_three):
    z, x, gz = (lax.axis_index(a) for a in AXES)
    where = jnp.stack([x, gz // 2, gz % 2]).astype(jnp.int32)
    mine, theirs = project(where, field.reshape(4, 2, 32, 64, 256), basis_two.T, basis_three)
    groups = add_groups(where, mine, send(theirs, other_core))
    groups = sum_groups(exchange(groups, first_axis))
    projected = finish(exchange(groups, second_axis))
    rows = [projected] + [send(projected, lambda z, x, y, c, off=off: (z - off, x, y, c)) for off in (1, 2, 3)]
    part = gram_part(z.astype(jnp.int32).reshape(1), rows)
    part = part + send(part, other_core)
    gram = total(total(part, first_axis), second_axis)
    return (projected, gram)


def solution(mesh):
    placed = (P(None, "gx", "gz", "gy"), P("gy", None), P("gz", None))
    return jax.shard_map(
        body,
        mesh=mesh,
        in_specs=placed,
        out_specs=(P("gx", ("gy", "gz")), P("gx", None)),
        check_vma=False,
    )
```

time: 257 us -> 102 us (0.40)
  waiting for transfers between devices: 178 us -> 35.2 us
  matrix products: 36.6 us -> 0 us
  Pallas kernels: 0 us -> 28.5 us
  starting transfers between devices: 0.08 us -> 26.4 us
  blocking collectives: 14.1 us -> 0 us
  between operations: 14.1 us -> 0.72 us
    psum x1 -> x0, waiting for transfers between devices: 93.4 us -> none  [body(): gram = lax.psum(partial_gram, ('gy', 'gz')) / jnp.float32(V * R * R)]
    reduce_scatter x1 -> x0, waiting for transfers between devices: 84.5 us -> none  [body(): lax.psum_scatter(core, ('gy', 'gz'), scatter_dimension=1, tiled=True)]
    dot_general x3 -> x0, matrix products: 36.6 us -> none  [the longest x1 26.7 us: body(): first = jnp.einsum('vacb,bs->vacs', field, basis_two, precision=highest)]
    ppermute x0 -> x17, waiting for transfers between devices: none -> 35.2 us  [send(): return lax.ppermute(x, AXES, pairs(target))]
    pallas_call x0 -> x5, Pallas kernels: none -> 28.5 us  [the longest x1 23.5 us: project(): pl.pallas_call(project_kernel, out_shape=(part, part), grid_spec=pltpu.Pr...]
    ppermute x0 -> x17, starting transfers between devices: none -> 26.4 us  [send(): return lax.ppermute(x, AXES, pairs(target))]
    all_gather x1 -> x0, blocking collectives: 14.1 us -> none  [body(): lax.all_gather(projected, 'gx', axis=0, tiled=True)]
    unnamed x4 -> x20, local copies, waits for them, and re-layouts: 0.79 us -> 9.32 us
  transfers between devices with their start and end apart: 2 -> 17, of which waited for: 2 -> 16; matrix products, arithmetic and copies ran while one was open for 0% -> 0% of each run, Pallas kernels for 0% -> 0%
where the time goes in v1:
time: 102 us
  waiting for transfers between devices  35.2 us (35%)
  Pallas kernels  28.5 us (28%)
  starting transfers between devices  26.4 us (26%)
  local copies, waits for them, and re-layouts  9.32 us (9%)
  other arithmetic  1.59 us (2%)
    ppermute x17, waiting for transfers between devices, send(): return lax.ppermute(x, AXES, pairs(target))  35.2 us
    ppermute x17, starting transfers between devices, send(): return lax.ppermute(x, AXES, pairs(target))  26.4 us
    pallas_call x1, Pallas kernels, project(): pl.pallas_call(project_kernel, out_shape=(part, part), grid_spec=pltpu.Pr...  23.5 us
    unnamed x20, local copies, waits for them, and re-layouts  9.32 us
    pallas_call x1, Pallas kernels, gram_part(): pl.pallas_call(gram_kernel, out_shape=jax.ShapeDtypeStruct((64, 256), F32...  2.08 us
  transfers between devices with their start and end apart: 17, of which 16 were waited for; matrix products, arithmetic and copies ran while one was open for 0% of the time, Pallas kernels for 0%

profile of v1, /device:TPU:0, one launch (start us, length us, event | category | flops | bytes accessed | tf_op | source)
XLA Modules:
  0.0 101.7 jit_solution(18207197108922800661)
XLA Ops:
  0.6 0.1 pad_add_fusion.where
  0.7 5.8 %copy-done = f32[4,64,64,256]{3,2,1,0:T(8,128)S(1)} copy-done((f32[4,64,64,256]{3,2,1,0:T(8,128)S(1)}, f32[4,64,64,256]{3,2,1,0:T(8,128)}, u32[]{:S(2)}) %copy-start) | copy-done | bytes 16777240
  6.5 0.8 copy-done.2
  7.3 0.8 copy-done.3
  8.1 23.5 %project.1 = (f32[4,4,8,4096]{3,2,1,0:T(8,128)S(1)}, f32[4,4,8,4096]{3,2,1,0:T(8,128)S(1)}) custom-call(s32[3]{0:T(128)S(1)} %pad_add_fusion.where, f32[4,2,32,64,256]{4,3,2,1,0:T(8,128)S(1)} %bitcast.6, f32[64,256]{1,0:T(8,128)S(1)} %bitcast.7, f32[64,64]{1,0:T(8,128)S(1)} %copy-done.3), custom_call_target="tpu_custom_call" | custom-call | tf_op jit(solution)/shard_map/project/pallas_call | solution.py:62
  31.6 0.1 collective-permute-start
  31.7 4.1 %collective-permute-done.refs_4_.refs_5_.refs_6_.refs_7_ = f32[4,4,8,4096]{3,2,1,0:T(8,128)S(1)} collective-permute-done((f32[4,4,8,4096]{3,2,1,0:T(8,128)S(1)}, f32[4,4,8,4096]{3,2,1,0:T(8,128)S(1)}, u32[]{:S(2)}, u32[]{:S(2)}) %collective-permute-start) | collective-permute-done | bytes 2097184 | tf_op jit(solution)/shard_map/ppermute | solution.py:178
  35.8 0.9 add_cores.1
  36.7 1.6 %collective-permute-start.1 = (f32[4,8,4096]{2,1,0:T(8,128)S(1)}, f32[4,8,4096]{2,1,0:T(8,128)S(1)}, u32[]{:S(2)}, u32[]{:S(2)}) collective-permute-start(f32[4,8,4096]{2,1,0:T(8,128)S(1)} %get-tuple-element.15), channel_id=1, source_target_pairs={{0,8},{1,3},{2,10},{3,5},{4,12},{5,7},{6,14},{7,1},{8,16},{9,11},{... | collective-permute-start | bytes 1572872 | tf_op jit(solution)/shard_map/ppermute | solution.py:178
  38.3 2.7 %collective-permute-start.2 = (f32[4,8,4096]{2,1,0:T(8,128)S(1)}, f32[4,8,4096]{2,1,0:T(8,128)S(1)}, u32[]{:S(2)}, u32[]{:S(2)}) collective-permute-start(f32[4,8,4096]{2,1,0:T(8,128)S(1)} %get-tuple-element.16), channel_id=1, source_target_pairs={{0,16},{1,5},{2,18},{3,7},{4,20},{5,1},{6,22},{7,3},{8,24},{9,13},... | collective-permute-start | bytes 1572872 | tf_op jit(solution)/shard_map/ppermute | solution.py:178
  41.1 1.4 %collective-permute-start.3 = (f32[4,8,4096]{2,1,0:T(8,128)S(1)}, f32[4,8,4096]{2,1,0:T(8,128)S(1)}, u32[]{:S(2)}, u32[]{:S(2)}) collective-permute-start(f32[4,8,4096]{2,1,0:T(8,128)S(1)} %get-tuple-element.17), channel_id=1, source_target_pairs={{0,24},{1,7},{2,26},{3,1},{4,28},{5,3},{6,30},{7,5},{8,0},{9,15},{... | collective-permute-start | bytes 1572872 | tf_op jit(solution)/shard_map/ppermute | solution.py:178
  42.5 4.7 %collective-permute-done.1.b = f32[4,8,4096]{2,1,0:T(8,128)S(1)} collective-permute-done((f32[4,8,4096]{2,1,0:T(8,128)S(1)}, f32[4,8,4096]{2,1,0:T(8,128)S(1)}, u32[]{:S(2)}, u32[]{:S(2)}) %collective-permute-start.1) | collective-permute-done | bytes 524320 | tf_op jit(solution)/shard_map/ppermute | solution.py:178
  47.2 6.7 %collective-permute-done.2.c = f32[4,8,4096]{2,1,0:T(8,128)S(1)} collective-permute-done((f32[4,8,4096]{2,1,0:T(8,128)S(1)}, f32[4,8,4096]{2,1,0:T(8,128)S(1)}, u32[]{:S(2)}, u32[]{:S(2)}) %collective-permute-start.2) | collective-permute-done | bytes 524320 | tf_op jit(solution)/shard_map/ppermute | solution.py:178
  53.8 0.1 sum_first_axis.1
  54.0 0.6 copy-done.1
  54.6 1.6 %collective-permute-start.4 = (f32[8,4096]{1,0:T(8,128)S(1)}, f32[8,4096]{1,0:T(8,128)S(1)}, u32[]{:S(2)}, u32[]{:S(2)}) collective-permute-start(f32[8,4096]{1,0:T(8,128)S(1)} %get-tuple-element.19), channel_id=1, source_target_pairs={{0,2},{1,9},{2,4},{3,11},{4,6},{5,13},{6,0},{7,15},{8,10},{9,17},{... | collective-permute-start | bytes 393224 | tf_op jit(solution)/shard_map/ppermute | solution.py:178
  56.2 2.9 %collective-permute-start.5 = (f32[8,4096]{1,0:T(8,128)S(1)}, f32[8,4096]{1,0:T(8,128)S(1)}, u32[]{:S(2)}, u32[]{:S(2)}) collective-permute-start(f32[8,4096]{1,0:T(8,128)S(1)} %get-tuple-element.20), channel_id=1, source_target_pairs={{0,4},{1,17},{2,6},{3,19},{4,0},{5,21},{6,2},{7,23},{8,12},{9,25},... | collective-permute-start | bytes 393224 | tf_op jit(solution)/shard_map/ppermute | solution.py:178
  59.1 1.3 %collective-permute-start.6 = (f32[8,4096]{1,0:T(8,128)S(1)}, f32[8,4096]{1,0:T(8,128)S(1)}, u32[]{:S(2)}, u32[]{:S(2)}) collective-permute-start(f32[8,4096]{1,0:T(8,128)S(1)} %get-tuple-element.21), channel_id=1, source_target_pairs={{0,6},{1,25},{2,0},{3,27},{4,2},{5,29},{6,4},{7,31},{8,14},{9,1},{... | collective-permute-start | bytes 393224 | tf_op jit(solution)/shard_map/ppermute | solution.py:178
  60.4 0.4 collective-permute-done.4.b
  60.8 2.6 %collective-permute-done.5.c = f32[8,4096]{1,0:T(8,128)S(1)} collective-permute-done((f32[8,4096]{1,0:T(8,128)S(1)}, f32[8,4096]{1,0:T(8,128)S(1)}, u32[]{:S(2)}, u32[]{:S(2)}) %collective-permute-start.5) | collective-permute-done | bytes 131104 | tf_op jit(solution)/shard_map/ppermute | solution.py:178
  63.4 0.6 collective-permute-done.6.d
  64.0 0.0 copy-done.5
  64.1 0.6 copy-done.6
  64.7 2.0 %sum_second_axis.1.a = f32[64,512]{1,0:T(8,128)} custom-call(f32[8,4096]{1,0:T(8,128)} %copy-done.1, f32[8,4096]{1,0:T(8,128)} %copy-done.4, f32[8,4096]{1,0:T(8,128)} %copy-done.5, f32[8,4096]{1,0:T(8,128)} %copy-done.6), custom_call_target="tpu_custom_call" | custom-call | tf_op jit(solution)/shard_map/sum_second_axis/pallas_call | solution.py:138
  66.7 1.9 %collective-permute-start.9 = (f32[64,512]{1,0:T(8,128)}, f32[64,512]{1,0:T(8,128)S(1)}, u32[]{:S(2)}, u32[]{:S(2)}) collective-permute-start(f32[64,512]{1,0:T(8,128)} %sum_second_axis.1.a), channel_id=1, source_target_pairs={{0,32},{1,33},{2,34},{3,35},{4,36},{5,37},{6,38},{7,39},{8,40},{9,... | collective-permute-start | bytes 393224 | tf_op jit(solution)/shard_map/ppermute | solution.py:178
  68.6 3.6 %collective-permute-start.8 = (f32[64,512]{1,0:T(8,128)}, f32[64,512]{1,0:T(8,128)S(1)}, u32[]{:S(2)}, u32[]{:S(2)}) collective-permute-start(f32[64,512]{1,0:T(8,128)} %sum_second_axis.1.a), channel_id=1, source_target_pairs={{0,64},{1,65},{2,66},{3,67},{4,68},{5,69},{6,70},{7,71},{8,72},{9,... | collective-permute-start | bytes 393224 | tf_op jit(solution)/shard_map/ppermute | solution.py:178
  72.2 1.0 collective-permute-start.7
  73.2 1.3 %collective-permute-done.9.d = f32[64,512]{1,0:T(8,128)S(1)} collective-permute-done((f32[64,512]{1,0:T(8,128)}, f32[64,512]{1,0:T(8,128)S(1)}, u32[]{:S(2)}, u32[]{:S(2)}) %collective-permute-start.9) | collective-permute-done | bytes 131104 | tf_op jit(solution)/shard_map/ppermute | solution.py:178
  74.4 2.3 %collective-permute-done.8.c = f32[64,512]{1,0:T(8,128)S(1)} collective-permute-done((f32[64,512]{1,0:T(8,128)}, f32[64,512]{1,0:T(8,128)S(1)}, u32[]{:S(2)}, u32[]{:S(2)}) %collective-permute-start.8) | collective-permute-done | bytes 131104 | tf_op jit(solution)/shard_map/ppermute | solution.py:178
  76.7 0.6 collective-permute-done.7.b
  77.3 0.0 copy-done.8
  77.4 0.6 copy-done.9
  78.0 2.1 %gram.1 = f32[64,256]{1,0:T(8,128)} custom-call(s32[1]{0:T(128)} %bitcast.5.z, f32[64,512]{1,0:T(8,128)} %sum_second_axis.1.a, f32[64,512]{1,0:T(8,128)} %copy-done.9, f32[64,512]{1,0:T(8,128)} %copy-done.8, f32[64,512]{1,0:T(8,128)} %copy-done.7), custom_call_target="tpu_custom_call" | custom-call | tf_op jit(solution)/shard_map/gram/pallas_call | solution.py:157
  80.1 1.5 %collective-permute-done.10 = f32[64,256]{1,0:T(8,128)S(1)} collective-permute-done((f32[64,256]{1,0:T(8,128)}, f32[64,256]{1,0:T(8,128)S(1)}, u32[]{:S(2)}, u32[]{:S(2)}) %collective-permute-start.10) | collective-permute-done | bytes 65568 | tf_op jit(solution)/shard_map/ppermute | solution.py:178
  81.5 0.9 add.27
  82.4 2.6 %collective-permute-start.13 = (f32[64,256]{1,0:T(8,128)S(1)}, f32[64,256]{1,0:T(8,128)S(1)}, u32[]{:S(2)}, u32[]{:S(2)}) collective-permute-start(f32[64,256]{1,0:T(8,128)S(1)} %add.27), channel_id=1, source_target_pairs={{0,24},{1,7},{2,26},{3,1},{4,28},{5,3},{6,30},{7,5},{8,0},{9,15},{... | collective-permute-start | bytes 196616 | tf_op jit(solution)/shard_map/ppermute | solution.py:178
  85.0 1.4 %collective-permute-start.12 = (f32[64,256]{1,0:T(8,128)S(1)}, f32[64,256]{1,0:T(8,128)S(1)}, u32[]{:S(2)}, u32[]{:S(2)}) collective-permute-start(f32[64,256]{1,0:T(8,128)S(1)} %add.27), channel_id=1, source_target_pairs={{0,16},{1,5},{2,18},{3,7},{4,20},{5,1},{6,22},{7,3},{8,24},{9,13},... | collective-permute-start | bytes 196616 | tf_op jit(solution)/shard_map/ppermute | solution.py:178
  86.4 0.4 collective-permute-start.11
  86.8 0.1 collective-permute-done.13
  86.9 3.9 %collective-permute-done.12 = f32[64,256]{1,0:T(8,128)S(1)} collective-permute-done((f32[64,256]{1,0:T(8,128)S(1)}, f32[64,256]{1,0:T(8,128)S(1)}, u32[]{:S(2)}, u32[]{:S(2)}) %collective-permute-start.12) | collective-permute-done | bytes 65568 | tf_op jit(solution)/shard_map/ppermute | solution.py:178
  90.8 1.1 %collective-permute-done.11 = f32[64,256]{1,0:T(8,128)S(1)} collective-permute-done((f32[64,256]{1,0:T(8,128)S(1)}, f32[64,256]{1,0:T(8,128)S(1)}, u32[]{:S(2)}, u32[]{:S(2)}) %collective-permute-start.11) | collective-permute-done | bytes 65568 | tf_op jit(solution)/shard_map/ppermute | solution.py:178
  91.9 2.6 %collective-permute-start.16 = (f32[64,256]{1,0:T(8,128)S(1)}, f32[64,256]{1,0:T(8,128)S(1)}, u32[]{:S(2)}, u32[]{:S(2)}) collective-permute-start(f32[64,256]{1,0:T(8,128)S(1)} %add_add_fusion.1), channel_id=1, source_target_pairs={{0,6},{1,25},{2,0},{3,27},{4,2},{5,29},{6,4},{7,31},{8,14},{9,1},{... | collective-permute-start | bytes 196616 | tf_op jit(solution)/shard_map/ppermute | solution.py:178
  94.5 0.5 collective-permute-start.15
  95.1 0.6 collective-permute-start.14
  95.6 0.8 collective-permute-done.16
  96.4 3.9 %collective-permute-done.15 = f32[64,256]{1,0:T(8,128)S(1)} collective-permute-done((f32[64,256]{1,0:T(8,128)S(1)}, f32[64,256]{1,0:T(8,128)S(1)}, u32[]{:S(2)}, u32[]{:S(2)}) %collective-permute-start.15) | collective-permute-done | bytes 65568 | tf_op jit(solution)/shard_map/ppermute | solution.py:178
  100.4 0.7 collective-permute-done.14
  101.0 0.6 add_add_fusion
  (15 shorter events, 0.0 us)
Async XLA Ops:
  0.7 5.8 %copy-start = (f32[4,64,64,256]{3,2,1,0:T(8,128)S(1)}, f32[4,64,64,256]{3,2,1,0:T(8,128)}, u32[]{:S(2)}) copy-start(f32[4,64,64,256]{3,2,1,0:T(8,128)} %param.3) | copy-start | bytes 50331652
  6.5 0.8 copy-start.2
  7.3 0.8 copy-start.3
  31.6 4.2 %collective-permute-start = (f32[4,4,8,4096]{3,2,1,0:T(8,128)S(1)}, f32[4,4,8,4096]{3,2,1,0:T(8,128)S(1)}, u32[]{:S(2)}, u32[]{:S(2)}) collective-permute-start(f32[4,4,8,4096]{3,2,1,0:T(8,128)S(1)} %get-tuple-element.13), channel_id=1, source_target_pairs={{0,1},{1,0},{2,3},{3,2},{4,5},{5,4},{6,7},{7,6},{8,9},{9,8},{10,11... | collective-permute-start | bytes 6291464 | tf_op jit(solution)/shard_map/ppermute | solution.py:178
  36.7 10.5 %collective-permute-start.1 = (f32[4,8,4096]{2,1,0:T(8,128)S(1)}, f32[4,8,4096]{2,1,0:T(8,128)S(1)}, u32[]{:S(2)}, u32[]{:S(2)}) collective-permute-start(f32[4,8,4096]{2,1,0:T(8,128)S(1)} %get-tuple-element.15), channel_id=1, source_target_pairs={{0,8},{1,3},{2,10},{3,5},{4,12},{5,7},{6,14},{7,1},{8,16},{9,11},{... | collective-permute-start | bytes 1572872 | tf_op jit(solution)/shard_map/ppermute | solution.py:178
  38.3 15.5 %collective-permute-start.2 = (f32[4,8,4096]{2,1,0:T(8,128)S(1)}, f32[4,8,4096]{2,1,0:T(8,128)S(1)}, u32[]{:S(2)}, u32[]{:S(2)}) collective-permute-start(f32[4,8,4096]{2,1,0:T(8,128)S(1)} %get-tuple-element.16), channel_id=1, source_target_pairs={{0,16},{1,5},{2,18},{3,7},{4,20},{5,1},{6,22},{7,3},{8,24},{9,13},... | collective-permute-start | bytes 1572872 | tf_op jit(solution)/shard_map/ppermute | solution.py:178
  41.1 12.8 %collective-permute-start.3 = (f32[4,8,4096]{2,1,0:T(8,128)S(1)}, f32[4,8,4096]{2,1,0:T(8,128)S(1)}, u32[]{:S(2)}, u32[]{:S(2)}) collective-permute-start(f32[4,8,4096]{2,1,0:T(8,128)S(1)} %get-tuple-element.17), channel_id=1, source_target_pairs={{0,24},{1,7},{2,26},{3,1},{4,28},{5,3},{6,30},{7,5},{8,0},{9,15},{... | collective-permute-start | bytes 1572872 | tf_op jit(solution)/shard_map/ppermute | solution.py:178
  53.9 0.7 copy-start.1
  54.6 6.2 %collective-permute-start.4 = (f32[8,4096]{1,0:T(8,128)S(1)}, f32[8,4096]{1,0:T(8,128)S(1)}, u32[]{:S(2)}, u32[]{:S(2)}) collective-permute-start(f32[8,4096]{1,0:T(8,128)S(1)} %get-tuple-element.19), channel_id=1, source_target_pairs={{0,2},{1,9},{2,4},{3,11},{4,6},{5,13},{6,0},{7,15},{8,10},{9,17},{... | collective-permute-start | bytes 393224 | tf_op jit(solution)/shard_map/ppermute | solution.py:178
  56.2 7.2 %collective-permute-start.5 = (f32[8,4096]{1,0:T(8,128)S(1)}, f32[8,4096]{1,0:T(8,128)S(1)}, u32[]{:S(2)}, u32[]{:S(2)}) collective-permute-start(f32[8,4096]{1,0:T(8,128)S(1)} %get-tuple-element.20), channel_id=1, source_target_pairs={{0,4},{1,17},{2,6},{3,19},{4,0},{5,21},{6,2},{7,23},{8,12},{9,25},... | collective-permute-start | bytes 393224 | tf_op jit(solution)/shard_map/ppermute | solution.py:178
  59.1 5.0 %collective-permute-start.6 = (f32[8,4096]{1,0:T(8,128)S(1)}, f32[8,4096]{1,0:T(8,128)S(1)}, u32[]{:S(2)}, u32[]{:S(2)}) collective-permute-start(f32[8,4096]{1,0:T(8,128)S(1)} %get-tuple-element.21), channel_id=1, source_target_pairs={{0,6},{1,25},{2,0},{3,27},{4,2},{5,29},{6,4},{7,31},{8,14},{9,1},{... | collective-permute-start | bytes 393224 | tf_op jit(solution)/shard_map/ppermute | solution.py:178
  60.8 3.3 %copy-start.4 = (f32[8,4096]{1,0:T(8,128)}, f32[8,4096]{1,0:T(8,128)S(1)}, u32[]{:S(2)}) copy-start(f32[8,4096]{1,0:T(8,128)S(1)} %collective-permute-done.4.b) | copy-start | bytes 393220
  63.4 0.6 copy-start.5
  64.0 0.7 copy-start.6
  66.7 7.8 %collective-permute-start.9 = (f32[64,512]{1,0:T(8,128)}, f32[64,512]{1,0:T(8,128)S(1)}, u32[]{:S(2)}, u32[]{:S(2)}) collective-permute-start(f32[64,512]{1,0:T(8,128)} %sum_second_axis.1.a), channel_id=1, source_target_pairs={{0,32},{1,33},{2,34},{3,35},{4,36},{5,37},{6,38},{7,39},{8,40},{9,... | collective-permute-start | bytes 393224 | tf_op jit(solution)/shard_map/ppermute | solution.py:178
  68.6 8.1 %collective-permute-start.8 = (f32[64,512]{1,0:T(8,128)}, f32[64,512]{1,0:T(8,128)S(1)}, u32[]{:S(2)}, u32[]{:S(2)}) collective-permute-start(f32[64,512]{1,0:T(8,128)} %sum_second_axis.1.a), channel_id=1, source_target_pairs={{0,64},{1,65},{2,66},{3,67},{4,68},{5,69},{6,70},{7,71},{8,72},{9,... | collective-permute-start | bytes 393224 | tf_op jit(solution)/shard_map/ppermute | solution.py:178
  72.2 5.2 %collective-permute-start.7 = (f32[64,512]{1,0:T(8,128)}, f32[64,512]{1,0:T(8,128)S(1)}, u32[]{:S(2)}, u32[]{:S(2)}) collective-permute-start(f32[64,512]{1,0:T(8,128)} %sum_second_axis.1.a), channel_id=1, source_target_pairs={{0,96},{1,97},{2,98},{3,99},{4,100},{5,101},{6,102},{7,103},{8,104... | collective-permute-start | bytes 393224 | tf_op jit(solution)/shard_map/ppermute | solution.py:178
  74.4 2.9 %copy-start.7 = (f32[64,512]{1,0:T(8,128)}, f32[64,512]{1,0:T(8,128)S(1)}, u32[]{:S(2)}) copy-start(f32[64,512]{1,0:T(8,128)S(1)} %collective-permute-done.9.d) | copy-start | bytes 393220
  76.7 0.6 copy-start.8
  77.3 0.7 copy-start.9
  80.1 1.5 %collective-permute-start.10 = (f32[64,256]{1,0:T(8,128)}, f32[64,256]{1,0:T(8,128)S(1)}, u32[]{:S(2)}, u32[]{:S(2)}) collective-permute-start(f32[64,256]{1,0:T(8,128)} %gram.1), channel_id=1, source_target_pairs={{0,1},{1,0},{2,3},{3,2},{4,5},{5,4},{6,7},{7,6},{8,9},{9,8},{10,11... | collective-permute-start | bytes 196616 | tf_op jit(solution)/shard_map/ppermute | solution.py:178
  82.4 4.5 %collective-permute-start.13 = (f32[64,256]{1,0:T(8,128)S(1)}, f32[64,256]{1,0:T(8,128)S(1)}, u32[]{:S(2)}, u32[]{:S(2)}) collective-permute-start(f32[64,256]{1,0:T(8,128)S(1)} %add.27), channel_id=1, source_target_pairs={{0,24},{1,7},{2,26},{3,1},{4,28},{5,3},{6,30},{7,5},{8,0},{9,15},{... | collective-permute-start | bytes 196616 | tf_op jit(solution)/shard_map/ppermute | solution.py:178
  85.0 5.8 %collective-permute-start.12 = (f32[64,256]{1,0:T(8,128)S(1)}, f32[64,256]{1,0:T(8,128)S(1)}, u32[]{:S(2)}, u32[]{:S(2)}) collective-permute-start(f32[64,256]{1,0:T(8,128)S(1)} %add.27), channel_id=1, source_target_pairs={{0,16},{1,5},{2,18},{3,7},{4,20},{5,1},{6,22},{7,3},{8,24},{9,13},... | collective-permute-start | bytes 196616 | tf_op jit(solution)/shard_map/ppermute | solution.py:178
  86.4 5.5 %collective-permute-start.11 = (f32[64,256]{1,0:T(8,128)S(1)}, f32[64,256]{1,0:T(8,128)S(1)}, u32[]{:S(2)}, u32[]{:S(2)}) collective-permute-start(f32[64,256]{1,0:T(8,128)S(1)} %add.27), channel_id=1, source_target_pairs={{0,8},{1,3},{2,10},{3,5},{4,12},{5,7},{6,14},{7,1},{8,16},{9,11},{... | collective-permute-start | bytes 196616 | tf_op jit(solution)/shard_map/ppermute | solution.py:178
  91.9 4.5 %collective-permute-start.16 = (f32[64,256]{1,0:T(8,128)S(1)}, f32[64,256]{1,0:T(8,128)S(1)}, u32[]{:S(2)}, u32[]{:S(2)}) collective-permute-start(f32[64,256]{1,0:T(8,128)S(1)} %add_add_fusion.1), channel_id=1, source_target_pairs={{0,6},{1,25},{2,0},{3,27},{4,2},{5,29},{6,4},{7,31},{8,14},{9,1},{... | collective-permute-start | bytes 196616 | tf_op jit(solution)/shard_map/ppermute | solution.py:178
  94.5 5.8 %collective-permute-start.15 = (f32[64,256]{1,0:T(8,128)S(1)}, f32[64,256]{1,0:T(8,128)S(1)}, u32[]{:S(2)}, u32[]{:S(2)}) collective-permute-start(f32[64,256]{1,0:T(8,128)S(1)} %add_add_fusion.1), channel_id=1, source_target_pairs={{0,4},{1,17},{2,6},{3,19},{4,0},{5,21},{6,2},{7,23},{8,12},{9,25},... | collective-permute-start | bytes 196616 | tf_op jit(solution)/shard_map/ppermute | solution.py:178
  95.1 5.9 %collective-permute-start.14 = (f32[64,256]{1,0:T(8,128)S(1)}, f32[64,256]{1,0:T(8,128)S(1)}, u32[]{:S(2)}, u32[]{:S(2)}) collective-permute-start(f32[64,256]{1,0:T(8,128)S(1)} %add_add_fusion.1), channel_id=1, source_target_pairs={{0,2},{1,9},{2,4},{3,11},{4,6},{5,13},{6,0},{7,15},{8,10},{9,17},{... | collective-permute-start | bytes 196616 | tf_op jit(solution)/shard_map/ppermute | solution.py:178

commit v2 on v0

v2 whole, which is shorter than its diff:
```python
import functools

import jax
import jax.numpy as jnp
from jax import lax
from jax.experimental import pallas as pl
from jax.experimental.pallas import tpu as pltpu
from jax.sharding import PartitionSpec as P

V = 4
R = 64
AXES = ("gx", "gy", "gz")
F32, BF16 = jnp.float32, jnp.bfloat16
PARTS = ((0, 8), (8, 8))


def split(x):
    hi = x.astype(BF16)
    return hi, (x - hi.astype(F32)).astype(BF16)


def dot(a, b, contract):
    return lax.dot_general(a, b, ((contract[:1], contract[1:]), ((), ())), preferred_element_type=F32)


def project_kernel(begin, size, field, b2t_in, b3_in, mine, theirs, cells, b2t, b3, rows, w2, w3, sem, small_sem):
    x, gz = lax.axis_index("gy"), lax.axis_index("gz")
    small = [pltpu.make_async_copy(b2t_in, b2t, small_sem.at[0]), pltpu.make_async_copy(b3_in, b3, small_sem.at[1])]
    for copy in small:
        copy.start()

    def load(off):
        v = lax.rem(x + off, 4)
        return pltpu.make_async_copy(field.at[v, :, pl.ds(begin, size)], cells.at[off], sem.at[off])

    for off in range(4):
        load(off).start()
    for copy in small:
        copy.wait()

    for other in range(2):
        for off in range(4):
            start = (lax.rem(gz // 2 + off, 4) * 2 + lax.rem(gz + other, 2)) * 8
            rows[pl.ds((other * 4 + off) * 8, 8), :] = b2t[pl.ds(pl.multiple_of(start, 8), 8), :]
    hi, lo = split(rows[...].T)
    zero = jnp.zeros_like(hi)
    w2[0:256, :] = jnp.concatenate([hi, zero, lo, zero], axis=1)
    w2[256:512, :] = jnp.concatenate([zero, hi, zero, lo], axis=1)
    tall = jnp.concatenate([jnp.concatenate([b3[...]] * 2, axis=1)] * 2, axis=0)
    block = [lax.broadcasted_iota(jnp.int32, (128, 128), i) // 64 for i in range(2)]
    hi, lo = split(jnp.where(block[0] == block[1], tall, 0.0))
    w3[0:128, :] = hi
    w3[128:256, :] = hi
    w3[256:384, :] = lo

    def chunk(off, _):
        load(off).wait()
        quads = [
            jnp.concatenate([cells[off, i, m, 0], cells[off, i, m, 1]], axis=1) for m in range(size) for i in range(2)
        ]
        hi, lo = split(jnp.concatenate(quads, axis=0))
        both = dot(hi, w2[...], (1, 0))
        first = both[:, :128] + both[:, 128:] + dot(lo, w2[:, :128], (1, 0))
        for m in range(size):
            hi, lo = split(first[m * 128 : (m + 1) * 128].T)
            core = dot(jnp.concatenate([hi, lo, hi], axis=1), w3[...], (1, 0))
            for r in range(2):
                lanes = slice((2 * m + r) * 128, (2 * m + r + 1) * 128)
                mine[off, :, :, lanes] = core[r * 64 : r * 64 + 32].reshape(4, 8, 128)
                theirs[off, :, :, lanes] = core[r * 64 + 32 : r * 64 + 64].reshape(4, 8, 128)
        return 0

    lax.fori_loop(0, 4, chunk, 0)


def project(begin, size, field, b2t, b3):
    part = jax.ShapeDtypeStruct((4, 4, 8, size * 256), F32)
    return pl.pallas_call(
        functools.partial(project_kernel, begin, size),
        out_shape=(part, part),
        in_specs=[pl.BlockSpec(memory_space=pltpu.HBM)] * 3,
        out_specs=[pl.BlockSpec(memory_space=pltpu.VMEM)] * 2,
        scratch_shapes=[
            pltpu.VMEM((4, 2, size, 2, 64, 256), F32),
            pltpu.VMEM((64, 256), F32),
            pltpu.VMEM((64, 64), F32),
            pltpu.VMEM((64, 256), F32),
            pltpu.VMEM((512, 256), BF16),
            pltpu.VMEM((384, 128), BF16),
            pltpu.SemaphoreType.DMA((4,)),
            pltpu.SemaphoreType.DMA((2,)),
        ],
        compiler_params=pltpu.CompilerParams(vmem_limit_bytes=24 * 2**20),
        cost_estimate=pl.CostEstimate(flops=size * 10**9, bytes_accessed=size * 2**20, transcendentals=0),
        name=f"project_{begin}",
    )(*(pltpu.with_memory_space_constraint(a, pltpu.HBM) for a in (field, b2t, b3)))


def add_kernel(mine, received, *outs):
    core = lax.rem(lax.axis_index("gz"), 2)
    for g in range(4):
        for h in range(4):
            v, y = g + (h - g) * core, h + (g - h) * core
            outs[g][h] = mine[v, y] + received[v, y]


def add_groups(mine, received):
    return pl.pallas_call(
        add_kernel,
        out_shape=[jax.ShapeDtypeStruct(mine.shape[1:], F32)] * 4,
        compiler_params=pltpu.CompilerParams(vmem_limit_bytes=8 * 2**20),
        name="add_cores",
    )(mine, received)


def sum_kernel(*refs):
    ins, outs = refs[:-4], refs[-4:]
    lane = 0
    for p in range(0, len(ins), 4):
        a, b, c, d = ins[p : p + 4]
        lanes = slice(lane, lane + a.shape[-1])
        lane += a.shape[-1]
        for h in range(4):
            outs[h][:, lanes] = (a[h] + b[h]) + (c[h] + d[h])


def sum_groups(parts):
    return pl.pallas_call(
        sum_kernel,
        out_shape=[jax.ShapeDtypeStruct((8, 4096), F32)] * 4,
        compiler_params=pltpu.CompilerParams(vmem_limit_bytes=8 * 2**20),
        name="sum_first_axis",
    )(*[x for part in parts for x in part])


def finish_kernel(a, b, c, d, out):
    total = (a[...] + b[...]) + (c[...] + d[...])
    rows = total.reshape(8, 32, 128)
    low = lax.broadcasted_iota(jnp.int32, (32, 128), 1) < 64
    for j in range(4):
        even, odd = rows[2 * j], rows[2 * j + 1]
        out[0:32, j * 128 : (j + 1) * 128] = jnp.where(low, even, pltpu.roll(odd, 64, 1))
        out[32:64, j * 128 : (j + 1) * 128] = jnp.where(low, pltpu.roll(even, 64, 1), odd)


def finish(parts):
    return pl.pallas_call(
        finish_kernel,
        out_shape=jax.ShapeDtypeStruct((64, 512), F32),
        compiler_params=pltpu.CompilerParams(vmem_limit_bytes=8 * 2**20),
        name="sum_second_axis",
    )(*parts)


def gram_kernel(a, b, c, d, out, cols):
    z = lax.axis_index("gx")
    for off, ref in enumerate((a, b, c, d)):
        start = pl.multiple_of(lax.rem(z + off, 4) * 64, 64)
        cols[pl.ds(start, 64), :] = ref[...]
    hi, lo = split(a[...])
    chi, clo = split(cols[...])
    both = dot(jnp.concatenate([hi, lo], axis=0), chi, (1, 1))
    out[...] = (both[:64] + both[64:] + dot(hi, clo, (1, 1))) * (1.0 / (V * R * R))


def gram_part(parts):
    return pl.pallas_call(
        gram_kernel,
        out_shape=jax.ShapeDtypeStruct((64, 256), F32),
        scratch_shapes=[pltpu.VMEM((256, 512), F32)],
        compiler_params=pltpu.CompilerParams(vmem_limit_bytes=8 * 2**20),
        name="gram",
    )(*parts)


def pairs(target):
    out = []
    for z in range(4):
        for x in range(4):
            for y in range(4):
                for c in range(2):
                    tz, tx, ty, tc = target(z, x, y, c)
                    out.append((((z * 4 + x) * 4 + y) * 2 + c, (((tz % 4) * 4 + tx % 4) * 4 + ty % 4) * 2 + tc))
    return out


def send(x, target):
    return lax.ppermute(x, AXES, pairs(target))


def first_axis(off):
    return lambda z, x, y, c: (z, x + off * (1 - c), y + off * c, c)


def second_axis(off):
    return lambda z, x, y, c: (z, x + off * c, y + off * (1 - c), c)


def other_core(z, x, y, c):
    return (z, x, y, 1 - c)


def exchange(parts, axis):
    late = {off: send(parts[off], axis(off)) for off in (2, 1, 3)}
    return [parts[0], late[1], late[2], late[3]]


def total(x, axis):
    return sum(exchange([x] * 4, axis))


def body(field, basis_two, basis_three):
    field = field.reshape(4, 2, 16, 2, 64, 256)
    halves = [project(begin, size, field, basis_two.T, basis_three) for begin, size in PARTS]
    received = [send(theirs, other_core) for _, theirs in halves]
    groups = [add_groups(mine, part) for (mine, _), part in zip(halves, received)]
    groups = sum_groups([exchange(part, first_axis) for part in groups])
    projected = finish(exchange(groups, second_axis))
    rows = [projected] + [send(projected, lambda z, x, y, c, off=off: (z - off, x, y, c)) for off in (1, 2, 3)]
    part = gram_part(rows)
    part = part + send(part, other_core)
    gram = total(total(part, first_axis), second_axis)
    return (projected, gram)


def solution(mesh):
    placed = (P(None, "gx", "gz", "gy"), P("gy", None), P("gz", None))
    return jax.shard_map(
        body,
        mesh=mesh,
        in_specs=placed,
        out_specs=(P("gx", ("gy", "gz")), P("gx", None)),
        check_vma=False,
    )
```

time: 257 us -> 75.2 us (0.29)
  waiting for transfers between devices: 178 us -> 27.8 us
  matrix products: 36.6 us -> 0 us
  starting transfers between devices: 0.08 us -> 30.2 us
  Pallas kernels: 0 us -> 14.8 us
  blocking collectives: 14.1 us -> 0 us
  between operations: 14.1 us -> 0.7 us
  local copies, waits for them, and re-layouts: 11.8 us -> 0.9 us
    psum x1 -> x0, waiting for transfers between devices: 93.4 us -> none  [body(): gram = lax.psum(partial_gram, ('gy', 'gz')) / jnp.float32(V * R * R)]
    reduce_scatter x1 -> x0, waiting for transfers between devices: 84.5 us -> none  [body(): lax.psum_scatter(core, ('gy', 'gz'), scatter_dimension=1, tiled=True)]
    dot_general x3 -> x0, matrix products: 36.6 us -> none  [the longest x1 26.7 us: body(): first = jnp.einsum('vacb,bs->vacs', field, basis_two, precision=highest)]
    ppermute x0 -> x21, starting transfers between devices: none -> 30.2 us  [send(): return lax.ppermute(x, AXES, pairs(target))]
    ppermute x0 -> x21, waiting for transfers between devices: none -> 27.8 us  [send(): return lax.ppermute(x, AXES, pairs(target))]
    pallas_call x0 -> x7, Pallas kernels: none -> 14.8 us  [the longest x2 13.3 us: project(): pl.pallas_call(functools.partial(project_kernel, begin, size), out_shape=...]
    all_gather x1 -> x0, blocking collectives: 14.1 us -> none  [body(): lax.all_gather(projected, 'gx', axis=0, tiled=True)]
    reshape x1 -> x0, local copies, waits for them, and re-layouts: 6.89 us -> none  [body(): core = core.reshape(rows, -1)]
  transfers between devices with their start and end apart: 2 -> 21, of which waited for: 2 -> 18; matrix products, arithmetic and copies ran while one was open for 0% -> 0% of each run, Pallas kernels for 0% -> 9%
where the time goes in v2:
time: 75.2 us; the launch traced here: 75.1 us
  starting transfers between devices  30.2 us (40%)
  waiting for transfers between devices  27.8 us (37%)
  Pallas kernels  14.8 us (20%)
  local copies, waits for them, and re-layouts  0.9 us (1%)
    ppermute x21, starting transfers between devices, send(): return lax.ppermute(x, AXES, pairs(target))  30.2 us
    ppermute x21, waiting for transfers between devices, send(): return lax.ppermute(x, AXES, pairs(target))  27.8 us
    pallas_call x2, Pallas kernels, project(): pl.pallas_call(functools.partial(project_kernel, begin, size), out_shape=...  13.3 us
  transfers between devices with their start and end apart: 21, of which 18 were waited for; matrix products, arithmetic and copies ran while one was open for 0% of the time, Pallas kernels for 9%

profile of v2, /device:TPU:0, one launch (start us, length us, event | category | flops | bytes accessed | tf_op | source)
XLA Modules:
  0.0 75.1 jit_solution(11245489933013102167)
XLA Ops:
  0.6 6.7 %project_8.1 = (f32[4,4,8,2048]{3,2,1,0:T(8,128)S(1)}, f32[4,4,8,2048]{3,2,1,0:T(8,128)S(1)}) custom-call(f32[4,2,16,2,64,256]{5,4,3,2,1,0:T(8,128)} %bitcast.2, f32[64,256]{1,0:T(8,128)} %bitcast.4, f32[64,64]{1,0:T(8,128)} %b3_in.3), custom_call_target="tpu_custom_call" | custom-call | flops 8000000000 | bytes 8388608 | tf_op jit(solution)/shard_map/project_8/pallas_call | solution.py:78
  7.3 0.1 collective-permute-start.4
  7.4 6.7 %project_0.1 = (f32[4,4,8,2048]{3,2,1,0:T(8,128)S(1)}, f32[4,4,8,2048]{3,2,1,0:T(8,128)S(1)}) custom-call(f32[4,2,16,2,64,256]{5,4,3,2,1,0:T(8,128)} %bitcast.3, f32[64,256]{1,0:T(8,128)} %bitcast.5, f32[64,64]{1,0:T(8,128)} %b3_in.3), custom_call_target="tpu_custom_call" | custom-call | flops 8000000000 | bytes 8388608 | tf_op jit(solution)/shard_map/project_0/pallas_call | solution.py:78
  14.1 0.6 collective-permute-start
  14.6 0.1 add_cores.3
  14.7 1.6 %collective-permute-start.5 = (f32[4,8,2048]{2,1,0:T(8,128)S(1)}, f32[4,8,2048]{2,1,0:T(8,128)S(1)}, u32[]{:S(2)}, u32[]{:S(2)}) collective-permute-start(f32[4,8,2048]{2,1,0:T(8,128)S(1)} %get-tuple-element.27), channel_id=1, source_target_pairs={{0,8},{1,3},{2,10},{3,5},{4,12},{5,7},{6,14},{7,1},{8,16},{9,11},{... | collective-permute-start | bytes 786440 | tf_op jit(solution)/shard_map/ppermute | solution.py:188
  16.4 2.7 %collective-permute-start.6 = (f32[4,8,2048]{2,1,0:T(8,128)S(1)}, f32[4,8,2048]{2,1,0:T(8,128)S(1)}, u32[]{:S(2)}, u32[]{:S(2)}) collective-permute-start(f32[4,8,2048]{2,1,0:T(8,128)S(1)} %get-tuple-element.28), channel_id=1, source_target_pairs={{0,16},{1,5},{2,18},{3,7},{4,20},{5,1},{6,22},{7,3},{8,24},{9,13},... | collective-permute-start | bytes 786440 | tf_op jit(solution)/shard_map/ppermute | solution.py:188
  19.1 1.4 %collective-permute-start.7 = (f32[4,8,2048]{2,1,0:T(8,128)S(1)}, f32[4,8,2048]{2,1,0:T(8,128)S(1)}, u32[]{:S(2)}, u32[]{:S(2)}) collective-permute-start(f32[4,8,2048]{2,1,0:T(8,128)S(1)} %get-tuple-element.29), channel_id=1, source_target_pairs={{0,24},{1,7},{2,26},{3,1},{4,28},{5,3},{6,30},{7,5},{8,0},{9,15},{... | collective-permute-start | bytes 786440 | tf_op jit(solution)/shard_map/ppermute | solution.py:188
  20.6 0.1 add_cores.2
  20.7 0.7 collective-permute-start.1
  21.3 0.9 %collective-permute-start.2 = (f32[4,8,2048]{2,1,0:T(8,128)S(1)}, f32[4,8,2048]{2,1,0:T(8,128)S(1)}, u32[]{:S(2)}, u32[]{:S(2)}) collective-permute-start(f32[4,8,2048]{2,1,0:T(8,128)S(1)} %get-tuple-element.22), channel_id=1, source_target_pairs={{0,16},{1,5},{2,18},{3,7},{4,20},{5,1},{6,22},{7,3},{8,24},{9,13},... | collective-permute-start | bytes 786440 | tf_op jit(solution)/shard_map/ppermute | solution.py:188
  22.2 0.2 collective-permute-done.5.refs_5_
  22.4 1.7 %collective-permute-start.3 = (f32[4,8,2048]{2,1,0:T(8,128)S(1)}, f32[4,8,2048]{2,1,0:T(8,128)S(1)}, u32[]{:S(2)}, u32[]{:S(2)}) collective-permute-start(f32[4,8,2048]{2,1,0:T(8,128)S(1)} %get-tuple-element.23), channel_id=1, source_target_pairs={{0,24},{1,7},{2,26},{3,1},{4,28},{5,3},{6,30},{7,5},{8,0},{9,15},{... | collective-permute-start | bytes 786440 | tf_op jit(solution)/shard_map/ppermute | solution.py:188
  24.1 2.3 %collective-permute-done.6.refs_6_ = f32[4,8,2048]{2,1,0:T(8,128)S(1)} collective-permute-done((f32[4,8,2048]{2,1,0:T(8,128)S(1)}, f32[4,8,2048]{2,1,0:T(8,128)S(1)}, u32[]{:S(2)}, u32[]{:S(2)}) %collective-permute-start.6) | collective-permute-done | bytes 262176 | tf_op jit(solution)/shard_map/ppermute | solution.py:188
  26.4 2.7 %collective-permute-done.1.refs_1_ = f32[4,8,2048]{2,1,0:T(8,128)S(1)} collective-permute-done((f32[4,8,2048]{2,1,0:T(8,128)S(1)}, f32[4,8,2048]{2,1,0:T(8,128)S(1)}, u32[]{:S(2)}, u32[]{:S(2)}) %collective-permute-start.1) | collective-permute-done | bytes 262176 | tf_op jit(solution)/shard_map/ppermute | solution.py:188
  29.1 2.8 %collective-permute-done.2.refs_2_ = f32[4,8,2048]{2,1,0:T(8,128)S(1)} collective-permute-done((f32[4,8,2048]{2,1,0:T(8,128)S(1)}, f32[4,8,2048]{2,1,0:T(8,128)S(1)}, u32[]{:S(2)}, u32[]{:S(2)}) %collective-permute-start.2) | collective-permute-done | bytes 262176 | tf_op jit(solution)/shard_map/ppermute | solution.py:188
  31.9 0.1 collective-permute-done.3.refs_3_
  32.0 0.1 sum_first_axis.1
  32.1 1.7 %collective-permute-start.8 = (f32[8,4096]{1,0:T(8,128)S(1)}, f32[8,4096]{1,0:T(8,128)S(1)}, u32[]{:S(2)}, u32[]{:S(2)}) collective-permute-start(f32[8,4096]{1,0:T(8,128)S(1)} %get-tuple-element.31), channel_id=1, source_target_pairs={{0,2},{1,9},{2,4},{3,11},{4,6},{5,13},{6,0},{7,15},{8,10},{9,17},{... | collective-permute-start | bytes 393224 | tf_op jit(solution)/shard_map/ppermute | solution.py:188
  33.8 2.9 %collective-permute-start.9 = (f32[8,4096]{1,0:T(8,128)S(1)}, f32[8,4096]{1,0:T(8,128)S(1)}, u32[]{:S(2)}, u32[]{:S(2)}) collective-permute-start(f32[8,4096]{1,0:T(8,128)S(1)} %get-tuple-element.32), channel_id=1, source_target_pairs={{0,4},{1,17},{2,6},{3,19},{4,0},{5,21},{6,2},{7,23},{8,12},{9,25},... | collective-permute-start | bytes 393224 | tf_op jit(solution)/shard_map/ppermute | solution.py:188
  36.7 1.3 %collective-permute-start.10 = (f32[8,4096]{1,0:T(8,128)S(1)}, f32[8,4096]{1,0:T(8,128)S(1)}, u32[]{:S(2)}, u32[]{:S(2)}) collective-permute-start(f32[8,4096]{1,0:T(8,128)S(1)} %get-tuple-element.33), channel_id=1, source_target_pairs={{0,6},{1,25},{2,0},{3,27},{4,2},{5,29},{6,4},{7,31},{8,14},{9,1},{... | collective-permute-start | bytes 393224 | tf_op jit(solution)/shard_map/ppermute | solution.py:188
  38.0 0.4 collective-permute-done.8.b
  38.4 2.6 %collective-permute-done.9.c = f32[8,4096]{1,0:T(8,128)S(1)} collective-permute-done((f32[8,4096]{1,0:T(8,128)S(1)}, f32[8,4096]{1,0:T(8,128)S(1)}, u32[]{:S(2)}, u32[]{:S(2)}) %collective-permute-start.9) | collective-permute-done | bytes 131104 | tf_op jit(solution)/shard_map/ppermute | solution.py:188
  41.0 0.6 collective-permute-done.10.d
  41.7 0.8 %sum_second_axis.1.a = f32[64,512]{1,0:T(8,128)} custom-call(f32[8,4096]{1,0:T(8,128)S(1)} %get-tuple-element.30.a, f32[8,4096]{1,0:T(8,128)S(1)} %collective-permute-done.8.b, f32[8,4096]{1,0:T(8,128)S(1)} %collective-permute-done.9.c, f32[8,4096]{1,0:T(8,128)S(1)} %collective-permute-done.10.d), custom_call_target="tpu_custom_call" | custom-call | tf_op jit(solution)/shard_map/sum_second_axis/pallas_call | solution.py:147
  42.4 1.9 %collective-permute-start.13 = (f32[64,512]{1,0:T(8,128)}, f32[64,512]{1,0:T(8,128)S(1)}, u32[]{:S(2)}, u32[]{:S(2)}) collective-permute-start(f32[64,512]{1,0:T(8,128)} %sum_second_axis.1.a), channel_id=1, source_target_pairs={{0,32},{1,33},{2,34},{3,35},{4,36},{5,37},{6,38},{7,39},{8,40},{9,... | collective-permute-start | bytes 393224 | tf_op jit(solution)/shard_map/ppermute | solution.py:188
  44.3 3.6 %collective-permute-start.12 = (f32[64,512]{1,0:T(8,128)}, f32[64,512]{1,0:T(8,128)S(1)}, u32[]{:S(2)}, u32[]{:S(2)}) collective-permute-start(f32[64,512]{1,0:T(8,128)} %sum_second_axis.1.a), channel_id=1, source_target_pairs={{0,64},{1,65},{2,66},{3,67},{4,68},{5,69},{6,70},{7,71},{8,72},{9,... | collective-permute-start | bytes 393224 | tf_op jit(solution)/shard_map/ppermute | solution.py:188
  47.9 1.0 %collective-permute-start.11 = (f32[64,512]{1,0:T(8,128)}, f32[64,512]{1,0:T(8,128)S(1)}, u32[]{:S(2)}, u32[]{:S(2)}) collective-permute-start(f32[64,512]{1,0:T(8,128)} %sum_second_axis.1.a), channel_id=1, source_target_pairs={{0,96},{1,97},{2,98},{3,99},{4,100},{5,101},{6,102},{7,103},{8,104... | collective-permute-start | bytes 393224 | tf_op jit(solution)/shard_map/ppermute | solution.py:188
  48.9 1.0 %collective-permute-done.13.d = f32[64,512]{1,0:T(8,128)S(1)} collective-permute-done((f32[64,512]{1,0:T(8,128)}, f32[64,512]{1,0:T(8,128)S(1)}, u32[]{:S(2)}, u32[]{:S(2)}) %collective-permute-start.13) | collective-permute-done | bytes 131104 | tf_op jit(solution)/shard_map/ppermute | solution.py:188
  50.0 2.5 %collective-permute-done.12.c = f32[64,512]{1,0:T(8,128)S(1)} collective-permute-done((f32[64,512]{1,0:T(8,128)}, f32[64,512]{1,0:T(8,128)S(1)}, u32[]{:S(2)}, u32[]{:S(2)}) %collective-permute-start.12) | collective-permute-done | bytes 131104 | tf_op jit(solution)/shard_map/ppermute | solution.py:188
  52.5 0.6 collective-permute-done.11.b
  53.1 0.9 %copy-done = f32[64,512]{1,0:T(8,128)S(1)} copy-done((f32[64,512]{1,0:T(8,128)S(1)}, f32[64,512]{1,0:T(8,128)}, u32[]{:S(2)}) %copy-start) | copy-done | bytes 131096
  54.0 0.3 gram.1
  54.4 0.1 collective-permute-start.14
  54.5 1.2 %collective-permute-done.14 = f32[64,256]{1,0:T(8,128)S(1)} collective-permute-done((f32[64,256]{1,0:T(8,128)S(1)}, f32[64,256]{1,0:T(8,128)S(1)}, u32[]{:S(2)}, u32[]{:S(2)}) %collective-permute-start.14) | collective-permute-done | bytes 65568 | tf_op jit(solution)/shard_map/ppermute | solution.py:188
  55.7 2.5 %collective-permute-start.17 = (f32[64,256]{1,0:T(8,128)S(1)}, f32[64,256]{1,0:T(8,128)S(1)}, u32[]{:S(2)}, u32[]{:S(2)}) collective-permute-start(f32[64,256]{1,0:T(8,128)S(1)} %add.21), channel_id=1, source_target_pairs={{0,24},{1,7},{2,26},{3,1},{4,28},{5,3},{6,30},{7,5},{8,0},{9,15},{... | collective-permute-start | bytes 196616 | tf_op jit(solution)/shard_map/ppermute | solution.py:188
  58.2 1.6 %collective-permute-start.16 = (f32[64,256]{1,0:T(8,128)S(1)}, f32[64,256]{1,0:T(8,128)S(1)}, u32[]{:S(2)}, u32[]{:S(2)}) collective-permute-start(f32[64,256]{1,0:T(8,128)S(1)} %add.21), channel_id=1, source_target_pairs={{0,16},{1,5},{2,18},{3,7},{4,20},{5,1},{6,22},{7,3},{8,24},{9,13},... | collective-permute-start | bytes 196616 | tf_op jit(solution)/shard_map/ppermute | solution.py:188
  59.8 0.2 collective-permute-start.15
  60.1 0.1 collective-permute-done.17
  60.1 3.9 %collective-permute-done.16 = f32[64,256]{1,0:T(8,128)S(1)} collective-permute-done((f32[64,256]{1,0:T(8,128)S(1)}, f32[64,256]{1,0:T(8,128)S(1)}, u32[]{:S(2)}, u32[]{:S(2)}) %collective-permute-start.16) | collective-permute-done | bytes 65568 | tf_op jit(solution)/shard_map/ppermute | solution.py:188
  64.0 1.3 %collective-permute-done.15 = f32[64,256]{1,0:T(8,128)S(1)} collective-permute-done((f32[64,256]{1,0:T(8,128)S(1)}, f32[64,256]{1,0:T(8,128)S(1)}, u32[]{:S(2)}, u32[]{:S(2)}) %collective-permute-start.15) | collective-permute-done | bytes 65568 | tf_op jit(solution)/shard_map/ppermute | solution.py:188
  65.3 2.6 %collective-permute-start.20 = (f32[64,256]{1,0:T(8,128)S(1)}, f32[64,256]{1,0:T(8,128)S(1)}, u32[]{:S(2)}, u32[]{:S(2)}) collective-permute-start(f32[64,256]{1,0:T(8,128)S(1)} %add_add_fusion.1), channel_id=1, source_target_pairs={{0,6},{1,25},{2,0},{3,27},{4,2},{5,29},{6,4},{7,31},{8,14},{9,1},{... | collective-permute-start | bytes 196616 | tf_op jit(solution)/shard_map/ppermute | solution.py:188
  68.0 0.5 collective-permute-start.19
  68.5 0.6 collective-permute-start.18
  69.1 0.8 %collective-permute-done.20 = f32[64,256]{1,0:T(8,128)S(1)} collective-permute-done((f32[64,256]{1,0:T(8,128)S(1)}, f32[64,256]{1,0:T(8,128)S(1)}, u32[]{:S(2)}, u32[]{:S(2)}) %collective-permute-start.20) | collective-permute-done | bytes 65568 | tf_op jit(solution)/shard_map/ppermute | solution.py:188
  69.9 3.9 %collective-permute-done.19 = f32[64,256]{1,0:T(8,128)S(1)} collective-permute-done((f32[64,256]{1,0:T(8,128)S(1)}, f32[64,256]{1,0:T(8,128)S(1)}, u32[]{:S(2)}, u32[]{:S(2)}) %collective-permute-start.19) | collective-permute-done | bytes 65568 | tf_op jit(solution)/shard_map/ppermute | solution.py:188
  73.8 0.7 collective-permute-done.18
  74.4 0.6 add_add_fusion
  (6 shorter events, 0.0 us)
Async XLA Ops:
  7.3 7.3 %collective-permute-start.4 = (f32[4,4,8,2048]{3,2,1,0:T(8,128)S(1)}, f32[4,4,8,2048]{3,2,1,0:T(8,128)S(1)}, u32[]{:S(2)}, u32[]{:S(2)}) collective-permute-start(f32[4,4,8,2048]{3,2,1,0:T(8,128)S(1)} %get-tuple-element.25), channel_id=1, source_target_pairs={{0,1},{1,0},{2,3},{3,2},{4,5},{5,4},{6,7},{7,6},{8,9},{9,8},{10,11... | collective-permute-start | bytes 3145736 | tf_op jit(solution)/shard_map/ppermute | solution.py:188
  14.1 6.5 %collective-permute-start = (f32[4,4,8,2048]{3,2,1,0:T(8,128)S(1)}, f32[4,4,8,2048]{3,2,1,0:T(8,128)S(1)}, u32[]{:S(2)}, u32[]{:S(2)}) collective-permute-start(f32[4,4,8,2048]{3,2,1,0:T(8,128)S(1)} %get-tuple-element.19), channel_id=1, source_target_pairs={{0,1},{1,0},{2,3},{3,2},{4,5},{5,4},{6,7},{7,6},{8,9},{9,8},{10,11... | collective-permute-start | bytes 3145736 | tf_op jit(solution)/shard_map/ppermute | solution.py:188
  14.7 7.7 %collective-permute-start.5 = (f32[4,8,2048]{2,1,0:T(8,128)S(1)}, f32[4,8,2048]{2,1,0:T(8,128)S(1)}, u32[]{:S(2)}, u32[]{:S(2)}) collective-permute-start(f32[4,8,2048]{2,1,0:T(8,128)S(1)} %get-tuple-element.27), channel_id=1, source_target_pairs={{0,8},{1,3},{2,10},{3,5},{4,12},{5,7},{6,14},{7,1},{8,16},{9,11},{... | collective-permute-start | bytes 786440 | tf_op jit(solution)/shard_map/ppermute | solution.py:188
  16.4 10.0 %collective-permute-start.6 = (f32[4,8,2048]{2,1,0:T(8,128)S(1)}, f32[4,8,2048]{2,1,0:T(8,128)S(1)}, u32[]{:S(2)}, u32[]{:S(2)}) collective-permute-start(f32[4,8,2048]{2,1,0:T(8,128)S(1)} %get-tuple-element.28), channel_id=1, source_target_pairs={{0,16},{1,5},{2,18},{3,7},{4,20},{5,1},{6,22},{7,3},{8,24},{9,13},... | collective-permute-start | bytes 786440 | tf_op jit(solution)/shard_map/ppermute | solution.py:188
  19.1 7.2 %collective-permute-start.7 = (f32[4,8,2048]{2,1,0:T(8,128)S(1)}, f32[4,8,2048]{2,1,0:T(8,128)S(1)}, u32[]{:S(2)}, u32[]{:S(2)}) collective-permute-start(f32[4,8,2048]{2,1,0:T(8,128)S(1)} %get-tuple-element.29), channel_id=1, source_target_pairs={{0,24},{1,7},{2,26},{3,1},{4,28},{5,3},{6,30},{7,5},{8,0},{9,15},{... | collective-permute-start | bytes 786440 | tf_op jit(solution)/shard_map/ppermute | solution.py:188
  20.7 8.4 %collective-permute-start.1 = (f32[4,8,2048]{2,1,0:T(8,128)S(1)}, f32[4,8,2048]{2,1,0:T(8,128)S(1)}, u32[]{:S(2)}, u32[]{:S(2)}) collective-permute-start(f32[4,8,2048]{2,1,0:T(8,128)S(1)} %get-tuple-element.21), channel_id=1, source_target_pairs={{0,8},{1,3},{2,10},{3,5},{4,12},{5,7},{6,14},{7,1},{8,16},{9,11},{... | collective-permute-start | bytes 786440 | tf_op jit(solution)/shard_map/ppermute | solution.py:188
  21.3 10.6 %collective-permute-start.2 = (f32[4,8,2048]{2,1,0:T(8,128)S(1)}, f32[4,8,2048]{2,1,0:T(8,128)S(1)}, u32[]{:S(2)}, u32[]{:S(2)}) collective-permute-start(f32[4,8,2048]{2,1,0:T(8,128)S(1)} %get-tuple-element.22), channel_id=1, source_target_pairs={{0,16},{1,5},{2,18},{3,7},{4,20},{5,1},{6,22},{7,3},{8,24},{9,13},... | collective-permute-start | bytes 786440 | tf_op jit(solution)/shard_map/ppermute | solution.py:188
  22.4 9.6 %collective-permute-start.3 = (f32[4,8,2048]{2,1,0:T(8,128)S(1)}, f32[4,8,2048]{2,1,0:T(8,128)S(1)}, u32[]{:S(2)}, u32[]{:S(2)}) collective-permute-start(f32[4,8,2048]{2,1,0:T(8,128)S(1)} %get-tuple-element.23), channel_id=1, source_target_pairs={{0,24},{1,7},{2,26},{3,1},{4,28},{5,3},{6,30},{7,5},{8,0},{9,15},{... | collective-permute-start | bytes 786440 | tf_op jit(solution)/shard_map/ppermute | solution.py:188
  32.1 6.2 %collective-permute-start.8 = (f32[8,4096]{1,0:T(8,128)S(1)}, f32[8,4096]{1,0:T(8,128)S(1)}, u32[]{:S(2)}, u32[]{:S(2)}) collective-permute-start(f32[8,4096]{1,0:T(8,128)S(1)} %get-tuple-element.31), channel_id=1, source_target_pairs={{0,2},{1,9},{2,4},{3,11},{4,6},{5,13},{6,0},{7,15},{8,10},{9,17},{... | collective-permute-start | bytes 393224 | tf_op jit(solution)/shard_map/ppermute | solution.py:188
  33.8 7.2 %collective-permute-start.9 = (f32[8,4096]{1,0:T(8,128)S(1)}, f32[8,4096]{1,0:T(8,128)S(1)}, u32[]{:S(2)}, u32[]{:S(2)}) collective-permute-start(f32[8,4096]{1,0:T(8,128)S(1)} %get-tuple-element.32), channel_id=1, source_target_pairs={{0,4},{1,17},{2,6},{3,19},{4,0},{5,21},{6,2},{7,23},{8,12},{9,25},... | collective-permute-start | bytes 393224 | tf_op jit(solution)/shard_map/ppermute | solution.py:188
  36.7 5.0 %collective-permute-start.10 = (f32[8,4096]{1,0:T(8,128)S(1)}, f32[8,4096]{1,0:T(8,128)S(1)}, u32[]{:S(2)}, u32[]{:S(2)}) collective-permute-start(f32[8,4096]{1,0:T(8,128)S(1)} %get-tuple-element.33), channel_id=1, source_target_pairs={{0,6},{1,25},{2,0},{3,27},{4,2},{5,29},{6,4},{7,31},{8,14},{9,1},{... | collective-permute-start | bytes 393224 | tf_op jit(solution)/shard_map/ppermute | solution.py:188
  42.4 7.5 %collective-permute-start.13 = (f32[64,512]{1,0:T(8,128)}, f32[64,512]{1,0:T(8,128)S(1)}, u32[]{:S(2)}, u32[]{:S(2)}) collective-permute-start(f32[64,512]{1,0:T(8,128)} %sum_second_axis.1.a), channel_id=1, source_target_pairs={{0,32},{1,33},{2,34},{3,35},{4,36},{5,37},{6,38},{7,39},{8,40},{9,... | collective-permute-start | bytes 393224 | tf_op jit(solution)/shard_map/ppermute | solution.py:188
  44.3 8.2 %collective-permute-start.12 = (f32[64,512]{1,0:T(8,128)}, f32[64,512]{1,0:T(8,128)S(1)}, u32[]{:S(2)}, u32[]{:S(2)}) collective-permute-start(f32[64,512]{1,0:T(8,128)} %sum_second_axis.1.a), channel_id=1, source_target_pairs={{0,64},{1,65},{2,66},{3,67},{4,68},{5,69},{6,70},{7,71},{8,72},{9,... | collective-permute-start | bytes 393224 | tf_op jit(solution)/shard_map/ppermute | solution.py:188
  47.9 5.2 %collective-permute-start.11 = (f32[64,512]{1,0:T(8,128)}, f32[64,512]{1,0:T(8,128)S(1)}, u32[]{:S(2)}, u32[]{:S(2)}) collective-permute-start(f32[64,512]{1,0:T(8,128)} %sum_second_axis.1.a), channel_id=1, source_target_pairs={{0,96},{1,97},{2,98},{3,99},{4,100},{5,101},{6,102},{7,103},{8,104... | collective-permute-start | bytes 393224 | tf_op jit(solution)/shard_map/ppermute | solution.py:188
  53.1 0.9 %copy-start = (f32[64,512]{1,0:T(8,128)S(1)}, f32[64,512]{1,0:T(8,128)}, u32[]{:S(2)}) copy-start(f32[64,512]{1,0:T(8,128)} %sum_second_axis.1.a) | copy-start | bytes 393220
  54.4 1.3 %collective-permute-start.14 = (f32[64,256]{1,0:T(8,128)S(1)}, f32[64,256]{1,0:T(8,128)S(1)}, u32[]{:S(2)}, u32[]{:S(2)}) collective-permute-start(f32[64,256]{1,0:T(8,128)S(1)} %gram.1), channel_id=1, source_target_pairs={{0,1},{1,0},{2,3},{3,2},{4,5},{5,4},{6,7},{7,6},{8,9},{9,8},{10,11... | collective-permute-start | bytes 196616 | tf_op jit(solution)/shard_map/ppermute | solution.py:188
  55.7 4.4 %collective-permute-start.17 = (f32[64,256]{1,0:T(8,128)S(1)}, f32[64,256]{1,0:T(8,128)S(1)}, u32[]{:S(2)}, u32[]{:S(2)}) collective-permute-start(f32[64,256]{1,0:T(8,128)S(1)} %add.21), channel_id=1, source_target_pairs={{0,24},{1,7},{2,26},{3,1},{4,28},{5,3},{6,30},{7,5},{8,0},{9,15},{... | collective-permute-start | bytes 196616 | tf_op jit(solution)/shard_map/ppermute | solution.py:188
  58.2 5.8 %collective-permute-start.16 = (f32[64,256]{1,0:T(8,128)S(1)}, f32[64,256]{1,0:T(8,128)S(1)}, u32[]{:S(2)}, u32[]{:S(2)}) collective-permute-start(f32[64,256]{1,0:T(8,128)S(1)} %add.21), channel_id=1, source_target_pairs={{0,16},{1,5},{2,18},{3,7},{4,20},{5,1},{6,22},{7,3},{8,24},{9,13},... | collective-permute-start | bytes 196616 | tf_op jit(solution)/shard_map/ppermute | solution.py:188
  59.8 5.5 %collective-permute-start.15 = (f32[64,256]{1,0:T(8,128)S(1)}, f32[64,256]{1,0:T(8,128)S(1)}, u32[]{:S(2)}, u32[]{:S(2)}) collective-permute-start(f32[64,256]{1,0:T(8,128)S(1)} %add.21), channel_id=1, source_target_pairs={{0,8},{1,3},{2,10},{3,5},{4,12},{5,7},{6,14},{7,1},{8,16},{9,11},{... | collective-permute-start | bytes 196616 | tf_op jit(solution)/shard_map/ppermute | solution.py:188
  65.3 4.5 %collective-permute-start.20 = (f32[64,256]{1,0:T(8,128)S(1)}, f32[64,256]{1,0:T(8,128)S(1)}, u32[]{:S(2)}, u32[]{:S(2)}) collective-permute-start(f32[64,256]{1,0:T(8,128)S(1)} %add_add_fusion.1), channel_id=1, source_target_pairs={{0,6},{1,25},{2,0},{3,27},{4,2},{5,29},{6,4},{7,31},{8,14},{9,1},{... | collective-permute-start | bytes 196616 | tf_op jit(solution)/shard_map/ppermute | solution.py:188
  68.0 5.8 %collective-permute-start.19 = (f32[64,256]{1,0:T(8,128)S(1)}, f32[64,256]{1,0:T(8,128)S(1)}, u32[]{:S(2)}, u32[]{:S(2)}) collective-permute-start(f32[64,256]{1,0:T(8,128)S(1)} %add_add_fusion.1), channel_id=1, source_target_pairs={{0,4},{1,17},{2,6},{3,19},{4,0},{5,21},{6,2},{7,23},{8,12},{9,25},... | collective-permute-start | bytes 196616 | tf_op jit(solution)/shard_map/ppermute | solution.py:188
  68.5 6.0 %collective-permute-start.18 = (f32[64,256]{1,0:T(8,128)S(1)}, f32[64,256]{1,0:T(8,128)S(1)}, u32[]{:S(2)}, u32[]{:S(2)}) collective-permute-start(f32[64,256]{1,0:T(8,128)S(1)} %add_add_fusion.1), channel_id=1, source_target_pairs={{0,2},{1,9},{2,4},{3,11},{4,6},{5,13},{6,0},{7,15},{8,10},{9,17},{... | collective-permute-start | bytes 196616 | tf_op jit(solution)/shard_map/ppermute | solution.py:188

commit v3 on v2

v3 whole, which is shorter than its diff:
```python
import functools

import jax
import jax.numpy as jnp
from jax import lax
from jax.experimental import pallas as pl
from jax.experimental.pallas import tpu as pltpu
from jax.sharding import PartitionSpec as P

V = 4
R = 64
OFFSETS = (0, 1, 3, 2)
AXES = ("gx", "gy", "gz")
F32, BF16 = jnp.float32, jnp.bfloat16
SIZES = (8, 8)


def split(x):
    hi = x.astype(BF16)
    return hi, (x - hi.astype(F32)).astype(BF16)


def dot(a, b, contract):
    return lax.dot_general(a, b, ((contract[:1], contract[1:]), ((), ())), preferred_element_type=F32)


def contract(cells, w2, w3, mine, theirs):
    size = cells.shape[1]
    quads = [
        jnp.concatenate([cells[i, m, 0], cells[i, m, 1]], axis=1) for m in range(size) for i in range(2)
    ]
    hi, lo = split(jnp.concatenate(quads, axis=0))
    both = dot(hi, w2[...], (1, 0))
    first = both[:, :128] + both[:, 128:] + dot(lo, w2[:, :128], (1, 0))
    for m in range(size):
        hi, lo = split(first[m * 128 : (m + 1) * 128].T)
        core = dot(jnp.concatenate([hi, lo, hi], axis=1), w3[...], (1, 0))
        for r in range(2):
            lanes = slice((2 * m + r) * 128, (2 * m + r + 1) * 128)
            mine[:, :, lanes] = core[r * 64 : r * 64 + 32].reshape(4, 8, 128)
            theirs[:, :, lanes] = core[r * 64 + 32 : r * 64 + 64].reshape(4, 8, 128)


def first_part_kernel(field, b2t_in, b3_in, mine, theirs, later, w2, w3, cells, b2t, b3, rows, sem, small_sem):
    x, gz = lax.axis_index("gy"), lax.axis_index("gz")
    small = [pltpu.make_async_copy(b2t_in, b2t, small_sem.at[0]), pltpu.make_async_copy(b3_in, b3, small_sem.at[1])]
    for copy in small:
        copy.start()

    def load(n):
        part, off = n // 4, n % 4
        cut = pl.ds(part * SIZES[0], SIZES[part])
        to = later if part else cells
        return pltpu.make_async_copy(field.at[lax.rem(x + off, 4), :, cut], to.at[off], sem.at[n])

    load(0).start()
    for copy in small:
        copy.wait()

    for other in range(2):
        for off in range(4):
            start = (lax.rem(gz // 2 + off, 4) * 2 + lax.rem(gz + other, 2)) * 8
            rows[pl.ds((other * 4 + off) * 8, 8), :] = b2t[pl.ds(pl.multiple_of(start, 8), 8), :]
    hi, lo = split(rows[...].T)
    zero = jnp.zeros_like(hi)
    w2[0:256, :] = jnp.concatenate([hi, zero, lo, zero], axis=1)
    w2[256:512, :] = jnp.concatenate([zero, hi, zero, lo], axis=1)
    tall = jnp.concatenate([jnp.concatenate([b3[...]] * 2, axis=1)] * 2, axis=0)
    block = [lax.broadcasted_iota(jnp.int32, (128, 128), i) // 64 for i in range(2)]
    hi, lo = split(jnp.where(block[0] == block[1], tall, 0.0))
    w3[0:128, :] = hi
    w3[128:256, :] = hi
    w3[256:384, :] = lo

    load(1).start()
    for off, ahead in enumerate(((2,), (3, 4), (5, 6), ())):
        load(off).wait()
        for n in ahead:
            load(n).start()
        contract(cells.at[off], w2, w3, mine.at[off], theirs.at[off])
    for n in range(4, 7):
        load(n).wait()


def second_part_kernel(field, early, w2, w3, mine, theirs, late, sem):
    x = lax.axis_index("gy")

    def load():
        cut = pl.ds(SIZES[0], SIZES[1])
        return pltpu.make_async_copy(field.at[lax.rem(x + 3, 4), :, cut], late, sem)

    load().start()
    for off in range(4):
        if off == 3:
            load().wait()
        contract(early.at[off] if off < 3 else late, w2, w3, mine.at[off], theirs.at[off])


def project(field, b2t, b3):
    parts = [jax.ShapeDtypeStruct((4, 4, 8, size * 256), F32) for size in SIZES]
    cells = [(4, 2, size, 2, 64, 256) for size in SIZES]
    costs = [pl.CostEstimate(flops=size * 10**9, bytes_accessed=size * 2**20, transcendentals=0) for size in SIZES]
    params = pltpu.CompilerParams(vmem_limit_bytes=26 * 2**20)
    vmem = pl.BlockSpec(memory_space=pltpu.VMEM)
    field, b2t, b3 = (pltpu.with_memory_space_constraint(a, pltpu.HBM) for a in (field, b2t, b3))
    mine, theirs, later, w2, w3 = pl.pallas_call(
        first_part_kernel,
        out_shape=(
            parts[0],
            parts[0],
            jax.ShapeDtypeStruct((3, *cells[1][1:]), F32),
            jax.ShapeDtypeStruct((512, 256), BF16),
            jax.ShapeDtypeStruct((384, 128), BF16),
        ),
        in_specs=[pl.BlockSpec(memory_space=pltpu.HBM)] * 3,
        out_specs=[vmem] * 5,
        scratch_shapes=[
            pltpu.VMEM(cells[0], F32),
            pltpu.VMEM((64, 256), F32),
            pltpu.VMEM((64, 64), F32),
            pltpu.VMEM((64, 256), F32),
            pltpu.SemaphoreType.DMA((7,)),
            pltpu.SemaphoreType.DMA((2,)),
        ],
        compiler_params=params,
        cost_estimate=costs[0],
        name="project_first_part",
    )(field, b2t, b3)
    second = pl.pallas_call(
        second_part_kernel,
        out_shape=(parts[1], parts[1]),
        in_specs=[pl.BlockSpec(memory_space=pltpu.HBM)] + [vmem] * 3,
        out_specs=[vmem] * 2,
        scratch_shapes=[pltpu.VMEM(cells[1][1:], F32), pltpu.SemaphoreType.DMA],
        compiler_params=params,
        cost_estimate=costs[1],
        name="project_second_part",
    )(field, later, w2, w3)
    return (mine, theirs), second


def add_kernel(mine, received, *rest):
    outs = rest[-4:]
    core = lax.rem(lax.axis_index("gz"), 2)
    for g in range(4):
        for h in range(4):
            v, y = g + (h - g) * core, h + (g - h) * core
            outs[g][h] = mine[v, y] + received[v, y]


def add_groups(mine, received, after):
    vmem = pl.BlockSpec(memory_space=pltpu.VMEM)
    return pl.pallas_call(
        add_kernel,
        in_specs=[vmem] * 2 + [pl.BlockSpec(memory_space=pl.ANY)] * len(after),
        out_shape=[jax.ShapeDtypeStruct(mine.shape[1:], F32)] * 4,
        compiler_params=pltpu.CompilerParams(vmem_limit_bytes=8 * 2**20),
        name="add_cores",
    )(mine, received, *after)


def sum_kernel(*refs):
    ins, outs = refs[:-4], refs[-4:]
    lane = 0
    for p in range(0, len(ins), 4):
        a, b, c, d = ins[p : p + 4]
        lanes = slice(lane, lane + a.shape[-1])
        lane += a.shape[-1]
        for h in range(4):
            outs[h][:, lanes] = (a[h] + b[h]) + (c[h] + d[h])


def sum_groups(parts):
    return pl.pallas_call(
        sum_kernel,
        out_shape=[jax.ShapeDtypeStruct((8, 4096), F32)] * 4,
        compiler_params=pltpu.CompilerParams(vmem_limit_bytes=8 * 2**20),
        name="sum_first_axis",
    )(*[x for part in parts for x in part])


def finish_kernel(a, b, c, d, out):
    total = (a[...] + b[...]) + (c[...] + d[...])
    pairs = total.shape[1] // 128
    rows = total.reshape(8, pairs, 128)
    low = lax.broadcasted_iota(jnp.int32, (pairs, 128), 1) < 64
    for j in range(4):
        even, odd = rows[2 * j], rows[2 * j + 1]
        lanes = slice(j * 128, (j + 1) * 128)
        out[0:pairs, lanes] = jnp.where(low, even, pltpu.roll(odd, 64, 1))
        out[pairs : 2 * pairs, lanes] = jnp.where(low, pltpu.roll(even, 64, 1), odd)


def finish(parts):
    return pl.pallas_call(
        finish_kernel,
        out_shape=jax.ShapeDtypeStruct((parts[0].shape[1] // 64, 512), F32),
        compiler_params=pltpu.CompilerParams(vmem_limit_bytes=8 * 2**20),
        name="sum_second_axis",
    )(*parts)


def copy_kernel(x, out):
    out[...] = x[...]


def copy(x):
    return pl.pallas_call(
        copy_kernel,
        out_shape=jax.ShapeDtypeStruct(x.shape, x.dtype),
        compiler_params=pltpu.CompilerParams(vmem_limit_bytes=8 * 2**20),
        name="copy",
    )(x)


def gram_kernel(a, b, c, d, out, cols):
    z = lax.axis_index("gx")
    for off, ref in zip(OFFSETS, (a, b, c, d)):
        start = pl.multiple_of(lax.rem(z + off, 4) * 64, 64)
        cols[pl.ds(start, 64), :] = ref[...]
    hi, lo = split(a[...])
    chi, clo = split(cols[...])
    both = dot(jnp.concatenate([hi, lo], axis=0), chi, (1, 1))
    out[...] = (both[:64] + both[64:] + dot(hi, clo, (1, 1))) * (1.0 / (V * R * R))


def gram_part(parts):
    return pl.pallas_call(
        gram_kernel,
        out_shape=jax.ShapeDtypeStruct((64, 256), F32),
        scratch_shapes=[pltpu.VMEM((256, 512), F32)],
        compiler_params=pltpu.CompilerParams(vmem_limit_bytes=8 * 2**20),
        name="gram",
    )(*parts)


def pairs(target):
    out = []
    for z in range(4):
        for x in range(4):
            for y in range(4):
                for c in range(2):
                    tz, tx, ty, tc = target(z, x, y, c)
                    out.append((((z * 4 + x) * 4 + y) * 2 + c, (((tz % 4) * 4 + tx % 4) * 4 + ty % 4) * 2 + tc))
    return out


def send(x, target):
    return lax.ppermute(x, AXES, pairs(target))


def first_axis(off):
    return lambda z, x, y, c: (z, x + off * (1 - c), y + off * c, c)


def second_axis(off):
    return lambda z, x, y, c: (z, x + off * c, y + off * (1 - c), c)


def other_core(z, x, y, c):
    return (z, x, y, 1 - c)


def exchange(parts, axis):
    return [parts[0]] + [send(parts[off], axis(off)) for off in (2, 1, 3)]


def total(x, axis):
    return sum([x] + [send(x, axis(off)) for off in (1, 3, 2)])


def body(field, basis_two, basis_three):
    field = field.reshape(4, 2, 16, 2, 64, 256)
    halves = project(field, basis_two.T, basis_three)
    received = [send(theirs, other_core) for _, theirs in halves]
    groups = []
    for (mine, _), part in zip(halves, received):
        groups.append(add_groups(mine, part, groups[-1][:1] if groups else []))
    groups = sum_groups([exchange(part, first_axis) for part in groups])
    rows = finish(exchange(groups, second_axis))
    gathered = [rows] + [send(rows, lambda z, x, y, c, off=off: (z - off, x, y, c)) for off in OFFSETS[1:]]
    gram = total(total(gram_part(gathered), first_axis), second_axis)
    return (copy(rows), gram + send(gram, other_core))


def solution(mesh):
    placed = (P(None, "gx", "gz", "gy"), P("gy", None), P("gz", None))
    return jax.shard_map(
        body,
        mesh=mesh,
        in_specs=placed,
        out_specs=(P("gx", ("gy", "gz")), P("gx", None)),
        check_vma=False,
    )
```

time: 75.2 us -> 70.2 us (0.934); the launches traced: 75.1 us -> 69 us
  waiting for transfers between devices: 27.8 us -> 22.8 us
  Pallas kernels: 14.8 us -> 11.3 us
  starting transfers between devices: 30.2 us -> 33.5 us
  local copies, waits for them, and re-layouts: 0.9 us -> 0 us
    ppermute x21, waiting for transfers between devices: 27.8 us -> 22.8 us  [send(): return lax.ppermute(x, AXES, pairs(target))]
    pallas_call x5 -> x6, Pallas kernels: 14.3 us -> 10.8 us  [the longest x1 6.44 us: project(): pl.pallas_call(first_part_kernel, out_shape=(parts[0], parts[0], jax.Shap...]
    ppermute x21, starting transfers between devices: 30.2 us -> 33.5 us  [send(): return lax.ppermute(x, AXES, pairs(target))]
    unnamed x2 -> x0, local copies, waits for them, and re-layouts: 0.9 us -> none
  transfers between devices with their start and end apart: 21 -> 21, of which waited for: 18 -> 13; matrix products, arithmetic and copies ran while one was open for 0% -> 0% of each run, Pallas kernels for 9% -> 6%
where the time goes in v3:
time: 70.2 us; the launch traced here: 69 us
  starting transfers between devices  33.5 us (48%)
  waiting for transfers between devices  22.8 us (32%)
  Pallas kernels  11.3 us (16%)
  between operations  0.72 us (1%)
    ppermute x21, starting transfers between devices, send(): return lax.ppermute(x, AXES, pairs(target))  33.5 us
    ppermute x21, waiting for transfers between devices, send(): return lax.ppermute(x, AXES, pairs(target))  22.8 us
    pallas_call x1, Pallas kernels, project(): pl.pallas_call(first_part_kernel, out_shape=(parts[0], parts[0], jax.Shap...  6.44 us
    pallas_call x1, Pallas kernels, project(): pl.pallas_call(second_part_kernel, out_shape=(parts[1], parts[1]), in_spe...  3.39 us
  transfers between devices with their start and end apart: 21, of which 13 were waited for; matrix products, arithmetic and copies ran while one was open for 0% of the time, Pallas kernels for 6%

profile of v3, /device:TPU:0, one launch (start us, length us, event | category | flops | bytes accessed | tf_op | source)
XLA Modules:
  0.0 69.0 jit_solution(11004225331303104733)
XLA Ops:
  0.6 6.4 %project_first_part.1 = (f32[4,4,8,2048]{3,2,1,0:T(8,128)S(1)}, f32[4,4,8,2048]{3,2,1,0:T(8,128)S(1)}, f32[3,2,8,2,64,256]{5,4,3,2,1,0:T(8,128)S(1)}, bf16[512,256]{1,0:T(8,128)(2,1)S(1)}, bf16[384,128]{1,0:T(8,128)(2,1)S(1)}) custom-call(f32[4,2,16,2,64,256]{5,4,3,2,1,0:T(8,128)} %bitcast.2, f32[64,256]{1,0:T(8,128)} %bitcast.4, f32[64,64]{1,0:T(8,128)} %b3_in.1), custom_call_target="tpu_custom_call" | custom-call | flops 8000000000 | bytes 8388608 | tf_op jit(solution)/shard_map/project_first_part/pallas_call | solution.py:106
  7.1 0.1 collective-permute-start
  7.2 3.4 %project_second_part.1 = (f32[4,4,8,2048]{3,2,1,0:T(8,128)S(1)}, f32[4,4,8,2048]{3,2,1,0:T(8,128)S(1)}) custom-call(f32[4,2,16,2,64,256]{5,4,3,2,1,0:T(8,128)} %bitcast.3, f32[3,2,8,2,64,256]{5,4,3,2,1,0:T(8,128)S(1)} %get-tuple-element.27.early, bf16[512,256]{1,0:T(8,128)(2,1)S(1)} %get-tuple-element.28.w2, bf16[384,128]{1,0:T(8,128)(2,1)S(1)} %get-tuple-element.29.w3), custom_call_target="tpu_custom_call" | custom-call | flops 8000000000 | bytes 8388608 | tf_op jit(solution)/shard_map/project_second_part/pallas_call | solution.py:129
  10.6 0.6 collective-permute-start.4
  11.1 0.0 collective-permute-done.received
  11.2 0.1 add_cores.2
  11.3 3.2 %collective-permute-start.1 = (f32[4,8,2048]{2,1,0:T(8,128)S(1)}, f32[4,8,2048]{2,1,0:T(8,128)S(1)}, u32[]{:S(2)}, u32[]{:S(2)}) collective-permute-start(f32[4,8,2048]{2,1,0:T(8,128)S(1)} %get-tuple-element.24), channel_id=1, source_target_pairs={{0,16},{1,5},{2,18},{3,7},{4,20},{5,1},{6,22},{7,3},{8,24},{9,13},... | collective-permute-start | bytes 786440 | tf_op jit(solution)/shard_map/ppermute | solution.py:249
  14.4 0.6 collective-permute-start.2
  15.0 2.6 %collective-permute-start.3 = (f32[4,8,2048]{2,1,0:T(8,128)S(1)}, f32[4,8,2048]{2,1,0:T(8,128)S(1)}, u32[]{:S(2)}, u32[]{:S(2)}) collective-permute-start(f32[4,8,2048]{2,1,0:T(8,128)S(1)} %get-tuple-element.26), channel_id=1, source_target_pairs={{0,24},{1,7},{2,26},{3,1},{4,28},{5,3},{6,30},{7,5},{8,0},{9,15},{... | collective-permute-start | bytes 786440 | tf_op jit(solution)/shard_map/ppermute | solution.py:249
  17.7 0.0 collective-permute-done.4.received
  17.7 0.1 add_cores.3
  17.8 0.1 collective-permute-start.5
  17.9 0.8 %collective-permute-start.6 = (f32[4,8,2048]{2,1,0:T(8,128)S(1)}, f32[4,8,2048]{2,1,0:T(8,128)S(1)}, u32[]{:S(2)}, u32[]{:S(2)}) collective-permute-start(f32[4,8,2048]{2,1,0:T(8,128)S(1)} %get-tuple-element.34), channel_id=1, source_target_pairs={{0,8},{1,3},{2,10},{3,5},{4,12},{5,7},{6,14},{7,1},{8,16},{9,11},{... | collective-permute-start | bytes 786440 | tf_op jit(solution)/shard_map/ppermute | solution.py:249
  18.7 0.5 collective-permute-done.1.refs_1_
  19.2 2.8 %collective-permute-start.7 = (f32[4,8,2048]{2,1,0:T(8,128)S(1)}, f32[4,8,2048]{2,1,0:T(8,128)S(1)}, u32[]{:S(2)}, u32[]{:S(2)}) collective-permute-start(f32[4,8,2048]{2,1,0:T(8,128)S(1)} %get-tuple-element.35), channel_id=1, source_target_pairs={{0,24},{1,7},{2,26},{3,1},{4,28},{5,3},{6,30},{7,5},{8,0},{9,15},{... | collective-permute-start | bytes 786440 | tf_op jit(solution)/shard_map/ppermute | solution.py:249
  22.1 2.4 %collective-permute-done.3.refs_3_ = f32[4,8,2048]{2,1,0:T(8,128)S(1)} collective-permute-done((f32[4,8,2048]{2,1,0:T(8,128)S(1)}, f32[4,8,2048]{2,1,0:T(8,128)S(1)}, u32[]{:S(2)}, u32[]{:S(2)}) %collective-permute-start.3) | collective-permute-done | bytes 262176 | tf_op jit(solution)/shard_map/ppermute | solution.py:249
  24.4 1.4 %collective-permute-done.5.refs_5_ = f32[4,8,2048]{2,1,0:T(8,128)S(1)} collective-permute-done((f32[4,8,2048]{2,1,0:T(8,128)S(1)}, f32[4,8,2048]{2,1,0:T(8,128)S(1)}, u32[]{:S(2)}, u32[]{:S(2)}) %collective-permute-start.5) | collective-permute-done | bytes 262176 | tf_op jit(solution)/shard_map/ppermute | solution.py:249
  25.9 2.5 %collective-permute-done.6.refs_6_ = f32[4,8,2048]{2,1,0:T(8,128)S(1)} collective-permute-done((f32[4,8,2048]{2,1,0:T(8,128)S(1)}, f32[4,8,2048]{2,1,0:T(8,128)S(1)}, u32[]{:S(2)}, u32[]{:S(2)}) %collective-permute-start.6) | collective-permute-done | bytes 262176 | tf_op jit(solution)/shard_map/ppermute | solution.py:249
  28.4 0.0 collective-permute-done.7.refs_7_
  28.4 0.1 sum_first_axis.1
  28.5 3.3 %collective-permute-start.8 = (f32[8,4096]{1,0:T(8,128)S(1)}, f32[8,4096]{1,0:T(8,128)S(1)}, u32[]{:S(2)}, u32[]{:S(2)}) collective-permute-start(f32[8,4096]{1,0:T(8,128)S(1)} %get-tuple-element.37), channel_id=1, source_target_pairs={{0,4},{1,17},{2,6},{3,19},{4,0},{5,21},{6,2},{7,23},{8,12},{9,25},... | collective-permute-start | bytes 393224 | tf_op jit(solution)/shard_map/ppermute | solution.py:249
  31.7 0.7 collective-permute-start.9
  32.4 2.6 %collective-permute-start.10 = (f32[8,4096]{1,0:T(8,128)S(1)}, f32[8,4096]{1,0:T(8,128)S(1)}, u32[]{:S(2)}, u32[]{:S(2)}) collective-permute-start(f32[8,4096]{1,0:T(8,128)S(1)} %get-tuple-element.39), channel_id=1, source_target_pairs={{0,6},{1,25},{2,0},{3,27},{4,2},{5,29},{6,4},{7,31},{8,14},{9,1},{... | collective-permute-start | bytes 393224 | tf_op jit(solution)/shard_map/ppermute | solution.py:249
  35.0 0.0 collective-permute-done.8.b
  35.0 2.9 %collective-permute-done.9.c = f32[8,4096]{1,0:T(8,128)S(1)} collective-permute-done((f32[8,4096]{1,0:T(8,128)S(1)}, f32[8,4096]{1,0:T(8,128)S(1)}, u32[]{:S(2)}, u32[]{:S(2)}) %collective-permute-start.9) | collective-permute-done | bytes 131104 | tf_op jit(solution)/shard_map/ppermute | solution.py:249
  37.9 0.0 collective-permute-done.10.d
  37.9 0.1 sum_second_axis.1.x.a
  38.0 4.0 %collective-permute-start.13 = (f32[64,512]{1,0:T(8,128)S(1)}, f32[64,512]{1,0:T(8,128)S(1)}, u32[]{:S(2)}, u32[]{:S(2)}) collective-permute-start(f32[64,512]{1,0:T(8,128)S(1)} %sum_second_axis.1.x.a), channel_id=1, source_target_pairs={{0,64},{1,65},{2,66},{3,67},{4,68},{5,69},{6,70},{7,71},{8,72},{9,... | collective-permute-start | bytes 393224 | tf_op jit(solution)/shard_map/ppermute | solution.py:249
  42.0 1.0 %collective-permute-start.12 = (f32[64,512]{1,0:T(8,128)S(1)}, f32[64,512]{1,0:T(8,128)S(1)}, u32[]{:S(2)}, u32[]{:S(2)}) collective-permute-start(f32[64,512]{1,0:T(8,128)S(1)} %sum_second_axis.1.x.a), channel_id=1, source_target_pairs={{0,32},{1,33},{2,34},{3,35},{4,36},{5,37},{6,38},{7,39},{8,40},{9,... | collective-permute-start | bytes 393224 | tf_op jit(solution)/shard_map/ppermute | solution.py:249
  43.0 2.2 %collective-permute-start.11 = (f32[64,512]{1,0:T(8,128)S(1)}, f32[64,512]{1,0:T(8,128)S(1)}, u32[]{:S(2)}, u32[]{:S(2)}) collective-permute-start(f32[64,512]{1,0:T(8,128)S(1)} %sum_second_axis.1.x.a), channel_id=1, source_target_pairs={{0,96},{1,97},{2,98},{3,99},{4,100},{5,101},{6,102},{7,103},{8,104... | collective-permute-start | bytes 393224 | tf_op jit(solution)/shard_map/ppermute | solution.py:249
  45.3 2.9 %collective-permute-done.12.c = f32[64,512]{1,0:T(8,128)S(1)} collective-permute-done((f32[64,512]{1,0:T(8,128)S(1)}, f32[64,512]{1,0:T(8,128)S(1)}, u32[]{:S(2)}, u32[]{:S(2)}) %collective-permute-start.12) | collective-permute-done | bytes 131104 | tf_op jit(solution)/shard_map/ppermute | solution.py:249
  48.2 0.3 gram.1
  48.5 2.3 %collective-permute-start.16 = (f32[64,256]{1,0:T(8,128)S(1)}, f32[64,256]{1,0:T(8,128)S(1)}, u32[]{:S(2)}, u32[]{:S(2)}) collective-permute-start(f32[64,256]{1,0:T(8,128)S(1)} %gram.1), channel_id=1, source_target_pairs={{0,16},{1,5},{2,18},{3,7},{4,20},{5,1},{6,22},{7,3},{8,24},{9,13},... | collective-permute-start | bytes 196616 | tf_op jit(solution)/shard_map/ppermute | solution.py:249
  50.9 1.4 %collective-permute-start.15 = (f32[64,256]{1,0:T(8,128)S(1)}, f32[64,256]{1,0:T(8,128)S(1)}, u32[]{:S(2)}, u32[]{:S(2)}) collective-permute-start(f32[64,256]{1,0:T(8,128)S(1)} %gram.1), channel_id=1, source_target_pairs={{0,24},{1,7},{2,26},{3,1},{4,28},{5,3},{6,30},{7,5},{8,0},{9,15},{... | collective-permute-start | bytes 196616 | tf_op jit(solution)/shard_map/ppermute | solution.py:249
  52.3 0.6 collective-permute-start.14
  52.9 1.5 %collective-permute-done.16 = f32[64,256]{1,0:T(8,128)S(1)} collective-permute-done((f32[64,256]{1,0:T(8,128)S(1)}, f32[64,256]{1,0:T(8,128)S(1)}, u32[]{:S(2)}, u32[]{:S(2)}) %collective-permute-start.16) | collective-permute-done | bytes 65568 | tf_op jit(solution)/shard_map/ppermute | solution.py:249
  54.4 0.7 %collective-permute-done.15 = f32[64,256]{1,0:T(8,128)S(1)} collective-permute-done((f32[64,256]{1,0:T(8,128)S(1)}, f32[64,256]{1,0:T(8,128)S(1)}, u32[]{:S(2)}, u32[]{:S(2)}) %collective-permute-start.15) | collective-permute-done | bytes 65568 | tf_op jit(solution)/shard_map/ppermute | solution.py:249
  55.1 2.6 %collective-permute-done.14 = f32[64,256]{1,0:T(8,128)S(1)} collective-permute-done((f32[64,256]{1,0:T(8,128)S(1)}, f32[64,256]{1,0:T(8,128)S(1)}, u32[]{:S(2)}, u32[]{:S(2)}) %collective-permute-start.14) | collective-permute-done | bytes 65568 | tf_op jit(solution)/shard_map/ppermute | solution.py:249
  57.8 2.2 %collective-permute-start.19 = (f32[64,256]{1,0:T(8,128)S(1)}, f32[64,256]{1,0:T(8,128)S(1)}, u32[]{:S(2)}, u32[]{:S(2)}) collective-permute-start(f32[64,256]{1,0:T(8,128)S(1)} %add_add_fusion.1), channel_id=1, source_target_pairs={{0,4},{1,17},{2,6},{3,19},{4,0},{5,21},{6,2},{7,23},{8,12},{9,25},... | collective-permute-start | bytes 196616 | tf_op jit(solution)/shard_map/ppermute | solution.py:249
  60.0 1.6 %collective-permute-start.18 = (f32[64,256]{1,0:T(8,128)S(1)}, f32[64,256]{1,0:T(8,128)S(1)}, u32[]{:S(2)}, u32[]{:S(2)}) collective-permute-start(f32[64,256]{1,0:T(8,128)S(1)} %add_add_fusion.1), channel_id=1, source_target_pairs={{0,6},{1,25},{2,0},{3,27},{4,2},{5,29},{6,4},{7,31},{8,14},{9,1},{... | collective-permute-start | bytes 196616 | tf_op jit(solution)/shard_map/ppermute | solution.py:249
  61.5 0.8 %collective-permute-start.17 = (f32[64,256]{1,0:T(8,128)S(1)}, f32[64,256]{1,0:T(8,128)S(1)}, u32[]{:S(2)}, u32[]{:S(2)}) collective-permute-start(f32[64,256]{1,0:T(8,128)S(1)} %add_add_fusion.1), channel_id=1, source_target_pairs={{0,2},{1,9},{2,4},{3,11},{4,6},{5,13},{6,0},{7,15},{8,10},{9,17},{... | collective-permute-start | bytes 196616 | tf_op jit(solution)/shard_map/ppermute | solution.py:249
  62.3 1.3 %collective-permute-done.19 = f32[64,256]{1,0:T(8,128)S(1)} collective-permute-done((f32[64,256]{1,0:T(8,128)S(1)}, f32[64,256]{1,0:T(8,128)S(1)}, u32[]{:S(2)}, u32[]{:S(2)}) %collective-permute-start.19) | collective-permute-done | bytes 65568 | tf_op jit(solution)/shard_map/ppermute | solution.py:249
  63.6 1.6 %collective-permute-done.18 = f32[64,256]{1,0:T(8,128)S(1)} collective-permute-done((f32[64,256]{1,0:T(8,128)S(1)}, f32[64,256]{1,0:T(8,128)S(1)}, u32[]{:S(2)}, u32[]{:S(2)}) %collective-permute-start.18) | collective-permute-done | bytes 65568 | tf_op jit(solution)/shard_map/ppermute | solution.py:249
  65.2 1.8 %collective-permute-done.17 = f32[64,256]{1,0:T(8,128)S(1)} collective-permute-done((f32[64,256]{1,0:T(8,128)S(1)}, f32[64,256]{1,0:T(8,128)S(1)}, u32[]{:S(2)}, u32[]{:S(2)}) %collective-permute-start.17) | collective-permute-done | bytes 65568 | tf_op jit(solution)/shard_map/ppermute | solution.py:249
  67.0 0.1 collective-permute-start.20
  67.1 0.7 copy.6
  67.8 0.6 collective-permute-done.20
  68.4 0.6 add.27
  (5 shorter events, 0.0 us)
Async XLA Ops:
  7.1 4.1 %collective-permute-start = (f32[4,4,8,2048]{3,2,1,0:T(8,128)S(1)}, f32[4,4,8,2048]{3,2,1,0:T(8,128)S(1)}, u32[]{:S(2)}, u32[]{:S(2)}) collective-permute-start(f32[4,4,8,2048]{3,2,1,0:T(8,128)S(1)} %get-tuple-element.22), channel_id=1, source_target_pairs={{0,1},{1,0},{2,3},{3,2},{4,5},{5,4},{6,7},{7,6},{8,9},{9,8},{10,11... | collective-permute-start | bytes 3145736 | tf_op jit(solution)/shard_map/ppermute | solution.py:249
  10.6 7.1 %collective-permute-start.4 = (f32[4,4,8,2048]{3,2,1,0:T(8,128)S(1)}, f32[4,4,8,2048]{3,2,1,0:T(8,128)S(1)}, u32[]{:S(2)}, u32[]{:S(2)}) collective-permute-start(f32[4,4,8,2048]{3,2,1,0:T(8,128)S(1)} %get-tuple-element.31), channel_id=1, source_target_pairs={{0,1},{1,0},{2,3},{3,2},{4,5},{5,4},{6,7},{7,6},{8,9},{9,8},{10,11... | collective-permute-start | bytes 3145736 | tf_op jit(solution)/shard_map/ppermute | solution.py:249
  11.3 8.0 %collective-permute-start.1 = (f32[4,8,2048]{2,1,0:T(8,128)S(1)}, f32[4,8,2048]{2,1,0:T(8,128)S(1)}, u32[]{:S(2)}, u32[]{:S(2)}) collective-permute-start(f32[4,8,2048]{2,1,0:T(8,128)S(1)} %get-tuple-element.24), channel_id=1, source_target_pairs={{0,16},{1,5},{2,18},{3,7},{4,20},{5,1},{6,22},{7,3},{8,24},{9,13},... | collective-permute-start | bytes 786440 | tf_op jit(solution)/shard_map/ppermute | solution.py:249
  14.4 7.6 %collective-permute-start.2 = (f32[4,8,2048]{2,1,0:T(8,128)S(1)}, f32[4,8,2048]{2,1,0:T(8,128)S(1)}, u32[]{:S(2)}, u32[]{:S(2)}) collective-permute-start(f32[4,8,2048]{2,1,0:T(8,128)S(1)} %get-tuple-element.25), channel_id=1, source_target_pairs={{0,8},{1,3},{2,10},{3,5},{4,12},{5,7},{6,14},{7,1},{8,16},{9,11},{... | collective-permute-start | bytes 786440 | tf_op jit(solution)/shard_map/ppermute | solution.py:249
  15.0 9.4 %collective-permute-start.3 = (f32[4,8,2048]{2,1,0:T(8,128)S(1)}, f32[4,8,2048]{2,1,0:T(8,128)S(1)}, u32[]{:S(2)}, u32[]{:S(2)}) collective-permute-start(f32[4,8,2048]{2,1,0:T(8,128)S(1)} %get-tuple-element.26), channel_id=1, source_target_pairs={{0,24},{1,7},{2,26},{3,1},{4,28},{5,3},{6,30},{7,5},{8,0},{9,15},{... | collective-permute-start | bytes 786440 | tf_op jit(solution)/shard_map/ppermute | solution.py:249
  17.8 8.1 %collective-permute-start.5 = (f32[4,8,2048]{2,1,0:T(8,128)S(1)}, f32[4,8,2048]{2,1,0:T(8,128)S(1)}, u32[]{:S(2)}, u32[]{:S(2)}) collective-permute-start(f32[4,8,2048]{2,1,0:T(8,128)S(1)} %get-tuple-element.33), channel_id=1, source_target_pairs={{0,16},{1,5},{2,18},{3,7},{4,20},{5,1},{6,22},{7,3},{8,24},{9,13},... | collective-permute-start | bytes 786440 | tf_op jit(solution)/shard_map/ppermute | solution.py:249
  17.9 10.5 %collective-permute-start.6 = (f32[4,8,2048]{2,1,0:T(8,128)S(1)}, f32[4,8,2048]{2,1,0:T(8,128)S(1)}, u32[]{:S(2)}, u32[]{:S(2)}) collective-permute-start(f32[4,8,2048]{2,1,0:T(8,128)S(1)} %get-tuple-element.34), channel_id=1, source_target_pairs={{0,8},{1,3},{2,10},{3,5},{4,12},{5,7},{6,14},{7,1},{8,16},{9,11},{... | collective-permute-start | bytes 786440 | tf_op jit(solution)/shard_map/ppermute | solution.py:249
  19.2 9.1 %collective-permute-start.7 = (f32[4,8,2048]{2,1,0:T(8,128)S(1)}, f32[4,8,2048]{2,1,0:T(8,128)S(1)}, u32[]{:S(2)}, u32[]{:S(2)}) collective-permute-start(f32[4,8,2048]{2,1,0:T(8,128)S(1)} %get-tuple-element.35), channel_id=1, source_target_pairs={{0,24},{1,7},{2,26},{3,1},{4,28},{5,3},{6,30},{7,5},{8,0},{9,15},{... | collective-permute-start | bytes 786440 | tf_op jit(solution)/shard_map/ppermute | solution.py:249
  28.5 6.6 %collective-permute-start.8 = (f32[8,4096]{1,0:T(8,128)S(1)}, f32[8,4096]{1,0:T(8,128)S(1)}, u32[]{:S(2)}, u32[]{:S(2)}) collective-permute-start(f32[8,4096]{1,0:T(8,128)S(1)} %get-tuple-element.37), channel_id=1, source_target_pairs={{0,4},{1,17},{2,6},{3,19},{4,0},{5,21},{6,2},{7,23},{8,12},{9,25},... | collective-permute-start | bytes 393224 | tf_op jit(solution)/shard_map/ppermute | solution.py:249
  31.7 6.2 %collective-permute-start.9 = (f32[8,4096]{1,0:T(8,128)S(1)}, f32[8,4096]{1,0:T(8,128)S(1)}, u32[]{:S(2)}, u32[]{:S(2)}) collective-permute-start(f32[8,4096]{1,0:T(8,128)S(1)} %get-tuple-element.38), channel_id=1, source_target_pairs={{0,2},{1,9},{2,4},{3,11},{4,6},{5,13},{6,0},{7,15},{8,10},{9,17},{... | collective-permute-start | bytes 393224 | tf_op jit(solution)/shard_map/ppermute | solution.py:249
  32.4 5.5 %collective-permute-start.10 = (f32[8,4096]{1,0:T(8,128)S(1)}, f32[8,4096]{1,0:T(8,128)S(1)}, u32[]{:S(2)}, u32[]{:S(2)}) collective-permute-start(f32[8,4096]{1,0:T(8,128)S(1)} %get-tuple-element.39), channel_id=1, source_target_pairs={{0,6},{1,25},{2,0},{3,27},{4,2},{5,29},{6,4},{7,31},{8,14},{9,1},{... | collective-permute-start | bytes 393224 | tf_op jit(solution)/shard_map/ppermute | solution.py:249
  38.0 7.2 %collective-permute-start.13 = (f32[64,512]{1,0:T(8,128)S(1)}, f32[64,512]{1,0:T(8,128)S(1)}, u32[]{:S(2)}, u32[]{:S(2)}) collective-permute-start(f32[64,512]{1,0:T(8,128)S(1)} %sum_second_axis.1.x.a), channel_id=1, source_target_pairs={{0,64},{1,65},{2,66},{3,67},{4,68},{5,69},{6,70},{7,71},{8,72},{9,... | collective-permute-start | bytes 393224 | tf_op jit(solution)/shard_map/ppermute | solution.py:249
  42.0 6.2 %collective-permute-start.12 = (f32[64,512]{1,0:T(8,128)S(1)}, f32[64,512]{1,0:T(8,128)S(1)}, u32[]{:S(2)}, u32[]{:S(2)}) collective-permute-start(f32[64,512]{1,0:T(8,128)S(1)} %sum_second_axis.1.x.a), channel_id=1, source_target_pairs={{0,32},{1,33},{2,34},{3,35},{4,36},{5,37},{6,38},{7,39},{8,40},{9,... | collective-permute-start | bytes 393224 | tf_op jit(solution)/shard_map/ppermute | solution.py:249
  43.0 5.2 %collective-permute-start.11 = (f32[64,512]{1,0:T(8,128)S(1)}, f32[64,512]{1,0:T(8,128)S(1)}, u32[]{:S(2)}, u32[]{:S(2)}) collective-permute-start(f32[64,512]{1,0:T(8,128)S(1)} %sum_second_axis.1.x.a), channel_id=1, source_target_pairs={{0,96},{1,97},{2,98},{3,99},{4,100},{5,101},{6,102},{7,103},{8,104... | collective-permute-start | bytes 393224 | tf_op jit(solution)/shard_map/ppermute | solution.py:249
  48.5 5.8 %collective-permute-start.16 = (f32[64,256]{1,0:T(8,128)S(1)}, f32[64,256]{1,0:T(8,128)S(1)}, u32[]{:S(2)}, u32[]{:S(2)}) collective-permute-start(f32[64,256]{1,0:T(8,128)S(1)} %gram.1), channel_id=1, source_target_pairs={{0,16},{1,5},{2,18},{3,7},{4,20},{5,1},{6,22},{7,3},{8,24},{9,13},... | collective-permute-start | bytes 196616 | tf_op jit(solution)/shard_map/ppermute | solution.py:249
  50.9 4.3 %collective-permute-start.15 = (f32[64,256]{1,0:T(8,128)S(1)}, f32[64,256]{1,0:T(8,128)S(1)}, u32[]{:S(2)}, u32[]{:S(2)}) collective-permute-start(f32[64,256]{1,0:T(8,128)S(1)} %gram.1), channel_id=1, source_target_pairs={{0,24},{1,7},{2,26},{3,1},{4,28},{5,3},{6,30},{7,5},{8,0},{9,15},{... | collective-permute-start | bytes 196616 | tf_op jit(solution)/shard_map/ppermute | solution.py:249
  52.3 5.5 %collective-permute-start.14 = (f32[64,256]{1,0:T(8,128)S(1)}, f32[64,256]{1,0:T(8,128)S(1)}, u32[]{:S(2)}, u32[]{:S(2)}) collective-permute-start(f32[64,256]{1,0:T(8,128)S(1)} %gram.1), channel_id=1, source_target_pairs={{0,8},{1,3},{2,10},{3,5},{4,12},{5,7},{6,14},{7,1},{8,16},{9,11},{... | collective-permute-start | bytes 196616 | tf_op jit(solution)/shard_map/ppermute | solution.py:249
  57.8 5.8 %collective-permute-start.19 = (f32[64,256]{1,0:T(8,128)S(1)}, f32[64,256]{1,0:T(8,128)S(1)}, u32[]{:S(2)}, u32[]{:S(2)}) collective-permute-start(f32[64,256]{1,0:T(8,128)S(1)} %add_add_fusion.1), channel_id=1, source_target_pairs={{0,4},{1,17},{2,6},{3,19},{4,0},{5,21},{6,2},{7,23},{8,12},{9,25},... | collective-permute-start | bytes 196616 | tf_op jit(solution)/shard_map/ppermute | solution.py:249
  60.0 5.3 %collective-permute-start.18 = (f32[64,256]{1,0:T(8,128)S(1)}, f32[64,256]{1,0:T(8,128)S(1)}, u32[]{:S(2)}, u32[]{:S(2)}) collective-permute-start(f32[64,256]{1,0:T(8,128)S(1)} %add_add_fusion.1), channel_id=1, source_target_pairs={{0,6},{1,25},{2,0},{3,27},{4,2},{5,29},{6,4},{7,31},{8,14},{9,1},{... | collective-permute-start | bytes 196616 | tf_op jit(solution)/shard_map/ppermute | solution.py:249
  61.5 5.5 %collective-permute-start.17 = (f32[64,256]{1,0:T(8,128)S(1)}, f32[64,256]{1,0:T(8,128)S(1)}, u32[]{:S(2)}, u32[]{:S(2)}) collective-permute-start(f32[64,256]{1,0:T(8,128)S(1)} %add_add_fusion.1), channel_id=1, source_target_pairs={{0,2},{1,9},{2,4},{3,11},{4,6},{5,13},{6,0},{7,15},{8,10},{9,17},{... | collective-permute-start | bytes 196616 | tf_op jit(solution)/shard_map/ppermute | solution.py:249
  67.0 1.3 %collective-permute-start.20 = (f32[64,256]{1,0:T(8,128)S(1)}, f32[64,256]{1,0:T(8,128)S(1)}, u32[]{:S(2)}, u32[]{:S(2)}) collective-permute-start(f32[64,256]{1,0:T(8,128)S(1)} %add_add_fusion), channel_id=1, source_target_pairs={{0,1},{1,0},{2,3},{3,2},{4,5},{5,4},{6,7},{7,6},{8,9},{9,8},{10,11... | collective-permute-start | bytes 196616 | tf_op jit(solution)/shard_map/ppermute | solution.py:249

commit v4 on v3

--- a/solution.py
+++ b/solution.py
@@ -9,7 +9,9 @@
 
 V = 4
 R = 64
-OFFSETS = (0, 1, 3, 2)
+OFFSETS = (0, 2, 1, 3)
+FIRST = ((2, 1, 3), (2, 1, 3))
+SECOND = (1, 3, 2)
 AXES = ("gx", "gy", "gz")
 F32, BF16 = jnp.float32, jnp.bfloat16
 SIZES = (8, 8)
@@ -261,12 +263,59 @@
     return (z, x, y, 1 - c)
 
 
-def exchange(parts, axis):
-    return [parts[0]] + [send(parts[off], axis(off)) for off in (2, 1, 3)]
-
-
-def total(x, axis):
-    return sum([x] + [send(x, axis(off)) for off in (1, 3, 2)])
+def exchange(parts, axis, order):
+    return [parts[0]] + [send(parts[off], axis(off)) for off in order]
+
+
+def add_halves_kernel(*refs):
+    ins, (out, half) = refs[:-2], refs[-2:]
+    total = sum(x[...] for x in ins[1:]) + ins[0][...]
+    rows = half.shape[0]
+    out[...] = total
+    half[...] = jnp.where(lax.rem(lax.axis_index("gz"), 2) == 0, total[:rows], total[rows:])
+
+
+def add_halves(*parts):
+    rows, lanes = parts[0].shape
+    return pl.pallas_call(
+        add_halves_kernel,
+        out_shape=[jax.ShapeDtypeStruct((rows, lanes), F32), jax.ShapeDtypeStruct((rows // 2, lanes), F32)],
+        compiler_params=pltpu.CompilerParams(vmem_limit_bytes=8 * 2**20),
+        name="add_halves",
+    )(*parts)
+
+
+def hear_kernel(whole, half, out):
+    rows = half.shape[0]
+    out[...] = whole[...]
+    mine = pl.ds(pl.multiple_of(lax.rem(lax.axis_index("gz"), 2) * rows, rows), rows)
+    out[mine, :] = out[mine, :] + half[...]
+
+
+def hear(whole, half):
+    return pl.pallas_call(
+        hear_kernel,
+        out_shape=jax.ShapeDtypeStruct(whole.shape, F32),
+        compiler_params=pltpu.CompilerParams(vmem_limit_bytes=8 * 2**20),
+        name="hear",
+    )(whole, half)
+
+
+def plane_total(part):
+    terms = (part, send(part, other_core))
+    for along_x in (1, 0):
+
+        def whole(z, x, y, c):
+            step = 2 - c
+            return (z, x + step * along_x, y + step * (1 - along_x), c)
+
+        def shared(z, x, y, c):
+            return (z, x + 3 * along_x, y + 3 * (1 - along_x), c)
+
+        part, half = add_halves(*terms)
+        heard = hear(send(part, whole), send(half, shared))
+        terms = (part, heard, send(heard, other_core))
+    return sum(terms)
 
 
 def body(field, basis_two, basis_three):
@@ -276,11 +325,10 @@
     groups = []
     for (mine, _), part in zip(halves, received):
         groups.append(add_groups(mine, part, groups[-1][:1] if groups else []))
-    groups = sum_groups([exchange(part, first_axis) for part in groups])
-    rows = finish(exchange(groups, second_axis))
+    groups = sum_groups([exchange(part, first_axis, order) for part, order in zip(groups, FIRST)])
+    rows = finish(exchange(groups, second_axis, SECOND))
     gathered = [rows] + [send(rows, lambda z, x, y, c, off=off: (z - off, x, y, c)) for off in OFFSETS[1:]]
-    gram = total(total(gram_part(gathered), first_axis), second_axis)
-    return (copy(rows), gram + send(gram, other_core))
+    return (copy(rows), plane_total(gram_part(gathered)))
 
 
 def solution(mesh):

time: 70.2 us -> 67.7 us (0.964)
  starting transfers between devices: 33.5 us -> 29.4 us
  waiting for transfers between devices: 22.8 us -> 24.4 us
    ppermute x21, starting transfers between devices: 33.5 us -> 29.4 us  [send(): return lax.ppermute(x, AXES, pairs(target))]
    ppermute x21, waiting for transfers between devices: 22.8 us -> 24.4 us  [send(): return lax.ppermute(x, AXES, pairs(target))]
  transfers between devices with their start and end apart: 21 -> 21, of which waited for: 13 -> 14; matrix products, arithmetic and copies ran while one was open for 0% -> 0% of each run, Pallas kernels for 6% -> 6%
where the time goes in v4:
time: 67.7 us; the launch traced here: 66.5 us
  starting transfers between devices  29.4 us (43%)
  waiting for transfers between devices  24.4 us (36%)
  Pallas kernels  11.3 us (17%)
  between operations  0.75 us (1%)
    ppermute x21, starting transfers between devices, send(): return lax.ppermute(x, AXES, pairs(target))  29.4 us
    ppermute x21, waiting for transfers between devices, send(): return lax.ppermute(x, AXES, pairs(target))  24.4 us
    pallas_call x1, Pallas kernels, project(): pl.pallas_call(first_part_kernel, out_shape=(parts[0], parts[0], jax.Shap...  6.44 us
    pallas_call x1, Pallas kernels, project(): pl.pallas_call(second_part_kernel, out_shape=(parts[1], parts[1]), in_spe...  3.39 us
  transfers between devices with their start and end apart: 21, of which 14 were waited for; matrix products, arithmetic and copies ran while one was open for 0% of the time, Pallas kernels for 6%

profile of v4, /device:TPU:0, one launch (start us, length us, event | category | flops | bytes accessed | tf_op | source)
XLA Modules:
  0.0 66.5 jit_solution(8562861149618298587)
XLA Ops:
  0.6 6.4 %project_first_part.1 = (f32[4,4,8,2048]{3,2,1,0:T(8,128)S(1)}, f32[4,4,8,2048]{3,2,1,0:T(8,128)S(1)}, f32[3,2,8,2,64,256]{5,4,3,2,1,0:T(8,128)S(1)}, bf16[512,256]{1,0:T(8,128)(2,1)S(1)}, bf16[384,128]{1,0:T(8,128)(2,1)S(1)}) custom-call(f32[4,2,16,2,64,256]{5,4,3,2,1,0:T(8,128)} %bitcast.2, f32[64,256]{1,0:T(8,128)} %bitcast.4, f32[64,64]{1,0:T(8,128)} %b3_in.1), custom_call_target="tpu_custom_call" | custom-call | flops 8000000000 | bytes 8388608 | tf_op jit(solution)/shard_map/project_first_part/pallas_call | solution.py:108
  7.1 0.1 collective-permute-start
  7.2 3.4 %project_second_part.1 = (f32[4,4,8,2048]{3,2,1,0:T(8,128)S(1)}, f32[4,4,8,2048]{3,2,1,0:T(8,128)S(1)}) custom-call(f32[4,2,16,2,64,256]{5,4,3,2,1,0:T(8,128)} %bitcast.3, f32[3,2,8,2,64,256]{5,4,3,2,1,0:T(8,128)S(1)} %get-tuple-element.31.early, bf16[512,256]{1,0:T(8,128)(2,1)S(1)} %get-tuple-element.32.w2, bf16[384,128]{1,0:T(8,128)(2,1)S(1)} %get-tuple-element.33.w3), custom_call_target="tpu_custom_call" | custom-call | flops 8000000000 | bytes 8388608 | tf_op jit(solution)/shard_map/project_second_part/pallas_call | solution.py:131
  10.6 0.6 collective-permute-start.4
  11.2 0.1 add_cores.2
  11.3 3.2 %collective-permute-start.1 = (f32[4,8,2048]{2,1,0:T(8,128)S(1)}, f32[4,8,2048]{2,1,0:T(8,128)S(1)}, u32[]{:S(2)}, u32[]{:S(2)}) collective-permute-start(f32[4,8,2048]{2,1,0:T(8,128)S(1)} %get-tuple-element.28), channel_id=1, source_target_pairs={{0,16},{1,5},{2,18},{3,7},{4,20},{5,1},{6,22},{7,3},{8,24},{9,13},... | collective-permute-start | bytes 786440 | tf_op jit(solution)/shard_map/ppermute | solution.py:251
  14.4 0.6 collective-permute-start.2
  15.0 2.6 %collective-permute-start.3 = (f32[4,8,2048]{2,1,0:T(8,128)S(1)}, f32[4,8,2048]{2,1,0:T(8,128)S(1)}, u32[]{:S(2)}, u32[]{:S(2)}) collective-permute-start(f32[4,8,2048]{2,1,0:T(8,128)S(1)} %get-tuple-element.30), channel_id=1, source_target_pairs={{0,24},{1,7},{2,26},{3,1},{4,28},{5,3},{6,30},{7,5},{8,0},{9,15},{... | collective-permute-start | bytes 786440 | tf_op jit(solution)/shard_map/ppermute | solution.py:251
  17.7 0.0 collective-permute-done.4.received
  17.7 0.1 add_cores.3
  17.8 0.1 collective-permute-start.5
  17.9 0.8 %collective-permute-start.6 = (f32[4,8,2048]{2,1,0:T(8,128)S(1)}, f32[4,8,2048]{2,1,0:T(8,128)S(1)}, u32[]{:S(2)}, u32[]{:S(2)}) collective-permute-start(f32[4,8,2048]{2,1,0:T(8,128)S(1)} %get-tuple-element.38), channel_id=1, source_target_pairs={{0,8},{1,3},{2,10},{3,5},{4,12},{5,7},{6,14},{7,1},{8,16},{9,11},{... | collective-permute-start | bytes 786440 | tf_op jit(solution)/shard_map/ppermute | solution.py:251
  18.7 0.5 collective-permute-done.1.refs_1_
  19.2 2.8 %collective-permute-start.7 = (f32[4,8,2048]{2,1,0:T(8,128)S(1)}, f32[4,8,2048]{2,1,0:T(8,128)S(1)}, u32[]{:S(2)}, u32[]{:S(2)}) collective-permute-start(f32[4,8,2048]{2,1,0:T(8,128)S(1)} %get-tuple-element.39), channel_id=1, source_target_pairs={{0,24},{1,7},{2,26},{3,1},{4,28},{5,3},{6,30},{7,5},{8,0},{9,15},{... | collective-permute-start | bytes 786440 | tf_op jit(solution)/shard_map/ppermute | solution.py:251
  22.1 0.0 collective-permute-done.2.refs_2_
  22.1 2.4 %collective-permute-done.3.refs_3_ = f32[4,8,2048]{2,1,0:T(8,128)S(1)} collective-permute-done((f32[4,8,2048]{2,1,0:T(8,128)S(1)}, f32[4,8,2048]{2,1,0:T(8,128)S(1)}, u32[]{:S(2)}, u32[]{:S(2)}) %collective-permute-start.3) | collective-permute-done | bytes 262176 | tf_op jit(solution)/shard_map/ppermute | solution.py:251
  24.4 1.4 %collective-permute-done.5.refs_5_ = f32[4,8,2048]{2,1,0:T(8,128)S(1)} collective-permute-done((f32[4,8,2048]{2,1,0:T(8,128)S(1)}, f32[4,8,2048]{2,1,0:T(8,128)S(1)}, u32[]{:S(2)}, u32[]{:S(2)}) %collective-permute-start.5) | collective-permute-done | bytes 262176 | tf_op jit(solution)/shard_map/ppermute | solution.py:251
  25.9 2.5 %collective-permute-done.6.refs_6_ = f32[4,8,2048]{2,1,0:T(8,128)S(1)} collective-permute-done((f32[4,8,2048]{2,1,0:T(8,128)S(1)}, f32[4,8,2048]{2,1,0:T(8,128)S(1)}, u32[]{:S(2)}, u32[]{:S(2)}) %collective-permute-start.6) | collective-permute-done | bytes 262176 | tf_op jit(solution)/shard_map/ppermute | solution.py:251
  28.4 0.1 sum_first_axis.1
  28.5 1.6 %collective-permute-start.8 = (f32[8,4096]{1,0:T(8,128)S(1)}, f32[8,4096]{1,0:T(8,128)S(1)}, u32[]{:S(2)}, u32[]{:S(2)}) collective-permute-start(f32[8,4096]{1,0:T(8,128)S(1)} %get-tuple-element.41), channel_id=1, source_target_pairs={{0,2},{1,9},{2,4},{3,11},{4,6},{5,13},{6,0},{7,15},{8,10},{9,17},{... | collective-permute-start | bytes 393224 | tf_op jit(solution)/shard_map/ppermute | solution.py:251
  30.1 1.7 %collective-permute-start.9 = (f32[8,4096]{1,0:T(8,128)S(1)}, f32[8,4096]{1,0:T(8,128)S(1)}, u32[]{:S(2)}, u32[]{:S(2)}) collective-permute-start(f32[8,4096]{1,0:T(8,128)S(1)} %get-tuple-element.42), channel_id=1, source_target_pairs={{0,6},{1,25},{2,0},{3,27},{4,2},{5,29},{6,4},{7,31},{8,14},{9,1},{... | collective-permute-start | bytes 393224 | tf_op jit(solution)/shard_map/ppermute | solution.py:251
  31.8 2.0 %collective-permute-start.10 = (f32[8,4096]{1,0:T(8,128)S(1)}, f32[8,4096]{1,0:T(8,128)S(1)}, u32[]{:S(2)}, u32[]{:S(2)}) collective-permute-start(f32[8,4096]{1,0:T(8,128)S(1)} %get-tuple-element.43), channel_id=1, source_target_pairs={{0,4},{1,17},{2,6},{3,19},{4,0},{5,21},{6,2},{7,23},{8,12},{9,25},... | collective-permute-start | bytes 393224 | tf_op jit(solution)/shard_map/ppermute | solution.py:251
  33.8 1.0 %collective-permute-done.8.b = f32[8,4096]{1,0:T(8,128)S(1)} collective-permute-done((f32[8,4096]{1,0:T(8,128)S(1)}, f32[8,4096]{1,0:T(8,128)S(1)}, u32[]{:S(2)}, u32[]{:S(2)}) %collective-permute-start.8) | collective-permute-done | bytes 131104 | tf_op jit(solution)/shard_map/ppermute | solution.py:251
  34.7 0.4 collective-permute-done.9.c
  35.1 3.2 %collective-permute-done.10.d = f32[8,4096]{1,0:T(8,128)S(1)} collective-permute-done((f32[8,4096]{1,0:T(8,128)S(1)}, f32[8,4096]{1,0:T(8,128)S(1)}, u32[]{:S(2)}, u32[]{:S(2)}) %collective-permute-start.10) | collective-permute-done | bytes 131104 | tf_op jit(solution)/shard_map/ppermute | solution.py:251
  38.2 0.1 sum_second_axis.1.x.a
  38.4 2.0 %collective-permute-start.13 = (f32[64,512]{1,0:T(8,128)S(1)}, f32[64,512]{1,0:T(8,128)S(1)}, u32[]{:S(2)}, u32[]{:S(2)}) collective-permute-start(f32[64,512]{1,0:T(8,128)S(1)} %sum_second_axis.1.x.a), channel_id=1, source_target_pairs={{0,32},{1,33},{2,34},{3,35},{4,36},{5,37},{6,38},{7,39},{8,40},{9,... | collective-permute-start | bytes 393224 | tf_op jit(solution)/shard_map/ppermute | solution.py:251
  40.4 2.4 %collective-permute-start.12 = (f32[64,512]{1,0:T(8,128)S(1)}, f32[64,512]{1,0:T(8,128)S(1)}, u32[]{:S(2)}, u32[]{:S(2)}) collective-permute-start(f32[64,512]{1,0:T(8,128)S(1)} %sum_second_axis.1.x.a), channel_id=1, source_target_pairs={{0,96},{1,97},{2,98},{3,99},{4,100},{5,101},{6,102},{7,103},{8,104... | collective-permute-start | bytes 393224 | tf_op jit(solution)/shard_map/ppermute | solution.py:251
  42.7 1.6 %collective-permute-start.11 = (f32[64,512]{1,0:T(8,128)S(1)}, f32[64,512]{1,0:T(8,128)S(1)}, u32[]{:S(2)}, u32[]{:S(2)}) collective-permute-start(f32[64,512]{1,0:T(8,128)S(1)} %sum_second_axis.1.x.a), channel_id=1, source_target_pairs={{0,64},{1,65},{2,66},{3,67},{4,68},{5,69},{6,70},{7,71},{8,72},{9,... | collective-permute-start | bytes 393224 | tf_op jit(solution)/shard_map/ppermute | solution.py:251
  44.3 2.2 %collective-permute-done.13.d = f32[64,512]{1,0:T(8,128)S(1)} collective-permute-done((f32[64,512]{1,0:T(8,128)S(1)}, f32[64,512]{1,0:T(8,128)S(1)}, u32[]{:S(2)}, u32[]{:S(2)}) %collective-permute-start.13) | collective-permute-done | bytes 131104 | tf_op jit(solution)/shard_map/ppermute | solution.py:251
  46.6 0.0 collective-permute-done.12.c
  46.6 2.6 %collective-permute-done.11.b = f32[64,512]{1,0:T(8,128)S(1)} collective-permute-done((f32[64,512]{1,0:T(8,128)S(1)}, f32[64,512]{1,0:T(8,128)S(1)}, u32[]{:S(2)}, u32[]{:S(2)}) %collective-permute-start.11) | collective-permute-done | bytes 131104 | tf_op jit(solution)/shard_map/ppermute | solution.py:251
  49.2 0.3 gram.1.refs_0_
  49.6 0.1 collective-permute-start.14
  49.6 1.2 %collective-permute-done.14.refs_1_ = f32[64,256]{1,0:T(8,128)S(1)} collective-permute-done((f32[64,256]{1,0:T(8,128)S(1)}, f32[64,256]{1,0:T(8,128)S(1)}, u32[]{:S(2)}, u32[]{:S(2)}) %collective-permute-start.14) | collective-permute-done | bytes 65568 | tf_op jit(solution)/shard_map/ppermute | solution.py:251
  50.9 2.3 %collective-permute-start.15 = (f32[64,256]{1,0:T(8,128)S(1)}, f32[64,256]{1,0:T(8,128)S(1)}, u32[]{:S(2)}, u32[]{:S(2)}) collective-permute-start(f32[64,256]{1,0:T(8,128)S(1)} %get-tuple-element.44.refs_0_), channel_id=1, source_target_pairs={{0,16},{1,9},{2,18},{3,11},{4,20},{5,13},{6,22},{7,15},{8,24},{9,1... | collective-permute-start | bytes 196616 | tf_op jit(solution)/shard_map/ppermute | solution.py:251
  53.2 1.4 %collective-permute-start.16 = (f32[32,256]{1,0:T(8,128)S(1)}, f32[32,256]{1,0:T(8,128)S(1)}, u32[]{:S(2)}, u32[]{:S(2)}) collective-permute-start(f32[32,256]{1,0:T(8,128)S(1)} %get-tuple-element.45), channel_id=1, source_target_pairs={{0,24},{1,25},{2,26},{3,27},{4,28},{5,29},{6,30},{7,31},{8,0},{9,1... | collective-permute-start | bytes 98312 | tf_op jit(solution)/shard_map/ppermute | solution.py:251
  54.6 2.5 %collective-permute-done.16.half = f32[32,256]{1,0:T(8,128)S(1)} collective-permute-done((f32[32,256]{1,0:T(8,128)S(1)}, f32[32,256]{1,0:T(8,128)S(1)}, u32[]{:S(2)}, u32[]{:S(2)}) %collective-permute-start.16) | collective-permute-done | bytes 32800 | tf_op jit(solution)/shard_map/ppermute | solution.py:251
  57.1 0.1 collective-permute-start.17
  57.2 1.2 %collective-permute-done.17.refs_2_ = f32[64,256]{1,0:T(8,128)S(1)} collective-permute-done((f32[64,256]{1,0:T(8,128)S(1)}, f32[64,256]{1,0:T(8,128)S(1)}, u32[]{:S(2)}, u32[]{:S(2)}) %collective-permute-start.17) | collective-permute-done | bytes 65568 | tf_op jit(solution)/shard_map/ppermute | solution.py:251
  58.5 2.1 %collective-permute-start.18 = (f32[64,256]{1,0:T(8,128)S(1)}, f32[64,256]{1,0:T(8,128)S(1)}, u32[]{:S(2)}, u32[]{:S(2)}) collective-permute-start(f32[64,256]{1,0:T(8,128)S(1)} %get-tuple-element.46), channel_id=1, source_target_pairs={{0,4},{1,3},{2,6},{3,5},{4,0},{5,7},{6,2},{7,1},{8,12},{9,11},{10,... | collective-permute-start | bytes 196616 | tf_op jit(solution)/shard_map/ppermute | solution.py:251
  60.6 1.2 %collective-permute-start.19 = (f32[32,256]{1,0:T(8,128)S(1)}, f32[32,256]{1,0:T(8,128)S(1)}, u32[]{:S(2)}, u32[]{:S(2)}) collective-permute-start(f32[32,256]{1,0:T(8,128)S(1)} %get-tuple-element.47), channel_id=1, source_target_pairs={{0,6},{1,7},{2,0},{3,1},{4,2},{5,3},{6,4},{7,5},{8,14},{9,15},{10,... | collective-permute-start | bytes 98312 | tf_op jit(solution)/shard_map/ppermute | solution.py:251
  61.8 2.7 %collective-permute-done.19.half = f32[32,256]{1,0:T(8,128)S(1)} collective-permute-done((f32[32,256]{1,0:T(8,128)S(1)}, f32[32,256]{1,0:T(8,128)S(1)}, u32[]{:S(2)}, u32[]{:S(2)}) %collective-permute-start.19) | collective-permute-done | bytes 32800 | tf_op jit(solution)/shard_map/ppermute | solution.py:251
  64.5 0.0 collective-permute-done.18.whole
  64.5 0.1 collective-permute-start.20
  64.6 0.7 %copy.6 = f32[64,512]{1,0:T(8,128)} custom-call(f32[64,512]{1,0:T(8,128)S(1)} %sum_second_axis.1.x.a), custom_call_target="tpu_custom_call" | custom-call | tf_op jit(solution)/shard_map/copy/pallas_call | solution.py:210
  65.3 0.6 collective-permute-done.20
  65.8 0.6 add_add_fusion
  (7 shorter events, 0.1 us)
Async XLA Ops:
  7.1 4.1 %collective-permute-start = (f32[4,4,8,2048]{3,2,1,0:T(8,128)S(1)}, f32[4,4,8,2048]{3,2,1,0:T(8,128)S(1)}, u32[]{:S(2)}, u32[]{:S(2)}) collective-permute-start(f32[4,4,8,2048]{3,2,1,0:T(8,128)S(1)} %get-tuple-element.26), channel_id=1, source_target_pairs={{0,1},{1,0},{2,3},{3,2},{4,5},{5,4},{6,7},{7,6},{8,9},{9,8},{10,11... | collective-permute-start | bytes 3145736 | tf_op jit(solution)/shard_map/ppermute | solution.py:251
  10.6 7.1 %collective-permute-start.4 = (f32[4,4,8,2048]{3,2,1,0:T(8,128)S(1)}, f32[4,4,8,2048]{3,2,1,0:T(8,128)S(1)}, u32[]{:S(2)}, u32[]{:S(2)}) collective-permute-start(f32[4,4,8,2048]{3,2,1,0:T(8,128)S(1)} %get-tuple-element.35), channel_id=1, source_target_pairs={{0,1},{1,0},{2,3},{3,2},{4,5},{5,4},{6,7},{7,6},{8,9},{9,8},{10,11... | collective-permute-start | bytes 3145736 | tf_op jit(solution)/shard_map/ppermute | solution.py:251
  11.3 8.0 %collective-permute-start.1 = (f32[4,8,2048]{2,1,0:T(8,128)S(1)}, f32[4,8,2048]{2,1,0:T(8,128)S(1)}, u32[]{:S(2)}, u32[]{:S(2)}) collective-permute-start(f32[4,8,2048]{2,1,0:T(8,128)S(1)} %get-tuple-element.28), channel_id=1, source_target_pairs={{0,16},{1,5},{2,18},{3,7},{4,20},{5,1},{6,22},{7,3},{8,24},{9,13},... | collective-permute-start | bytes 786440 | tf_op jit(solution)/shard_map/ppermute | solution.py:251
  14.4 7.6 %collective-permute-start.2 = (f32[4,8,2048]{2,1,0:T(8,128)S(1)}, f32[4,8,2048]{2,1,0:T(8,128)S(1)}, u32[]{:S(2)}, u32[]{:S(2)}) collective-permute-start(f32[4,8,2048]{2,1,0:T(8,128)S(1)} %get-tuple-element.29), channel_id=1, source_target_pairs={{0,8},{1,3},{2,10},{3,5},{4,12},{5,7},{6,14},{7,1},{8,16},{9,11},{... | collective-permute-start | bytes 786440 | tf_op jit(solution)/shard_map/ppermute | solution.py:251
  15.0 9.4 %collective-permute-start.3 = (f32[4,8,2048]{2,1,0:T(8,128)S(1)}, f32[4,8,2048]{2,1,0:T(8,128)S(1)}, u32[]{:S(2)}, u32[]{:S(2)}) collective-permute-start(f32[4,8,2048]{2,1,0:T(8,128)S(1)} %get-tuple-element.30), channel_id=1, source_target_pairs={{0,24},{1,7},{2,26},{3,1},{4,28},{5,3},{6,30},{7,5},{8,0},{9,15},{... | collective-permute-start | bytes 786440 | tf_op jit(solution)/shard_map/ppermute | solution.py:251
  17.8 8.1 %collective-permute-start.5 = (f32[4,8,2048]{2,1,0:T(8,128)S(1)}, f32[4,8,2048]{2,1,0:T(8,128)S(1)}, u32[]{:S(2)}, u32[]{:S(2)}) collective-permute-start(f32[4,8,2048]{2,1,0:T(8,128)S(1)} %get-tuple-element.37), channel_id=1, source_target_pairs={{0,16},{1,5},{2,18},{3,7},{4,20},{5,1},{6,22},{7,3},{8,24},{9,13},... | collective-permute-start | bytes 786440 | tf_op jit(solution)/shard_map/ppermute | solution.py:251
  17.9 10.5 %collective-permute-start.6 = (f32[4,8,2048]{2,1,0:T(8,128)S(1)}, f32[4,8,2048]{2,1,0:T(8,128)S(1)}, u32[]{:S(2)}, u32[]{:S(2)}) collective-permute-start(f32[4,8,2048]{2,1,0:T(8,128)S(1)} %get-tuple-element.38), channel_id=1, source_target_pairs={{0,8},{1,3},{2,10},{3,5},{4,12},{5,7},{6,14},{7,1},{8,16},{9,11},{... | collective-permute-start | bytes 786440 | tf_op jit(solution)/shard_map/ppermute | solution.py:251
  19.2 9.1 %collective-permute-start.7 = (f32[4,8,2048]{2,1,0:T(8,128)S(1)}, f32[4,8,2048]{2,1,0:T(8,128)S(1)}, u32[]{:S(2)}, u32[]{:S(2)}) collective-permute-start(f32[4,8,2048]{2,1,0:T(8,128)S(1)} %get-tuple-element.39), channel_id=1, source_target_pairs={{0,24},{1,7},{2,26},{3,1},{4,28},{5,3},{6,30},{7,5},{8,0},{9,15},{... | collective-permute-start | bytes 786440 | tf_op jit(solution)/shard_map/ppermute | solution.py:251
  28.5 6.2 %collective-permute-start.8 = (f32[8,4096]{1,0:T(8,128)S(1)}, f32[8,4096]{1,0:T(8,128)S(1)}, u32[]{:S(2)}, u32[]{:S(2)}) collective-permute-start(f32[8,4096]{1,0:T(8,128)S(1)} %get-tuple-element.41), channel_id=1, source_target_pairs={{0,2},{1,9},{2,4},{3,11},{4,6},{5,13},{6,0},{7,15},{8,10},{9,17},{... | collective-permute-start | bytes 393224 | tf_op jit(solution)/shard_map/ppermute | solution.py:251
  30.1 5.0 %collective-permute-start.9 = (f32[8,4096]{1,0:T(8,128)S(1)}, f32[8,4096]{1,0:T(8,128)S(1)}, u32[]{:S(2)}, u32[]{:S(2)}) collective-permute-start(f32[8,4096]{1,0:T(8,128)S(1)} %get-tuple-element.42), channel_id=1, source_target_pairs={{0,6},{1,25},{2,0},{3,27},{4,2},{5,29},{6,4},{7,31},{8,14},{9,1},{... | collective-permute-start | bytes 393224 | tf_op jit(solution)/shard_map/ppermute | solution.py:251
  31.8 6.5 %collective-permute-start.10 = (f32[8,4096]{1,0:T(8,128)S(1)}, f32[8,4096]{1,0:T(8,128)S(1)}, u32[]{:S(2)}, u32[]{:S(2)}) collective-permute-start(f32[8,4096]{1,0:T(8,128)S(1)} %get-tuple-element.43), channel_id=1, source_target_pairs={{0,4},{1,17},{2,6},{3,19},{4,0},{5,21},{6,2},{7,23},{8,12},{9,25},... | collective-permute-start | bytes 393224 | tf_op jit(solution)/shard_map/ppermute | solution.py:251
  38.4 8.2 %collective-permute-start.13 = (f32[64,512]{1,0:T(8,128)S(1)}, f32[64,512]{1,0:T(8,128)S(1)}, u32[]{:S(2)}, u32[]{:S(2)}) collective-permute-start(f32[64,512]{1,0:T(8,128)S(1)} %sum_second_axis.1.x.a), channel_id=1, source_target_pairs={{0,32},{1,33},{2,34},{3,35},{4,36},{5,37},{6,38},{7,39},{8,40},{9,... | collective-permute-start | bytes 393224 | tf_op jit(solution)/shard_map/ppermute | solution.py:251
  40.4 6.2 %collective-permute-start.12 = (f32[64,512]{1,0:T(8,128)S(1)}, f32[64,512]{1,0:T(8,128)S(1)}, u32[]{:S(2)}, u32[]{:S(2)}) collective-permute-start(f32[64,512]{1,0:T(8,128)S(1)} %sum_second_axis.1.x.a), channel_id=1, source_target_pairs={{0,96},{1,97},{2,98},{3,99},{4,100},{5,101},{6,102},{7,103},{8,104... | collective-permute-start | bytes 393224 | tf_op jit(solution)/shard_map/ppermute | solution.py:251
  42.7 6.5 %collective-permute-start.11 = (f32[64,512]{1,0:T(8,128)S(1)}, f32[64,512]{1,0:T(8,128)S(1)}, u32[]{:S(2)}, u32[]{:S(2)}) collective-permute-start(f32[64,512]{1,0:T(8,128)S(1)} %sum_second_axis.1.x.a), channel_id=1, source_target_pairs={{0,64},{1,65},{2,66},{3,67},{4,68},{5,69},{6,70},{7,71},{8,72},{9,... | collective-permute-start | bytes 393224 | tf_op jit(solution)/shard_map/ppermute | solution.py:251
  49.6 1.3 %collective-permute-start.14 = (f32[64,256]{1,0:T(8,128)S(1)}, f32[64,256]{1,0:T(8,128)S(1)}, u32[]{:S(2)}, u32[]{:S(2)}) collective-permute-start(f32[64,256]{1,0:T(8,128)S(1)} %gram.1.refs_0_), channel_id=1, source_target_pairs={{0,1},{1,0},{2,3},{3,2},{4,5},{5,4},{6,7},{7,6},{8,9},{9,8},{10,11... | collective-permute-start | bytes 196616 | tf_op jit(solution)/shard_map/ppermute | solution.py:251
  50.9 6.2 %collective-permute-start.15 = (f32[64,256]{1,0:T(8,128)S(1)}, f32[64,256]{1,0:T(8,128)S(1)}, u32[]{:S(2)}, u32[]{:S(2)}) collective-permute-start(f32[64,256]{1,0:T(8,128)S(1)} %get-tuple-element.44.refs_0_), channel_id=1, source_target_pairs={{0,16},{1,9},{2,18},{3,11},{4,20},{5,13},{6,22},{7,15},{8,24},{9,1... | collective-permute-start | bytes 196616 | tf_op jit(solution)/shard_map/ppermute | solution.py:251
  53.2 3.9 %collective-permute-start.16 = (f32[32,256]{1,0:T(8,128)S(1)}, f32[32,256]{1,0:T(8,128)S(1)}, u32[]{:S(2)}, u32[]{:S(2)}) collective-permute-start(f32[32,256]{1,0:T(8,128)S(1)} %get-tuple-element.45), channel_id=1, source_target_pairs={{0,24},{1,25},{2,26},{3,27},{4,28},{5,29},{6,30},{7,31},{8,0},{9,1... | collective-permute-start | bytes 98312 | tf_op jit(solution)/shard_map/ppermute | solution.py:251
  57.1 1.3 %collective-permute-start.17 = (f32[64,256]{1,0:T(8,128)S(1)}, f32[64,256]{1,0:T(8,128)S(1)}, u32[]{:S(2)}, u32[]{:S(2)}) collective-permute-start(f32[64,256]{1,0:T(8,128)S(1)} %hear.2.refs_1_), channel_id=1, source_target_pairs={{0,1},{1,0},{2,3},{3,2},{4,5},{5,4},{6,7},{7,6},{8,9},{9,8},{10,11... | collective-permute-start | bytes 196616 | tf_op jit(solution)/shard_map/ppermute | solution.py:251
  58.5 6.0 %collective-permute-start.18 = (f32[64,256]{1,0:T(8,128)S(1)}, f32[64,256]{1,0:T(8,128)S(1)}, u32[]{:S(2)}, u32[]{:S(2)}) collective-permute-start(f32[64,256]{1,0:T(8,128)S(1)} %get-tuple-element.46), channel_id=1, source_target_pairs={{0,4},{1,3},{2,6},{3,5},{4,0},{5,7},{6,2},{7,1},{8,12},{9,11},{10,... | collective-permute-start | bytes 196616 | tf_op jit(solution)/shard_map/ppermute | solution.py:251
  60.6 3.9 %collective-permute-start.19 = (f32[32,256]{1,0:T(8,128)S(1)}, f32[32,256]{1,0:T(8,128)S(1)}, u32[]{:S(2)}, u32[]{:S(2)}) collective-permute-start(f32[32,256]{1,0:T(8,128)S(1)} %get-tuple-element.47), channel_id=1, source_target_pairs={{0,6},{1,7},{2,0},{3,1},{4,2},{5,3},{6,4},{7,5},{8,14},{9,15},{10,... | collective-permute-start | bytes 98312 | tf_op jit(solution)/shard_map/ppermute | solution.py:251
  64.5 1.3 %collective-permute-start.20 = (f32[64,256]{1,0:T(8,128)S(1)}, f32[64,256]{1,0:T(8,128)S(1)}, u32[]{:S(2)}, u32[]{:S(2)}) collective-permute-start(f32[64,256]{1,0:T(8,128)S(1)} %hear.3), channel_id=1, source_target_pairs={{0,1},{1,0},{2,3},{3,2},{4,5},{5,4},{6,7},{7,6},{8,9},{9,8},{10,11... | collective-permute-start | bytes 196616 | tf_op jit(solution)/shard_map/ppermute | solution.py:251

commit v5 on v4

--- a/solution.py
+++ b/solution.py
@@ -10,7 +10,7 @@
 V = 4
 R = 64
 OFFSETS = (0, 2, 1, 3)
-FIRST = ((2, 1, 3), (2, 1, 3))
+FIRST = ((1, 3, 2), (1, 3, 2))
 SECOND = (1, 3, 2)
 AXES = ("gx", "gy", "gz")
 F32, BF16 = jnp.float32, jnp.bfloat16
@@ -75,7 +75,7 @@
     w3[256:384, :] = lo
 
     load(1).start()
-    for off, ahead in enumerate(((2,), (3, 4), (5, 6), ())):
+    for off, ahead in enumerate(((2, 3), (4, 5), (6,), ())):
         load(off).wait()
         for n in ahead:
             load(n).start()

time: 67.7 us -> 67 us (0.990)
  no operation moved by 1% of the time
where the time goes in v5:
time: 67 us; the launch traced here: 65.8 us
  starting transfers between devices  29.1 us (43%)
  waiting for transfers between devices  24.4 us (36%)
  Pallas kernels  10.9 us (16%)
  between operations  0.74 us (1%)
    ppermute x21, starting transfers between devices, send(): return lax.ppermute(x, AXES, pairs(target))  29.1 us
    ppermute x21, waiting for transfers between devices, send(): return lax.ppermute(x, AXES, pairs(target))  24.4 us
    pallas_call x1, Pallas kernels, project(): pl.pallas_call(first_part_kernel, out_shape=(parts[0], parts[0], jax.Shap...  5.99 us
    pallas_call x1, Pallas kernels, project(): pl.pallas_call(second_part_kernel, out_shape=(parts[1], parts[1]), in_spe...  3.39 us
  transfers between devices with their start and end apart: 21, of which 14 were waited for; matrix products, arithmetic and copies ran while one was open for 0% of the time, Pallas kernels for 6%

profile of v5, /device:TPU:0, one launch (start us, length us, event | category | flops | bytes accessed | tf_op | source)
XLA Modules:
  0.0 65.8 jit_solution(16695905591603317714)
XLA Ops:
  0.6 6.0 %project_first_part.1 = (f32[4,4,8,2048]{3,2,1,0:T(8,128)S(1)}, f32[4,4,8,2048]{3,2,1,0:T(8,128)S(1)}, f32[3,2,8,2,64,256]{5,4,3,2,1,0:T(8,128)S(1)}, bf16[512,256]{1,0:T(8,128)(2,1)S(1)}, bf16[384,128]{1,0:T(8,128)(2,1)S(1)}) custom-call(f32[4,2,16,2,64,256]{5,4,3,2,1,0:T(8,128)} %bitcast.2, f32[64,256]{1,0:T(8,128)} %bitcast.4, f32[64,64]{1,0:T(8,128)} %b3_in.1), custom_call_target="tpu_custom_call" | custom-call | flops 8000000000 | bytes 8388608 | tf_op jit(solution)/shard_map/project_first_part/pallas_call | solution.py:108
  6.6 0.1 collective-permute-start
  6.7 3.4 %project_second_part.1 = (f32[4,4,8,2048]{3,2,1,0:T(8,128)S(1)}, f32[4,4,8,2048]{3,2,1,0:T(8,128)S(1)}) custom-call(f32[4,2,16,2,64,256]{5,4,3,2,1,0:T(8,128)} %bitcast.3, f32[3,2,8,2,64,256]{5,4,3,2,1,0:T(8,128)S(1)} %get-tuple-element.31.early, bf16[512,256]{1,0:T(8,128)(2,1)S(1)} %get-tuple-element.32.w2, bf16[384,128]{1,0:T(8,128)(2,1)S(1)} %get-tuple-element.33.w3), custom_call_target="tpu_custom_call" | custom-call | flops 8000000000 | bytes 8388608 | tf_op jit(solution)/shard_map/project_second_part/pallas_call | solution.py:131
  10.1 0.6 collective-permute-start.4
  10.7 0.0 collective-permute-done.received
  10.7 0.1 add_cores.2
  10.8 1.6 %collective-permute-start.1 = (f32[4,8,2048]{2,1,0:T(8,128)S(1)}, f32[4,8,2048]{2,1,0:T(8,128)S(1)}, u32[]{:S(2)}, u32[]{:S(2)}) collective-permute-start(f32[4,8,2048]{2,1,0:T(8,128)S(1)} %get-tuple-element.28), channel_id=1, source_target_pairs={{0,8},{1,3},{2,10},{3,5},{4,12},{5,7},{6,14},{7,1},{8,16},{9,11},{... | collective-permute-start | bytes 786440 | tf_op jit(solution)/shard_map/ppermute | solution.py:251
  12.5 1.7 %collective-permute-start.2 = (f32[4,8,2048]{2,1,0:T(8,128)S(1)}, f32[4,8,2048]{2,1,0:T(8,128)S(1)}, u32[]{:S(2)}, u32[]{:S(2)}) collective-permute-start(f32[4,8,2048]{2,1,0:T(8,128)S(1)} %get-tuple-element.29), channel_id=1, source_target_pairs={{0,24},{1,7},{2,26},{3,1},{4,28},{5,3},{6,30},{7,5},{8,0},{9,15},{... | collective-permute-start | bytes 786440 | tf_op jit(solution)/shard_map/ppermute | solution.py:251
  14.1 1.9 %collective-permute-start.3 = (f32[4,8,2048]{2,1,0:T(8,128)S(1)}, f32[4,8,2048]{2,1,0:T(8,128)S(1)}, u32[]{:S(2)}, u32[]{:S(2)}) collective-permute-start(f32[4,8,2048]{2,1,0:T(8,128)S(1)} %get-tuple-element.30), channel_id=1, source_target_pairs={{0,16},{1,5},{2,18},{3,7},{4,20},{5,1},{6,22},{7,3},{8,24},{9,13},... | collective-permute-start | bytes 786440 | tf_op jit(solution)/shard_map/ppermute | solution.py:251
  16.0 0.0 collective-permute-done.4.received
  16.0 0.1 add_cores.3
  16.1 0.7 %collective-permute-start.5 = (f32[4,8,2048]{2,1,0:T(8,128)S(1)}, f32[4,8,2048]{2,1,0:T(8,128)S(1)}, u32[]{:S(2)}, u32[]{:S(2)}) collective-permute-start(f32[4,8,2048]{2,1,0:T(8,128)S(1)} %get-tuple-element.37), channel_id=1, source_target_pairs={{0,8},{1,3},{2,10},{3,5},{4,12},{5,7},{6,14},{7,1},{8,16},{9,11},{... | collective-permute-start | bytes 786440 | tf_op jit(solution)/shard_map/ppermute | solution.py:251
  16.8 2.6 %collective-permute-start.6 = (f32[4,8,2048]{2,1,0:T(8,128)S(1)}, f32[4,8,2048]{2,1,0:T(8,128)S(1)}, u32[]{:S(2)}, u32[]{:S(2)}) collective-permute-start(f32[4,8,2048]{2,1,0:T(8,128)S(1)} %get-tuple-element.38), channel_id=1, source_target_pairs={{0,24},{1,7},{2,26},{3,1},{4,28},{5,3},{6,30},{7,5},{8,0},{9,15},{... | collective-permute-start | bytes 786440 | tf_op jit(solution)/shard_map/ppermute | solution.py:251
  19.4 0.0 collective-permute-done.1.refs_1_
  19.4 0.9 %collective-permute-start.7 = (f32[4,8,2048]{2,1,0:T(8,128)S(1)}, f32[4,8,2048]{2,1,0:T(8,128)S(1)}, u32[]{:S(2)}, u32[]{:S(2)}) collective-permute-start(f32[4,8,2048]{2,1,0:T(8,128)S(1)} %get-tuple-element.39), channel_id=1, source_target_pairs={{0,16},{1,5},{2,18},{3,7},{4,20},{5,1},{6,22},{7,3},{8,24},{9,13},... | collective-permute-start | bytes 786440 | tf_op jit(solution)/shard_map/ppermute | solution.py:251
  20.4 2.1 %collective-permute-done.3.refs_3_ = f32[4,8,2048]{2,1,0:T(8,128)S(1)} collective-permute-done((f32[4,8,2048]{2,1,0:T(8,128)S(1)}, f32[4,8,2048]{2,1,0:T(8,128)S(1)}, u32[]{:S(2)}, u32[]{:S(2)}) %collective-permute-start.3) | collective-permute-done | bytes 262176 | tf_op jit(solution)/shard_map/ppermute | solution.py:251
  22.4 2.7 %collective-permute-done.5.refs_5_ = f32[4,8,2048]{2,1,0:T(8,128)S(1)} collective-permute-done((f32[4,8,2048]{2,1,0:T(8,128)S(1)}, f32[4,8,2048]{2,1,0:T(8,128)S(1)}, u32[]{:S(2)}, u32[]{:S(2)}) %collective-permute-start.5) | collective-permute-done | bytes 262176 | tf_op jit(solution)/shard_map/ppermute | solution.py:251
  25.1 0.0 collective-permute-done.6.refs_6_
  25.2 2.8 %collective-permute-done.7.refs_7_ = f32[4,8,2048]{2,1,0:T(8,128)S(1)} collective-permute-done((f32[4,8,2048]{2,1,0:T(8,128)S(1)}, f32[4,8,2048]{2,1,0:T(8,128)S(1)}, u32[]{:S(2)}, u32[]{:S(2)}) %collective-permute-start.7) | collective-permute-done | bytes 262176 | tf_op jit(solution)/shard_map/ppermute | solution.py:251
  28.0 0.1 sum_first_axis.1
  28.1 1.6 %collective-permute-start.8 = (f32[8,4096]{1,0:T(8,128)S(1)}, f32[8,4096]{1,0:T(8,128)S(1)}, u32[]{:S(2)}, u32[]{:S(2)}) collective-permute-start(f32[8,4096]{1,0:T(8,128)S(1)} %get-tuple-element.41), channel_id=1, source_target_pairs={{0,2},{1,9},{2,4},{3,11},{4,6},{5,13},{6,0},{7,15},{8,10},{9,17},{... | collective-permute-start | bytes 393224 | tf_op jit(solution)/shard_map/ppermute | solution.py:251
  29.7 1.7 %collective-permute-start.9 = (f32[8,4096]{1,0:T(8,128)S(1)}, f32[8,4096]{1,0:T(8,128)S(1)}, u32[]{:S(2)}, u32[]{:S(2)}) collective-permute-start(f32[8,4096]{1,0:T(8,128)S(1)} %get-tuple-element.42), channel_id=1, source_target_pairs={{0,6},{1,25},{2,0},{3,27},{4,2},{5,29},{6,4},{7,31},{8,14},{9,1},{... | collective-permute-start | bytes 393224 | tf_op jit(solution)/shard_map/ppermute | solution.py:251
  31.4 2.0 %collective-permute-start.10 = (f32[8,4096]{1,0:T(8,128)S(1)}, f32[8,4096]{1,0:T(8,128)S(1)}, u32[]{:S(2)}, u32[]{:S(2)}) collective-permute-start(f32[8,4096]{1,0:T(8,128)S(1)} %get-tuple-element.43), channel_id=1, source_target_pairs={{0,4},{1,17},{2,6},{3,19},{4,0},{5,21},{6,2},{7,23},{8,12},{9,25},... | collective-permute-start | bytes 393224 | tf_op jit(solution)/shard_map/ppermute | solution.py:251
  33.3 1.0 %collective-permute-done.8.b = f32[8,4096]{1,0:T(8,128)S(1)} collective-permute-done((f32[8,4096]{1,0:T(8,128)S(1)}, f32[8,4096]{1,0:T(8,128)S(1)}, u32[]{:S(2)}, u32[]{:S(2)}) %collective-permute-start.8) | collective-permute-done | bytes 131104 | tf_op jit(solution)/shard_map/ppermute | solution.py:251
  34.3 0.4 collective-permute-done.9.c
  34.7 3.2 %collective-permute-done.10.d = f32[8,4096]{1,0:T(8,128)S(1)} collective-permute-done((f32[8,4096]{1,0:T(8,128)S(1)}, f32[8,4096]{1,0:T(8,128)S(1)}, u32[]{:S(2)}, u32[]{:S(2)}) %collective-permute-start.10) | collective-permute-done | bytes 131104 | tf_op jit(solution)/shard_map/ppermute | solution.py:251
  37.8 0.1 sum_second_axis.1.x.a
  38.0 2.0 %collective-permute-start.13 = (f32[64,512]{1,0:T(8,128)S(1)}, f32[64,512]{1,0:T(8,128)S(1)}, u32[]{:S(2)}, u32[]{:S(2)}) collective-permute-start(f32[64,512]{1,0:T(8,128)S(1)} %sum_second_axis.1.x.a), channel_id=1, source_target_pairs={{0,32},{1,33},{2,34},{3,35},{4,36},{5,37},{6,38},{7,39},{8,40},{9,... | collective-permute-start | bytes 393224 | tf_op jit(solution)/shard_map/ppermute | solution.py:251
  40.0 2.4 %collective-permute-start.12 = (f32[64,512]{1,0:T(8,128)S(1)}, f32[64,512]{1,0:T(8,128)S(1)}, u32[]{:S(2)}, u32[]{:S(2)}) collective-permute-start(f32[64,512]{1,0:T(8,128)S(1)} %sum_second_axis.1.x.a), channel_id=1, source_target_pairs={{0,96},{1,97},{2,98},{3,99},{4,100},{5,101},{6,102},{7,103},{8,104... | collective-permute-start | bytes 393224 | tf_op jit(solution)/shard_map/ppermute | solution.py:251
  42.3 1.6 %collective-permute-start.11 = (f32[64,512]{1,0:T(8,128)S(1)}, f32[64,512]{1,0:T(8,128)S(1)}, u32[]{:S(2)}, u32[]{:S(2)}) collective-permute-start(f32[64,512]{1,0:T(8,128)S(1)} %sum_second_axis.1.x.a), channel_id=1, source_target_pairs={{0,64},{1,65},{2,66},{3,67},{4,68},{5,69},{6,70},{7,71},{8,72},{9,... | collective-permute-start | bytes 393224 | tf_op jit(solution)/shard_map/ppermute | solution.py:251
  43.9 2.5 %collective-permute-done.13.d = f32[64,512]{1,0:T(8,128)S(1)} collective-permute-done((f32[64,512]{1,0:T(8,128)S(1)}, f32[64,512]{1,0:T(8,128)S(1)}, u32[]{:S(2)}, u32[]{:S(2)}) %collective-permute-start.13) | collective-permute-done | bytes 131104 | tf_op jit(solution)/shard_map/ppermute | solution.py:251
  46.4 2.4 %collective-permute-done.11.b = f32[64,512]{1,0:T(8,128)S(1)} collective-permute-done((f32[64,512]{1,0:T(8,128)S(1)}, f32[64,512]{1,0:T(8,128)S(1)}, u32[]{:S(2)}, u32[]{:S(2)}) %collective-permute-start.11) | collective-permute-done | bytes 131104 | tf_op jit(solution)/shard_map/ppermute | solution.py:251
  48.8 0.3 gram.1.refs_0_
  49.2 0.1 collective-permute-start.14
  49.2 1.2 %collective-permute-done.14.refs_1_ = f32[64,256]{1,0:T(8,128)S(1)} collective-permute-done((f32[64,256]{1,0:T(8,128)S(1)}, f32[64,256]{1,0:T(8,128)S(1)}, u32[]{:S(2)}, u32[]{:S(2)}) %collective-permute-start.14) | collective-permute-done | bytes 65568 | tf_op jit(solution)/shard_map/ppermute | solution.py:251
  50.5 1.7 %collective-permute-start.15 = (f32[64,256]{1,0:T(8,128)S(1)}, f32[64,256]{1,0:T(8,128)S(1)}, u32[]{:S(2)}, u32[]{:S(2)}) collective-permute-start(f32[64,256]{1,0:T(8,128)S(1)} %get-tuple-element.44.refs_0_), channel_id=1, source_target_pairs={{0,16},{1,9},{2,18},{3,11},{4,20},{5,13},{6,22},{7,15},{8,24},{9,1... | collective-permute-start | bytes 196616 | tf_op jit(solution)/shard_map/ppermute | solution.py:251
  52.2 2.5 %collective-permute-start.16 = (f32[32,256]{1,0:T(8,128)S(1)}, f32[32,256]{1,0:T(8,128)S(1)}, u32[]{:S(2)}, u32[]{:S(2)}) collective-permute-start(f32[32,256]{1,0:T(8,128)S(1)} %get-tuple-element.45), channel_id=1, source_target_pairs={{0,24},{1,25},{2,26},{3,27},{4,28},{5,29},{6,30},{7,31},{8,0},{9,1... | collective-permute-start | bytes 98312 | tf_op jit(solution)/shard_map/ppermute | solution.py:251
  54.7 1.6 %collective-permute-done.16.half = f32[32,256]{1,0:T(8,128)S(1)} collective-permute-done((f32[32,256]{1,0:T(8,128)S(1)}, f32[32,256]{1,0:T(8,128)S(1)}, u32[]{:S(2)}, u32[]{:S(2)}) %collective-permute-start.16) | collective-permute-done | bytes 32800 | tf_op jit(solution)/shard_map/ppermute | solution.py:251
  56.3 0.1 collective-permute-done.15.whole
  56.4 0.1 collective-permute-start.17
  56.5 1.2 %collective-permute-done.17.refs_2_ = f32[64,256]{1,0:T(8,128)S(1)} collective-permute-done((f32[64,256]{1,0:T(8,128)S(1)}, f32[64,256]{1,0:T(8,128)S(1)}, u32[]{:S(2)}, u32[]{:S(2)}) %collective-permute-start.17) | collective-permute-done | bytes 65568 | tf_op jit(solution)/shard_map/ppermute | solution.py:251
  57.8 2.0 %collective-permute-start.18 = (f32[64,256]{1,0:T(8,128)S(1)}, f32[64,256]{1,0:T(8,128)S(1)}, u32[]{:S(2)}, u32[]{:S(2)}) collective-permute-start(f32[64,256]{1,0:T(8,128)S(1)} %get-tuple-element.46), channel_id=1, source_target_pairs={{0,4},{1,3},{2,6},{3,5},{4,0},{5,7},{6,2},{7,1},{8,12},{9,11},{10,... | collective-permute-start | bytes 196616 | tf_op jit(solution)/shard_map/ppermute | solution.py:251
  59.8 1.2 %collective-permute-start.19 = (f32[32,256]{1,0:T(8,128)S(1)}, f32[32,256]{1,0:T(8,128)S(1)}, u32[]{:S(2)}, u32[]{:S(2)}) collective-permute-start(f32[32,256]{1,0:T(8,128)S(1)} %get-tuple-element.47), channel_id=1, source_target_pairs={{0,6},{1,7},{2,0},{3,1},{4,2},{5,3},{6,4},{7,5},{8,14},{9,15},{10,... | collective-permute-start | bytes 98312 | tf_op jit(solution)/shard_map/ppermute | solution.py:251
  61.1 2.7 %collective-permute-done.19.half = f32[32,256]{1,0:T(8,128)S(1)} collective-permute-done((f32[32,256]{1,0:T(8,128)S(1)}, f32[32,256]{1,0:T(8,128)S(1)}, u32[]{:S(2)}, u32[]{:S(2)}) %collective-permute-start.19) | collective-permute-done | bytes 32800 | tf_op jit(solution)/shard_map/ppermute | solution.py:251
  63.8 0.1 collective-permute-start.20
  63.9 0.7 %copy.6 = f32[64,512]{1,0:T(8,128)} custom-call(f32[64,512]{1,0:T(8,128)S(1)} %sum_second_axis.1.x.a), custom_call_target="tpu_custom_call" | custom-call | tf_op jit(solution)/shard_map/copy/pallas_call | solution.py:210
  64.5 0.6 collective-permute-done.20
  65.1 0.6 add_add_fusion
  (7 shorter events, 0.1 us)
Async XLA Ops:
  6.6 4.1 %collective-permute-start = (f32[4,4,8,2048]{3,2,1,0:T(8,128)S(1)}, f32[4,4,8,2048]{3,2,1,0:T(8,128)S(1)}, u32[]{:S(2)}, u32[]{:S(2)}) collective-permute-start(f32[4,4,8,2048]{3,2,1,0:T(8,128)S(1)} %get-tuple-element.26), channel_id=1, source_target_pairs={{0,1},{1,0},{2,3},{3,2},{4,5},{5,4},{6,7},{7,6},{8,9},{9,8},{10,11... | collective-permute-start | bytes 3145736 | tf_op jit(solution)/shard_map/ppermute | solution.py:251
  10.1 5.9 %collective-permute-start.4 = (f32[4,4,8,2048]{3,2,1,0:T(8,128)S(1)}, f32[4,4,8,2048]{3,2,1,0:T(8,128)S(1)}, u32[]{:S(2)}, u32[]{:S(2)}) collective-permute-start(f32[4,4,8,2048]{3,2,1,0:T(8,128)S(1)} %get-tuple-element.35), channel_id=1, source_target_pairs={{0,1},{1,0},{2,3},{3,2},{4,5},{5,4},{6,7},{7,6},{8,9},{9,8},{10,11... | collective-permute-start | bytes 3145736 | tf_op jit(solution)/shard_map/ppermute | solution.py:251
  10.8 8.6 %collective-permute-start.1 = (f32[4,8,2048]{2,1,0:T(8,128)S(1)}, f32[4,8,2048]{2,1,0:T(8,128)S(1)}, u32[]{:S(2)}, u32[]{:S(2)}) collective-permute-start(f32[4,8,2048]{2,1,0:T(8,128)S(1)} %get-tuple-element.28), channel_id=1, source_target_pairs={{0,8},{1,3},{2,10},{3,5},{4,12},{5,7},{6,14},{7,1},{8,16},{9,11},{... | collective-permute-start | bytes 786440 | tf_op jit(solution)/shard_map/ppermute | solution.py:251
  12.5 7.9 %collective-permute-start.2 = (f32[4,8,2048]{2,1,0:T(8,128)S(1)}, f32[4,8,2048]{2,1,0:T(8,128)S(1)}, u32[]{:S(2)}, u32[]{:S(2)}) collective-permute-start(f32[4,8,2048]{2,1,0:T(8,128)S(1)} %get-tuple-element.29), channel_id=1, source_target_pairs={{0,24},{1,7},{2,26},{3,1},{4,28},{5,3},{6,30},{7,5},{8,0},{9,15},{... | collective-permute-start | bytes 786440 | tf_op jit(solution)/shard_map/ppermute | solution.py:251
  14.1 8.3 %collective-permute-start.3 = (f32[4,8,2048]{2,1,0:T(8,128)S(1)}, f32[4,8,2048]{2,1,0:T(8,128)S(1)}, u32[]{:S(2)}, u32[]{:S(2)}) collective-permute-start(f32[4,8,2048]{2,1,0:T(8,128)S(1)} %get-tuple-element.30), channel_id=1, source_target_pairs={{0,16},{1,5},{2,18},{3,7},{4,20},{5,1},{6,22},{7,3},{8,24},{9,13},... | collective-permute-start | bytes 786440 | tf_op jit(solution)/shard_map/ppermute | solution.py:251
  16.1 9.0 %collective-permute-start.5 = (f32[4,8,2048]{2,1,0:T(8,128)S(1)}, f32[4,8,2048]{2,1,0:T(8,128)S(1)}, u32[]{:S(2)}, u32[]{:S(2)}) collective-permute-start(f32[4,8,2048]{2,1,0:T(8,128)S(1)} %get-tuple-element.37), channel_id=1, source_target_pairs={{0,8},{1,3},{2,10},{3,5},{4,12},{5,7},{6,14},{7,1},{8,16},{9,11},{... | collective-permute-start | bytes 786440 | tf_op jit(solution)/shard_map/ppermute | solution.py:251
  16.8 8.4 %collective-permute-start.6 = (f32[4,8,2048]{2,1,0:T(8,128)S(1)}, f32[4,8,2048]{2,1,0:T(8,128)S(1)}, u32[]{:S(2)}, u32[]{:S(2)}) collective-permute-start(f32[4,8,2048]{2,1,0:T(8,128)S(1)} %get-tuple-element.38), channel_id=1, source_target_pairs={{0,24},{1,7},{2,26},{3,1},{4,28},{5,3},{6,30},{7,5},{8,0},{9,15},{... | collective-permute-start | bytes 786440 | tf_op jit(solution)/shard_map/ppermute | solution.py:251
  19.4 8.5 %collective-permute-start.7 = (f32[4,8,2048]{2,1,0:T(8,128)S(1)}, f32[4,8,2048]{2,1,0:T(8,128)S(1)}, u32[]{:S(2)}, u32[]{:S(2)}) collective-permute-start(f32[4,8,2048]{2,1,0:T(8,128)S(1)} %get-tuple-element.39), channel_id=1, source_target_pairs={{0,16},{1,5},{2,18},{3,7},{4,20},{5,1},{6,22},{7,3},{8,24},{9,13},... | collective-permute-start | bytes 786440 | tf_op jit(solution)/shard_map/ppermute | solution.py:251
  28.1 6.2 %collective-permute-start.8 = (f32[8,4096]{1,0:T(8,128)S(1)}, f32[8,4096]{1,0:T(8,128)S(1)}, u32[]{:S(2)}, u32[]{:S(2)}) collective-permute-start(f32[8,4096]{1,0:T(8,128)S(1)} %get-tuple-element.41), channel_id=1, source_target_pairs={{0,2},{1,9},{2,4},{3,11},{4,6},{5,13},{6,0},{7,15},{8,10},{9,17},{... | collective-permute-start | bytes 393224 | tf_op jit(solution)/shard_map/ppermute | solution.py:251
  29.7 5.0 %collective-permute-start.9 = (f32[8,4096]{1,0:T(8,128)S(1)}, f32[8,4096]{1,0:T(8,128)S(1)}, u32[]{:S(2)}, u32[]{:S(2)}) collective-permute-start(f32[8,4096]{1,0:T(8,128)S(1)} %get-tuple-element.42), channel_id=1, source_target_pairs={{0,6},{1,25},{2,0},{3,27},{4,2},{5,29},{6,4},{7,31},{8,14},{9,1},{... | collective-permute-start | bytes 393224 | tf_op jit(solution)/shard_map/ppermute | solution.py:251
  31.4 6.5 %collective-permute-start.10 = (f32[8,4096]{1,0:T(8,128)S(1)}, f32[8,4096]{1,0:T(8,128)S(1)}, u32[]{:S(2)}, u32[]{:S(2)}) collective-permute-start(f32[8,4096]{1,0:T(8,128)S(1)} %get-tuple-element.43), channel_id=1, source_target_pairs={{0,4},{1,17},{2,6},{3,19},{4,0},{5,21},{6,2},{7,23},{8,12},{9,25},... | collective-permute-start | bytes 393224 | tf_op jit(solution)/shard_map/ppermute | solution.py:251
  38.0 8.5 %collective-permute-start.13 = (f32[64,512]{1,0:T(8,128)S(1)}, f32[64,512]{1,0:T(8,128)S(1)}, u32[]{:S(2)}, u32[]{:S(2)}) collective-permute-start(f32[64,512]{1,0:T(8,128)S(1)} %sum_second_axis.1.x.a), channel_id=1, source_target_pairs={{0,32},{1,33},{2,34},{3,35},{4,36},{5,37},{6,38},{7,39},{8,40},{9,... | collective-permute-start | bytes 393224 | tf_op jit(solution)/shard_map/ppermute | solution.py:251
  40.0 6.5 %collective-permute-start.12 = (f32[64,512]{1,0:T(8,128)S(1)}, f32[64,512]{1,0:T(8,128)S(1)}, u32[]{:S(2)}, u32[]{:S(2)}) collective-permute-start(f32[64,512]{1,0:T(8,128)S(1)} %sum_second_axis.1.x.a), channel_id=1, source_target_pairs={{0,96},{1,97},{2,98},{3,99},{4,100},{5,101},{6,102},{7,103},{8,104... | collective-permute-start | bytes 393224 | tf_op jit(solution)/shard_map/ppermute | solution.py:251
  42.3 6.5 %collective-permute-start.11 = (f32[64,512]{1,0:T(8,128)S(1)}, f32[64,512]{1,0:T(8,128)S(1)}, u32[]{:S(2)}, u32[]{:S(2)}) collective-permute-start(f32[64,512]{1,0:T(8,128)S(1)} %sum_second_axis.1.x.a), channel_id=1, source_target_pairs={{0,64},{1,65},{2,66},{3,67},{4,68},{5,69},{6,70},{7,71},{8,72},{9,... | collective-permute-start | bytes 393224 | tf_op jit(solution)/shard_map/ppermute | solution.py:251
  49.2 1.3 %collective-permute-start.14 = (f32[64,256]{1,0:T(8,128)S(1)}, f32[64,256]{1,0:T(8,128)S(1)}, u32[]{:S(2)}, u32[]{:S(2)}) collective-permute-start(f32[64,256]{1,0:T(8,128)S(1)} %gram.1.refs_0_), channel_id=1, source_target_pairs={{0,1},{1,0},{2,3},{3,2},{4,5},{5,4},{6,7},{7,6},{8,9},{9,8},{10,11... | collective-permute-start | bytes 196616 | tf_op jit(solution)/shard_map/ppermute | solution.py:251
  50.5 5.9 %collective-permute-start.15 = (f32[64,256]{1,0:T(8,128)S(1)}, f32[64,256]{1,0:T(8,128)S(1)}, u32[]{:S(2)}, u32[]{:S(2)}) collective-permute-start(f32[64,256]{1,0:T(8,128)S(1)} %get-tuple-element.44.refs_0_), channel_id=1, source_target_pairs={{0,16},{1,9},{2,18},{3,11},{4,20},{5,13},{6,22},{7,15},{8,24},{9,1... | collective-permute-start | bytes 196616 | tf_op jit(solution)/shard_map/ppermute | solution.py:251
  52.2 4.1 %collective-permute-start.16 = (f32[32,256]{1,0:T(8,128)S(1)}, f32[32,256]{1,0:T(8,128)S(1)}, u32[]{:S(2)}, u32[]{:S(2)}) collective-permute-start(f32[32,256]{1,0:T(8,128)S(1)} %get-tuple-element.45), channel_id=1, source_target_pairs={{0,24},{1,25},{2,26},{3,27},{4,28},{5,29},{6,30},{7,31},{8,0},{9,1... | collective-permute-start | bytes 98312 | tf_op jit(solution)/shard_map/ppermute | solution.py:251
  56.4 1.3 %collective-permute-start.17 = (f32[64,256]{1,0:T(8,128)S(1)}, f32[64,256]{1,0:T(8,128)S(1)}, u32[]{:S(2)}, u32[]{:S(2)}) collective-permute-start(f32[64,256]{1,0:T(8,128)S(1)} %hear.2.refs_1_), channel_id=1, source_target_pairs={{0,1},{1,0},{2,3},{3,2},{4,5},{5,4},{6,7},{7,6},{8,9},{9,8},{10,11... | collective-permute-start | bytes 196616 | tf_op jit(solution)/shard_map/ppermute | solution.py:251
  57.8 6.0 %collective-permute-start.18 = (f32[64,256]{1,0:T(8,128)S(1)}, f32[64,256]{1,0:T(8,128)S(1)}, u32[]{:S(2)}, u32[]{:S(2)}) collective-permute-start(f32[64,256]{1,0:T(8,128)S(1)} %get-tuple-element.46), channel_id=1, source_target_pairs={{0,4},{1,3},{2,6},{3,5},{4,0},{5,7},{6,2},{7,1},{8,12},{9,11},{10,... | collective-permute-start | bytes 196616 | tf_op jit(solution)/shard_map/ppermute | solution.py:251
  59.8 3.9 %collective-permute-start.19 = (f32[32,256]{1,0:T(8,128)S(1)}, f32[32,256]{1,0:T(8,128)S(1)}, u32[]{:S(2)}, u32[]{:S(2)}) collective-permute-start(f32[32,256]{1,0:T(8,128)S(1)} %get-tuple-element.47), channel_id=1, source_target_pairs={{0,6},{1,7},{2,0},{3,1},{4,2},{5,3},{6,4},{7,5},{8,14},{9,15},{10,... | collective-permute-start | bytes 98312 | tf_op jit(solution)/shard_map/ppermute | solution.py:251
  63.8 1.3 %collective-permute-start.20 = (f32[64,256]{1,0:T(8,128)S(1)}, f32[64,256]{1,0:T(8,128)S(1)}, u32[]{:S(2)}, u32[]{:S(2)}) collective-permute-start(f32[64,256]{1,0:T(8,128)S(1)} %hear.3), channel_id=1, source_target_pairs={{0,1},{1,0},{2,3},{3,2},{4,5},{5,4},{6,7},{7,6},{8,9},{9,8},{10,11... | collective-permute-start | bytes 196616 | tf_op jit(solution)/shard_map/ppermute | solution.py:251

commit v6 on v5

--- a/solution.py
+++ b/solution.py
@@ -9,9 +9,9 @@
 
 V = 4
 R = 64
-OFFSETS = (0, 2, 1, 3)
+OFFSETS = (0, 1, 2, 3)
 FIRST = ((1, 3, 2), (1, 3, 2))
-SECOND = (1, 3, 2)
+SECOND = (1, 2, 3)
 AXES = ("gx", "gy", "gz")
 F32, BF16 = jnp.float32, jnp.bfloat16
 SIZES = (8, 8)
@@ -306,7 +306,7 @@
     for along_x in (1, 0):
 
         def whole(z, x, y, c):
-            step = 2 - c
+            step = 1 + c
             return (z, x + step * along_x, y + step * (1 - along_x), c)
 
         def shared(z, x, y, c):

time: 67 us -> 66 us (0.985)
  waiting for transfers between devices: 24.4 us -> 23.1 us
    ppermute x21, waiting for transfers between devices: 24.4 us -> 23.1 us  [send(): return lax.ppermute(x, AXES, pairs(target))]
  transfers between devices with their start and end apart: 21 -> 21, of which waited for: 14 -> 16; matrix products, arithmetic and copies ran while one was open for 0% -> 0% of each run, Pallas kernels for 6% -> 7%
where the time goes in v6:
time: 66 us; the launch traced here: 64.8 us
  starting transfers between devices  29.4 us (45%)
  waiting for transfers between devices  23.1 us (35%)
  Pallas kernels  10.9 us (17%)
  between operations  0.73 us (1%)
    ppermute x21, starting transfers between devices, send(): return lax.ppermute(x, AXES, pairs(target))  29.4 us
    ppermute x21, waiting for transfers between devices, send(): return lax.ppermute(x, AXES, pairs(target))  23.1 us
    pallas_call x1, Pallas kernels, project(): pl.pallas_call(first_part_kernel, out_shape=(parts[0], parts[0], jax.Shap...  5.99 us
    pallas_call x1, Pallas kernels, project(): pl.pallas_call(second_part_kernel, out_shape=(parts[1], parts[1]), in_spe...  3.39 us
  transfers between devices with their start and end apart: 21, of which 16 were waited for; matrix products, arithmetic and copies ran while one was open for 0% of the time, Pallas kernels for 7%

profile of v6, /device:TPU:0, one launch (start us, length us, event | category | flops | bytes accessed | tf_op | source)
XLA Modules:
  0.0 64.8 jit_solution(15380698490400591720)
XLA Ops:
  0.6 6.0 %project_first_part.1 = (f32[4,4,8,2048]{3,2,1,0:T(8,128)S(1)}, f32[4,4,8,2048]{3,2,1,0:T(8,128)S(1)}, f32[3,2,8,2,64,256]{5,4,3,2,1,0:T(8,128)S(1)}, bf16[512,256]{1,0:T(8,128)(2,1)S(1)}, bf16[384,128]{1,0:T(8,128)(2,1)S(1)}) custom-call(f32[4,2,16,2,64,256]{5,4,3,2,1,0:T(8,128)} %bitcast.2, f32[64,256]{1,0:T(8,128)} %bitcast.4, f32[64,64]{1,0:T(8,128)} %b3_in.1), custom_call_target="tpu_custom_call" | custom-call | flops 8000000000 | bytes 8388608 | tf_op jit(solution)/shard_map/project_first_part/pallas_call | solution.py:108
  6.6 0.1 collective-permute-start
  6.7 3.4 %project_second_part.1 = (f32[4,4,8,2048]{3,2,1,0:T(8,128)S(1)}, f32[4,4,8,2048]{3,2,1,0:T(8,128)S(1)}) custom-call(f32[4,2,16,2,64,256]{5,4,3,2,1,0:T(8,128)} %bitcast.3, f32[3,2,8,2,64,256]{5,4,3,2,1,0:T(8,128)S(1)} %get-tuple-element.31.early, bf16[512,256]{1,0:T(8,128)(2,1)S(1)} %get-tuple-element.32.w2, bf16[384,128]{1,0:T(8,128)(2,1)S(1)} %get-tuple-element.33.w3), custom_call_target="tpu_custom_call" | custom-call | flops 8000000000 | bytes 8388608 | tf_op jit(solution)/shard_map/project_second_part/pallas_call | solution.py:131
  10.1 0.6 collective-permute-start.4
  10.7 0.0 collective-permute-done.received
  10.7 0.1 add_cores.2
  10.8 1.6 %collective-permute-start.1 = (f32[4,8,2048]{2,1,0:T(8,128)S(1)}, f32[4,8,2048]{2,1,0:T(8,128)S(1)}, u32[]{:S(2)}, u32[]{:S(2)}) collective-permute-start(f32[4,8,2048]{2,1,0:T(8,128)S(1)} %get-tuple-element.28), channel_id=1, source_target_pairs={{0,8},{1,3},{2,10},{3,5},{4,12},{5,7},{6,14},{7,1},{8,16},{9,11},{... | collective-permute-start | bytes 786440 | tf_op jit(solution)/shard_map/ppermute | solution.py:251
  12.5 1.7 %collective-permute-start.2 = (f32[4,8,2048]{2,1,0:T(8,128)S(1)}, f32[4,8,2048]{2,1,0:T(8,128)S(1)}, u32[]{:S(2)}, u32[]{:S(2)}) collective-permute-start(f32[4,8,2048]{2,1,0:T(8,128)S(1)} %get-tuple-element.29), channel_id=1, source_target_pairs={{0,24},{1,7},{2,26},{3,1},{4,28},{5,3},{6,30},{7,5},{8,0},{9,15},{... | collective-permute-start | bytes 786440 | tf_op jit(solution)/shard_map/ppermute | solution.py:251
  14.1 1.9 %collective-permute-start.3 = (f32[4,8,2048]{2,1,0:T(8,128)S(1)}, f32[4,8,2048]{2,1,0:T(8,128)S(1)}, u32[]{:S(2)}, u32[]{:S(2)}) collective-permute-start(f32[4,8,2048]{2,1,0:T(8,128)S(1)} %get-tuple-element.30), channel_id=1, source_target_pairs={{0,16},{1,5},{2,18},{3,7},{4,20},{5,1},{6,22},{7,3},{8,24},{9,13},... | collective-permute-start | bytes 786440 | tf_op jit(solution)/shard_map/ppermute | solution.py:251
  16.0 0.0 collective-permute-done.4.received
  16.0 0.1 add_cores.3
  16.1 0.7 %collective-permute-start.5 = (f32[4,8,2048]{2,1,0:T(8,128)S(1)}, f32[4,8,2048]{2,1,0:T(8,128)S(1)}, u32[]{:S(2)}, u32[]{:S(2)}) collective-permute-start(f32[4,8,2048]{2,1,0:T(8,128)S(1)} %get-tuple-element.37), channel_id=1, source_target_pairs={{0,8},{1,3},{2,10},{3,5},{4,12},{5,7},{6,14},{7,1},{8,16},{9,11},{... | collective-permute-start | bytes 786440 | tf_op jit(solution)/shard_map/ppermute | solution.py:251
  16.8 2.6 %collective-permute-start.6 = (f32[4,8,2048]{2,1,0:T(8,128)S(1)}, f32[4,8,2048]{2,1,0:T(8,128)S(1)}, u32[]{:S(2)}, u32[]{:S(2)}) collective-permute-start(f32[4,8,2048]{2,1,0:T(8,128)S(1)} %get-tuple-element.38), channel_id=1, source_target_pairs={{0,24},{1,7},{2,26},{3,1},{4,28},{5,3},{6,30},{7,5},{8,0},{9,15},{... | collective-permute-start | bytes 786440 | tf_op jit(solution)/shard_map/ppermute | solution.py:251
  19.4 0.9 %collective-permute-start.7 = (f32[4,8,2048]{2,1,0:T(8,128)S(1)}, f32[4,8,2048]{2,1,0:T(8,128)S(1)}, u32[]{:S(2)}, u32[]{:S(2)}) collective-permute-start(f32[4,8,2048]{2,1,0:T(8,128)S(1)} %get-tuple-element.39), channel_id=1, source_target_pairs={{0,16},{1,5},{2,18},{3,7},{4,20},{5,1},{6,22},{7,3},{8,24},{9,13},... | collective-permute-start | bytes 786440 | tf_op jit(solution)/shard_map/ppermute | solution.py:251
  20.4 2.1 %collective-permute-done.3.refs_3_ = f32[4,8,2048]{2,1,0:T(8,128)S(1)} collective-permute-done((f32[4,8,2048]{2,1,0:T(8,128)S(1)}, f32[4,8,2048]{2,1,0:T(8,128)S(1)}, u32[]{:S(2)}, u32[]{:S(2)}) %collective-permute-start.3) | collective-permute-done | bytes 262176 | tf_op jit(solution)/shard_map/ppermute | solution.py:251
  22.4 2.7 %collective-permute-done.5.refs_5_ = f32[4,8,2048]{2,1,0:T(8,128)S(1)} collective-permute-done((f32[4,8,2048]{2,1,0:T(8,128)S(1)}, f32[4,8,2048]{2,1,0:T(8,128)S(1)}, u32[]{:S(2)}, u32[]{:S(2)}) %collective-permute-start.5) | collective-permute-done | bytes 262176 | tf_op jit(solution)/shard_map/ppermute | solution.py:251
  25.2 2.8 %collective-permute-done.7.refs_7_ = f32[4,8,2048]{2,1,0:T(8,128)S(1)} collective-permute-done((f32[4,8,2048]{2,1,0:T(8,128)S(1)}, f32[4,8,2048]{2,1,0:T(8,128)S(1)}, u32[]{:S(2)}, u32[]{:S(2)}) %collective-permute-start.7) | collective-permute-done | bytes 262176 | tf_op jit(solution)/shard_map/ppermute | solution.py:251
  28.0 0.1 sum_first_axis.1
  28.1 1.6 %collective-permute-start.8 = (f32[8,4096]{1,0:T(8,128)S(1)}, f32[8,4096]{1,0:T(8,128)S(1)}, u32[]{:S(2)}, u32[]{:S(2)}) collective-permute-start(f32[8,4096]{1,0:T(8,128)S(1)} %get-tuple-element.41), channel_id=1, source_target_pairs={{0,2},{1,9},{2,4},{3,11},{4,6},{5,13},{6,0},{7,15},{8,10},{9,17},{... | collective-permute-start | bytes 393224 | tf_op jit(solution)/shard_map/ppermute | solution.py:251
  29.7 2.9 %collective-permute-start.9 = (f32[8,4096]{1,0:T(8,128)S(1)}, f32[8,4096]{1,0:T(8,128)S(1)}, u32[]{:S(2)}, u32[]{:S(2)}) collective-permute-start(f32[8,4096]{1,0:T(8,128)S(1)} %get-tuple-element.42), channel_id=1, source_target_pairs={{0,4},{1,17},{2,6},{3,19},{4,0},{5,21},{6,2},{7,23},{8,12},{9,25},... | collective-permute-start | bytes 393224 | tf_op jit(solution)/shard_map/ppermute | solution.py:251
  32.6 1.3 %collective-permute-start.10 = (f32[8,4096]{1,0:T(8,128)S(1)}, f32[8,4096]{1,0:T(8,128)S(1)}, u32[]{:S(2)}, u32[]{:S(2)}) collective-permute-start(f32[8,4096]{1,0:T(8,128)S(1)} %get-tuple-element.43), channel_id=1, source_target_pairs={{0,6},{1,25},{2,0},{3,27},{4,2},{5,29},{6,4},{7,31},{8,14},{9,1},{... | collective-permute-start | bytes 393224 | tf_op jit(solution)/shard_map/ppermute | solution.py:251
  34.0 0.4 collective-permute-done.8.b
  34.3 2.6 %collective-permute-done.9.c = f32[8,4096]{1,0:T(8,128)S(1)} collective-permute-done((f32[8,4096]{1,0:T(8,128)S(1)}, f32[8,4096]{1,0:T(8,128)S(1)}, u32[]{:S(2)}, u32[]{:S(2)}) %collective-permute-start.9) | collective-permute-done | bytes 131104 | tf_op jit(solution)/shard_map/ppermute | solution.py:251
  37.0 0.6 collective-permute-done.10.d
  37.6 0.1 sum_second_axis.1.x.a
  37.7 2.0 %collective-permute-start.13 = (f32[64,512]{1,0:T(8,128)S(1)}, f32[64,512]{1,0:T(8,128)S(1)}, u32[]{:S(2)}, u32[]{:S(2)}) collective-permute-start(f32[64,512]{1,0:T(8,128)S(1)} %sum_second_axis.1.x.a), channel_id=1, source_target_pairs={{0,32},{1,33},{2,34},{3,35},{4,36},{5,37},{6,38},{7,39},{8,40},{9,... | collective-permute-start | bytes 393224 | tf_op jit(solution)/shard_map/ppermute | solution.py:251
  39.7 3.6 %collective-permute-start.12 = (f32[64,512]{1,0:T(8,128)S(1)}, f32[64,512]{1,0:T(8,128)S(1)}, u32[]{:S(2)}, u32[]{:S(2)}) collective-permute-start(f32[64,512]{1,0:T(8,128)S(1)} %sum_second_axis.1.x.a), channel_id=1, source_target_pairs={{0,64},{1,65},{2,66},{3,67},{4,68},{5,69},{6,70},{7,71},{8,72},{9,... | collective-permute-start | bytes 393224 | tf_op jit(solution)/shard_map/ppermute | solution.py:251
  43.3 1.0 %collective-permute-start.11 = (f32[64,512]{1,0:T(8,128)S(1)}, f32[64,512]{1,0:T(8,128)S(1)}, u32[]{:S(2)}, u32[]{:S(2)}) collective-permute-start(f32[64,512]{1,0:T(8,128)S(1)} %sum_second_axis.1.x.a), channel_id=1, source_target_pairs={{0,96},{1,97},{2,98},{3,99},{4,100},{5,101},{6,102},{7,103},{8,104... | collective-permute-start | bytes 393224 | tf_op jit(solution)/shard_map/ppermute | solution.py:251
  44.3 1.2 %collective-permute-done.13.d = f32[64,512]{1,0:T(8,128)S(1)} collective-permute-done((f32[64,512]{1,0:T(8,128)S(1)}, f32[64,512]{1,0:T(8,128)S(1)}, u32[]{:S(2)}, u32[]{:S(2)}) %collective-permute-start.13) | collective-permute-done | bytes 131104 | tf_op jit(solution)/shard_map/ppermute | solution.py:251
  45.5 2.1 %collective-permute-done.12.c = f32[64,512]{1,0:T(8,128)S(1)} collective-permute-done((f32[64,512]{1,0:T(8,128)S(1)}, f32[64,512]{1,0:T(8,128)S(1)}, u32[]{:S(2)}, u32[]{:S(2)}) %collective-permute-start.12) | collective-permute-done | bytes 131104 | tf_op jit(solution)/shard_map/ppermute | solution.py:251
  47.6 0.6 collective-permute-done.11.b
  48.2 0.3 gram.1.refs_0_
  48.6 0.1 collective-permute-start.14
  48.7 1.2 %collective-permute-done.14.refs_1_ = f32[64,256]{1,0:T(8,128)S(1)} collective-permute-done((f32[64,256]{1,0:T(8,128)S(1)}, f32[64,256]{1,0:T(8,128)S(1)}, u32[]{:S(2)}, u32[]{:S(2)}) %collective-permute-start.14) | collective-permute-done | bytes 65568 | tf_op jit(solution)/shard_map/ppermute | solution.py:251
  49.9 1.5 %collective-permute-start.15 = (f32[64,256]{1,0:T(8,128)S(1)}, f32[64,256]{1,0:T(8,128)S(1)}, u32[]{:S(2)}, u32[]{:S(2)}) collective-permute-start(f32[64,256]{1,0:T(8,128)S(1)} %get-tuple-element.44.refs_0_), channel_id=1, source_target_pairs={{0,8},{1,17},{2,10},{3,19},{4,12},{5,21},{6,14},{7,23},{8,16},{9,2... | collective-permute-start | bytes 196616 | tf_op jit(solution)/shard_map/ppermute | solution.py:251
  51.5 1.8 %collective-permute-start.16 = (f32[32,256]{1,0:T(8,128)S(1)}, f32[32,256]{1,0:T(8,128)S(1)}, u32[]{:S(2)}, u32[]{:S(2)}) collective-permute-start(f32[32,256]{1,0:T(8,128)S(1)} %get-tuple-element.45), channel_id=1, source_target_pairs={{0,24},{1,25},{2,26},{3,27},{4,28},{5,29},{6,30},{7,31},{8,0},{9,1... | collective-permute-start | bytes 98312 | tf_op jit(solution)/shard_map/ppermute | solution.py:251
  53.2 2.1 %collective-permute-done.16.half = f32[32,256]{1,0:T(8,128)S(1)} collective-permute-done((f32[32,256]{1,0:T(8,128)S(1)}, f32[32,256]{1,0:T(8,128)S(1)}, u32[]{:S(2)}, u32[]{:S(2)}) %collective-permute-start.16) | collective-permute-done | bytes 32800 | tf_op jit(solution)/shard_map/ppermute | solution.py:251
  55.4 0.3 collective-permute-done.15.whole
  55.7 0.1 collective-permute-start.17
  55.8 1.2 %collective-permute-done.17.refs_2_ = f32[64,256]{1,0:T(8,128)S(1)} collective-permute-done((f32[64,256]{1,0:T(8,128)S(1)}, f32[64,256]{1,0:T(8,128)S(1)}, u32[]{:S(2)}, u32[]{:S(2)}) %collective-permute-start.17) | collective-permute-done | bytes 65568 | tf_op jit(solution)/shard_map/ppermute | solution.py:251
  57.0 1.1 %collective-permute-start.18 = (f32[64,256]{1,0:T(8,128)S(1)}, f32[64,256]{1,0:T(8,128)S(1)}, u32[]{:S(2)}, u32[]{:S(2)}) collective-permute-start(f32[64,256]{1,0:T(8,128)S(1)} %get-tuple-element.46), channel_id=1, source_target_pairs={{0,2},{1,5},{2,4},{3,7},{4,6},{5,1},{6,0},{7,3},{8,10},{9,13},{10,... | collective-permute-start | bytes 196616 | tf_op jit(solution)/shard_map/ppermute | solution.py:251
  58.1 2.2 %collective-permute-start.19 = (f32[32,256]{1,0:T(8,128)S(1)}, f32[32,256]{1,0:T(8,128)S(1)}, u32[]{:S(2)}, u32[]{:S(2)}) collective-permute-start(f32[32,256]{1,0:T(8,128)S(1)} %get-tuple-element.47), channel_id=1, source_target_pairs={{0,6},{1,7},{2,0},{3,1},{4,2},{5,3},{6,4},{7,5},{8,14},{9,15},{10,... | collective-permute-start | bytes 98312 | tf_op jit(solution)/shard_map/ppermute | solution.py:251
  60.3 2.0 %collective-permute-done.19.half = f32[32,256]{1,0:T(8,128)S(1)} collective-permute-done((f32[32,256]{1,0:T(8,128)S(1)}, f32[32,256]{1,0:T(8,128)S(1)}, u32[]{:S(2)}, u32[]{:S(2)}) %collective-permute-start.19) | collective-permute-done | bytes 32800 | tf_op jit(solution)/shard_map/ppermute | solution.py:251
  62.3 0.5 collective-permute-done.18.whole
  62.8 0.1 collective-permute-start.20
  62.9 0.7 %copy.6 = f32[64,512]{1,0:T(8,128)} custom-call(f32[64,512]{1,0:T(8,128)S(1)} %sum_second_axis.1.x.a), custom_call_target="tpu_custom_call" | custom-call | tf_op jit(solution)/shard_map/copy/pallas_call | solution.py:210
  63.5 0.6 collective-permute-done.20
  64.1 0.6 add_add_fusion
  (7 shorter events, 0.1 us)
Async XLA Ops:
  6.6 4.1 %collective-permute-start = (f32[4,4,8,2048]{3,2,1,0:T(8,128)S(1)}, f32[4,4,8,2048]{3,2,1,0:T(8,128)S(1)}, u32[]{:S(2)}, u32[]{:S(2)}) collective-permute-start(f32[4,4,8,2048]{3,2,1,0:T(8,128)S(1)} %get-tuple-element.26), channel_id=1, source_target_pairs={{0,1},{1,0},{2,3},{3,2},{4,5},{5,4},{6,7},{7,6},{8,9},{9,8},{10,11... | collective-permute-start | bytes 3145736 | tf_op jit(solution)/shard_map/ppermute | solution.py:251
  10.1 5.9 %collective-permute-start.4 = (f32[4,4,8,2048]{3,2,1,0:T(8,128)S(1)}, f32[4,4,8,2048]{3,2,1,0:T(8,128)S(1)}, u32[]{:S(2)}, u32[]{:S(2)}) collective-permute-start(f32[4,4,8,2048]{3,2,1,0:T(8,128)S(1)} %get-tuple-element.35), channel_id=1, source_target_pairs={{0,1},{1,0},{2,3},{3,2},{4,5},{5,4},{6,7},{7,6},{8,9},{9,8},{10,11... | collective-permute-start | bytes 3145736 | tf_op jit(solution)/shard_map/ppermute | solution.py:251
  10.8 8.6 %collective-permute-start.1 = (f32[4,8,2048]{2,1,0:T(8,128)S(1)}, f32[4,8,2048]{2,1,0:T(8,128)S(1)}, u32[]{:S(2)}, u32[]{:S(2)}) collective-permute-start(f32[4,8,2048]{2,1,0:T(8,128)S(1)} %get-tuple-element.28), channel_id=1, source_target_pairs={{0,8},{1,3},{2,10},{3,5},{4,12},{5,7},{6,14},{7,1},{8,16},{9,11},{... | collective-permute-start | bytes 786440 | tf_op jit(solution)/shard_map/ppermute | solution.py:251
  12.5 7.9 %collective-permute-start.2 = (f32[4,8,2048]{2,1,0:T(8,128)S(1)}, f32[4,8,2048]{2,1,0:T(8,128)S(1)}, u32[]{:S(2)}, u32[]{:S(2)}) collective-permute-start(f32[4,8,2048]{2,1,0:T(8,128)S(1)} %get-tuple-element.29), channel_id=1, source_target_pairs={{0,24},{1,7},{2,26},{3,1},{4,28},{5,3},{6,30},{7,5},{8,0},{9,15},{... | collective-permute-start | bytes 786440 | tf_op jit(solution)/shard_map/ppermute | solution.py:251
  14.1 8.3 %collective-permute-start.3 = (f32[4,8,2048]{2,1,0:T(8,128)S(1)}, f32[4,8,2048]{2,1,0:T(8,128)S(1)}, u32[]{:S(2)}, u32[]{:S(2)}) collective-permute-start(f32[4,8,2048]{2,1,0:T(8,128)S(1)} %get-tuple-element.30), channel_id=1, source_target_pairs={{0,16},{1,5},{2,18},{3,7},{4,20},{5,1},{6,22},{7,3},{8,24},{9,13},... | collective-permute-start | bytes 786440 | tf_op jit(solution)/shard_map/ppermute | solution.py:251
  16.1 9.0 %collective-permute-start.5 = (f32[4,8,2048]{2,1,0:T(8,128)S(1)}, f32[4,8,2048]{2,1,0:T(8,128)S(1)}, u32[]{:S(2)}, u32[]{:S(2)}) collective-permute-start(f32[4,8,2048]{2,1,0:T(8,128)S(1)} %get-tuple-element.37), channel_id=1, source_target_pairs={{0,8},{1,3},{2,10},{3,5},{4,12},{5,7},{6,14},{7,1},{8,16},{9,11},{... | collective-permute-start | bytes 786440 | tf_op jit(solution)/shard_map/ppermute | solution.py:251
  16.8 8.4 %collective-permute-start.6 = (f32[4,8,2048]{2,1,0:T(8,128)S(1)}, f32[4,8,2048]{2,1,0:T(8,128)S(1)}, u32[]{:S(2)}, u32[]{:S(2)}) collective-permute-start(f32[4,8,2048]{2,1,0:T(8,128)S(1)} %get-tuple-element.38), channel_id=1, source_target_pairs={{0,24},{1,7},{2,26},{3,1},{4,28},{5,3},{6,30},{7,5},{8,0},{9,15},{... | collective-permute-start | bytes 786440 | tf_op jit(solution)/shard_map/ppermute | solution.py:251
  19.4 8.5 %collective-permute-start.7 = (f32[4,8,2048]{2,1,0:T(8,128)S(1)}, f32[4,8,2048]{2,1,0:T(8,128)S(1)}, u32[]{:S(2)}, u32[]{:S(2)}) collective-permute-start(f32[4,8,2048]{2,1,0:T(8,128)S(1)} %get-tuple-element.39), channel_id=1, source_target_pairs={{0,16},{1,5},{2,18},{3,7},{4,20},{5,1},{6,22},{7,3},{8,24},{9,13},... | collective-permute-start | bytes 786440 | tf_op jit(solution)/shard_map/ppermute | solution.py:251
  28.1 6.2 %collective-permute-start.8 = (f32[8,4096]{1,0:T(8,128)S(1)}, f32[8,4096]{1,0:T(8,128)S(1)}, u32[]{:S(2)}, u32[]{:S(2)}) collective-permute-start(f32[8,4096]{1,0:T(8,128)S(1)} %get-tuple-element.41), channel_id=1, source_target_pairs={{0,2},{1,9},{2,4},{3,11},{4,6},{5,13},{6,0},{7,15},{8,10},{9,17},{... | collective-permute-start | bytes 393224 | tf_op jit(solution)/shard_map/ppermute | solution.py:251
  29.7 7.2 %collective-permute-start.9 = (f32[8,4096]{1,0:T(8,128)S(1)}, f32[8,4096]{1,0:T(8,128)S(1)}, u32[]{:S(2)}, u32[]{:S(2)}) collective-permute-start(f32[8,4096]{1,0:T(8,128)S(1)} %get-tuple-element.42), channel_id=1, source_target_pairs={{0,4},{1,17},{2,6},{3,19},{4,0},{5,21},{6,2},{7,23},{8,12},{9,25},... | collective-permute-start | bytes 393224 | tf_op jit(solution)/shard_map/ppermute | solution.py:251
  32.6 5.0 %collective-permute-start.10 = (f32[8,4096]{1,0:T(8,128)S(1)}, f32[8,4096]{1,0:T(8,128)S(1)}, u32[]{:S(2)}, u32[]{:S(2)}) collective-permute-start(f32[8,4096]{1,0:T(8,128)S(1)} %get-tuple-element.43), channel_id=1, source_target_pairs={{0,6},{1,25},{2,0},{3,27},{4,2},{5,29},{6,4},{7,31},{8,14},{9,1},{... | collective-permute-start | bytes 393224 | tf_op jit(solution)/shard_map/ppermute | solution.py:251
  37.7 7.8 %collective-permute-start.13 = (f32[64,512]{1,0:T(8,128)S(1)}, f32[64,512]{1,0:T(8,128)S(1)}, u32[]{:S(2)}, u32[]{:S(2)}) collective-permute-start(f32[64,512]{1,0:T(8,128)S(1)} %sum_second_axis.1.x.a), channel_id=1, source_target_pairs={{0,32},{1,33},{2,34},{3,35},{4,36},{5,37},{6,38},{7,39},{8,40},{9,... | collective-permute-start | bytes 393224 | tf_op jit(solution)/shard_map/ppermute | solution.py:251
  39.7 7.9 %collective-permute-start.12 = (f32[64,512]{1,0:T(8,128)S(1)}, f32[64,512]{1,0:T(8,128)S(1)}, u32[]{:S(2)}, u32[]{:S(2)}) collective-permute-start(f32[64,512]{1,0:T(8,128)S(1)} %sum_second_axis.1.x.a), channel_id=1, source_target_pairs={{0,64},{1,65},{2,66},{3,67},{4,68},{5,69},{6,70},{7,71},{8,72},{9,... | collective-permute-start | bytes 393224 | tf_op jit(solution)/shard_map/ppermute | solution.py:251
  43.3 5.0 %collective-permute-start.11 = (f32[64,512]{1,0:T(8,128)S(1)}, f32[64,512]{1,0:T(8,128)S(1)}, u32[]{:S(2)}, u32[]{:S(2)}) collective-permute-start(f32[64,512]{1,0:T(8,128)S(1)} %sum_second_axis.1.x.a), channel_id=1, source_target_pairs={{0,96},{1,97},{2,98},{3,99},{4,100},{5,101},{6,102},{7,103},{8,104... | collective-permute-start | bytes 393224 | tf_op jit(solution)/shard_map/ppermute | solution.py:251
  48.6 1.3 %collective-permute-start.14 = (f32[64,256]{1,0:T(8,128)S(1)}, f32[64,256]{1,0:T(8,128)S(1)}, u32[]{:S(2)}, u32[]{:S(2)}) collective-permute-start(f32[64,256]{1,0:T(8,128)S(1)} %gram.1.refs_0_), channel_id=1, source_target_pairs={{0,1},{1,0},{2,3},{3,2},{4,5},{5,4},{6,7},{7,6},{8,9},{9,8},{10,11... | collective-permute-start | bytes 196616 | tf_op jit(solution)/shard_map/ppermute | solution.py:251
  49.9 5.7 %collective-permute-start.15 = (f32[64,256]{1,0:T(8,128)S(1)}, f32[64,256]{1,0:T(8,128)S(1)}, u32[]{:S(2)}, u32[]{:S(2)}) collective-permute-start(f32[64,256]{1,0:T(8,128)S(1)} %get-tuple-element.44.refs_0_), channel_id=1, source_target_pairs={{0,8},{1,17},{2,10},{3,19},{4,12},{5,21},{6,14},{7,23},{8,16},{9,2... | collective-permute-start | bytes 196616 | tf_op jit(solution)/shard_map/ppermute | solution.py:251
  51.5 3.9 %collective-permute-start.16 = (f32[32,256]{1,0:T(8,128)S(1)}, f32[32,256]{1,0:T(8,128)S(1)}, u32[]{:S(2)}, u32[]{:S(2)}) collective-permute-start(f32[32,256]{1,0:T(8,128)S(1)} %get-tuple-element.45), channel_id=1, source_target_pairs={{0,24},{1,25},{2,26},{3,27},{4,28},{5,29},{6,30},{7,31},{8,0},{9,1... | collective-permute-start | bytes 98312 | tf_op jit(solution)/shard_map/ppermute | solution.py:251
  55.7 1.3 %collective-permute-start.17 = (f32[64,256]{1,0:T(8,128)S(1)}, f32[64,256]{1,0:T(8,128)S(1)}, u32[]{:S(2)}, u32[]{:S(2)}) collective-permute-start(f32[64,256]{1,0:T(8,128)S(1)} %hear.2.refs_1_), channel_id=1, source_target_pairs={{0,1},{1,0},{2,3},{3,2},{4,5},{5,4},{6,7},{7,6},{8,9},{9,8},{10,11... | collective-permute-start | bytes 196616 | tf_op jit(solution)/shard_map/ppermute | solution.py:251
  57.0 5.7 %collective-permute-start.18 = (f32[64,256]{1,0:T(8,128)S(1)}, f32[64,256]{1,0:T(8,128)S(1)}, u32[]{:S(2)}, u32[]{:S(2)}) collective-permute-start(f32[64,256]{1,0:T(8,128)S(1)} %get-tuple-element.46), channel_id=1, source_target_pairs={{0,2},{1,5},{2,4},{3,7},{4,6},{5,1},{6,0},{7,3},{8,10},{9,13},{10,... | collective-permute-start | bytes 196616 | tf_op jit(solution)/shard_map/ppermute | solution.py:251
  58.1 4.2 %collective-permute-start.19 = (f32[32,256]{1,0:T(8,128)S(1)}, f32[32,256]{1,0:T(8,128)S(1)}, u32[]{:S(2)}, u32[]{:S(2)}) collective-permute-start(f32[32,256]{1,0:T(8,128)S(1)} %get-tuple-element.47), channel_id=1, source_target_pairs={{0,6},{1,7},{2,0},{3,1},{4,2},{5,3},{6,4},{7,5},{8,14},{9,15},{10,... | collective-permute-start | bytes 98312 | tf_op jit(solution)/shard_map/ppermute | solution.py:251
  62.8 1.3 %collective-permute-start.20 = (f32[64,256]{1,0:T(8,128)S(1)}, f32[64,256]{1,0:T(8,128)S(1)}, u32[]{:S(2)}, u32[]{:S(2)}) collective-permute-start(f32[64,256]{1,0:T(8,128)S(1)} %hear.3), channel_id=1, source_target_pairs={{0,1},{1,0},{2,3},{3,2},{4,5},{5,4},{6,7},{7,6},{8,9},{9,8},{10,11... | collective-permute-start | bytes 196616 | tf_op jit(solution)/shard_map/ppermute | solution.py:251

commit v7 on v6

--- a/solution.py
+++ b/solution.py
@@ -75,7 +75,7 @@
     w3[256:384, :] = lo
 
     load(1).start()
-    for off, ahead in enumerate(((2, 3), (4, 5), (6,), ())):
+    for off, ahead in enumerate(((2, 3), (4, 5, 6), (), ())):
         load(off).wait()
         for n in ahead:
             load(n).start()
@@ -303,7 +303,7 @@
 
 def plane_total(part):
     terms = (part, send(part, other_core))
-    for along_x in (1, 0):
+    for along_x in (0, 1):
 
         def whole(z, x, y, c):
             step = 1 + c

time: 66 us -> 66 us (level)
  no operation moved by 1% of the time
where the time goes in v7:
time: 66 us; the launch traced here: 64.8 us
  starting transfers between devices  29.4 us (45%)
  waiting for transfers between devices  23.1 us (35%)
  Pallas kernels  10.9 us (17%)
  between operations  0.73 us (1%)
    ppermute x21, starting transfers between devices, send(): return lax.ppermute(x, AXES, pairs(target))  29.4 us
    ppermute x21, waiting for transfers between devices, send(): return lax.ppermute(x, AXES, pairs(target))  23.1 us
    pallas_call x1, Pallas kernels, project(): pl.pallas_call(first_part_kernel, out_shape=(parts[0], parts[0], jax.Shap...  6 us
    pallas_call x1, Pallas kernels, project(): pl.pallas_call(second_part_kernel, out_shape=(parts[1], parts[1]), in_spe...  3.4 us
  transfers between devices with their start and end apart: 21, of which 16 were waited for; matrix products, arithmetic and copies ran while one was open for 0% of the time, Pallas kernels for 7%

profile of v7, /device:TPU:0, one launch (start us, length us, event | category | flops | bytes accessed | tf_op | source)
XLA Modules:
  0.0 64.8 jit_solution(12632298985389272887)
XLA Ops:
  0.6 6.0 %project_first_part.1 = (f32[4,4,8,2048]{3,2,1,0:T(8,128)S(1)}, f32[4,4,8,2048]{3,2,1,0:T(8,128)S(1)}, f32[3,2,8,2,64,256]{5,4,3,2,1,0:T(8,128)S(1)}, bf16[512,256]{1,0:T(8,128)(2,1)S(1)}, bf16[384,128]{1,0:T(8,128)(2,1)S(1)}) custom-call(f32[4,2,16,2,64,256]{5,4,3,2,1,0:T(8,128)} %bitcast.2, f32[64,256]{1,0:T(8,128)} %bitcast.4, f32[64,64]{1,0:T(8,128)} %b3_in.1), custom_call_target="tpu_custom_call" | custom-call | flops 8000000000 | bytes 8388608 | tf_op jit(solution)/shard_map/project_first_part/pallas_call | solution.py:108
  6.6 0.1 collective-permute-start
  6.7 3.4 %project_second_part.1 = (f32[4,4,8,2048]{3,2,1,0:T(8,128)S(1)}, f32[4,4,8,2048]{3,2,1,0:T(8,128)S(1)}) custom-call(f32[4,2,16,2,64,256]{5,4,3,2,1,0:T(8,128)} %bitcast.3, f32[3,2,8,2,64,256]{5,4,3,2,1,0:T(8,128)S(1)} %get-tuple-element.31.early, bf16[512,256]{1,0:T(8,128)(2,1)S(1)} %get-tuple-element.32.w2, bf16[384,128]{1,0:T(8,128)(2,1)S(1)} %get-tuple-element.33.w3), custom_call_target="tpu_custom_call" | custom-call | flops 8000000000 | bytes 8388608 | tf_op jit(solution)/shard_map/project_second_part/pallas_call | solution.py:131
  10.1 0.6 collective-permute-start.4
  10.7 0.1 add_cores.2
  10.8 1.6 %collective-permute-start.1 = (f32[4,8,2048]{2,1,0:T(8,128)S(1)}, f32[4,8,2048]{2,1,0:T(8,128)S(1)}, u32[]{:S(2)}, u32[]{:S(2)}) collective-permute-start(f32[4,8,2048]{2,1,0:T(8,128)S(1)} %get-tuple-element.28), channel_id=1, source_target_pairs={{0,8},{1,3},{2,10},{3,5},{4,12},{5,7},{6,14},{7,1},{8,16},{9,11},{... | collective-permute-start | bytes 786440 | tf_op jit(solution)/shard_map/ppermute | solution.py:251
  12.5 1.7 %collective-permute-start.2 = (f32[4,8,2048]{2,1,0:T(8,128)S(1)}, f32[4,8,2048]{2,1,0:T(8,128)S(1)}, u32[]{:S(2)}, u32[]{:S(2)}) collective-permute-start(f32[4,8,2048]{2,1,0:T(8,128)S(1)} %get-tuple-element.29), channel_id=1, source_target_pairs={{0,24},{1,7},{2,26},{3,1},{4,28},{5,3},{6,30},{7,5},{8,0},{9,15},{... | collective-permute-start | bytes 786440 | tf_op jit(solution)/shard_map/ppermute | solution.py:251
  14.1 1.9 %collective-permute-start.3 = (f32[4,8,2048]{2,1,0:T(8,128)S(1)}, f32[4,8,2048]{2,1,0:T(8,128)S(1)}, u32[]{:S(2)}, u32[]{:S(2)}) collective-permute-start(f32[4,8,2048]{2,1,0:T(8,128)S(1)} %get-tuple-element.30), channel_id=1, source_target_pairs={{0,16},{1,5},{2,18},{3,7},{4,20},{5,1},{6,22},{7,3},{8,24},{9,13},... | collective-permute-start | bytes 786440 | tf_op jit(solution)/shard_map/ppermute | solution.py:251
  16.0 0.0 collective-permute-done.4.received
  16.0 0.1 add_cores.3
  16.1 0.7 %collective-permute-start.5 = (f32[4,8,2048]{2,1,0:T(8,128)S(1)}, f32[4,8,2048]{2,1,0:T(8,128)S(1)}, u32[]{:S(2)}, u32[]{:S(2)}) collective-permute-start(f32[4,8,2048]{2,1,0:T(8,128)S(1)} %get-tuple-element.37), channel_id=1, source_target_pairs={{0,8},{1,3},{2,10},{3,5},{4,12},{5,7},{6,14},{7,1},{8,16},{9,11},{... | collective-permute-start | bytes 786440 | tf_op jit(solution)/shard_map/ppermute | solution.py:251
  16.8 2.6 %collective-permute-start.6 = (f32[4,8,2048]{2,1,0:T(8,128)S(1)}, f32[4,8,2048]{2,1,0:T(8,128)S(1)}, u32[]{:S(2)}, u32[]{:S(2)}) collective-permute-start(f32[4,8,2048]{2,1,0:T(8,128)S(1)} %get-tuple-element.38), channel_id=1, source_target_pairs={{0,24},{1,7},{2,26},{3,1},{4,28},{5,3},{6,30},{7,5},{8,0},{9,15},{... | collective-permute-start | bytes 786440 | tf_op jit(solution)/shard_map/ppermute | solution.py:251
  19.4 0.0 collective-permute-done.1.refs_1_
  19.4 0.9 %collective-permute-start.7 = (f32[4,8,2048]{2,1,0:T(8,128)S(1)}, f32[4,8,2048]{2,1,0:T(8,128)S(1)}, u32[]{:S(2)}, u32[]{:S(2)}) collective-permute-start(f32[4,8,2048]{2,1,0:T(8,128)S(1)} %get-tuple-element.39), channel_id=1, source_target_pairs={{0,16},{1,5},{2,18},{3,7},{4,20},{5,1},{6,22},{7,3},{8,24},{9,13},... | collective-permute-start | bytes 786440 | tf_op jit(solution)/shard_map/ppermute | solution.py:251
  20.4 2.1 %collective-permute-done.3.refs_3_ = f32[4,8,2048]{2,1,0:T(8,128)S(1)} collective-permute-done((f32[4,8,2048]{2,1,0:T(8,128)S(1)}, f32[4,8,2048]{2,1,0:T(8,128)S(1)}, u32[]{:S(2)}, u32[]{:S(2)}) %collective-permute-start.3) | collective-permute-done | bytes 262176 | tf_op jit(solution)/shard_map/ppermute | solution.py:251
  22.5 2.7 %collective-permute-done.5.refs_5_ = f32[4,8,2048]{2,1,0:T(8,128)S(1)} collective-permute-done((f32[4,8,2048]{2,1,0:T(8,128)S(1)}, f32[4,8,2048]{2,1,0:T(8,128)S(1)}, u32[]{:S(2)}, u32[]{:S(2)}) %collective-permute-start.5) | collective-permute-done | bytes 262176 | tf_op jit(solution)/shard_map/ppermute | solution.py:251
  25.2 2.8 %collective-permute-done.7.refs_7_ = f32[4,8,2048]{2,1,0:T(8,128)S(1)} collective-permute-done((f32[4,8,2048]{2,1,0:T(8,128)S(1)}, f32[4,8,2048]{2,1,0:T(8,128)S(1)}, u32[]{:S(2)}, u32[]{:S(2)}) %collective-permute-start.7) | collective-permute-done | bytes 262176 | tf_op jit(solution)/shard_map/ppermute | solution.py:251
  28.0 0.1 sum_first_axis.1
  28.1 1.6 %collective-permute-start.8 = (f32[8,4096]{1,0:T(8,128)S(1)}, f32[8,4096]{1,0:T(8,128)S(1)}, u32[]{:S(2)}, u32[]{:S(2)}) collective-permute-start(f32[8,4096]{1,0:T(8,128)S(1)} %get-tuple-element.41), channel_id=1, source_target_pairs={{0,2},{1,9},{2,4},{3,11},{4,6},{5,13},{6,0},{7,15},{8,10},{9,17},{... | collective-permute-start | bytes 393224 | tf_op jit(solution)/shard_map/ppermute | solution.py:251
  29.7 2.9 %collective-permute-start.9 = (f32[8,4096]{1,0:T(8,128)S(1)}, f32[8,4096]{1,0:T(8,128)S(1)}, u32[]{:S(2)}, u32[]{:S(2)}) collective-permute-start(f32[8,4096]{1,0:T(8,128)S(1)} %get-tuple-element.42), channel_id=1, source_target_pairs={{0,4},{1,17},{2,6},{3,19},{4,0},{5,21},{6,2},{7,23},{8,12},{9,25},... | collective-permute-start | bytes 393224 | tf_op jit(solution)/shard_map/ppermute | solution.py:251
  32.6 1.3 %collective-permute-start.10 = (f32[8,4096]{1,0:T(8,128)S(1)}, f32[8,4096]{1,0:T(8,128)S(1)}, u32[]{:S(2)}, u32[]{:S(2)}) collective-permute-start(f32[8,4096]{1,0:T(8,128)S(1)} %get-tuple-element.43), channel_id=1, source_target_pairs={{0,6},{1,25},{2,0},{3,27},{4,2},{5,29},{6,4},{7,31},{8,14},{9,1},{... | collective-permute-start | bytes 393224 | tf_op jit(solution)/shard_map/ppermute | solution.py:251
  34.0 0.4 collective-permute-done.8.b
  34.3 2.6 %collective-permute-done.9.c = f32[8,4096]{1,0:T(8,128)S(1)} collective-permute-done((f32[8,4096]{1,0:T(8,128)S(1)}, f32[8,4096]{1,0:T(8,128)S(1)}, u32[]{:S(2)}, u32[]{:S(2)}) %collective-permute-start.9) | collective-permute-done | bytes 131104 | tf_op jit(solution)/shard_map/ppermute | solution.py:251
  37.0 0.6 collective-permute-done.10.d
  37.6 0.1 sum_second_axis.1.x.a
  37.7 2.0 %collective-permute-start.13 = (f32[64,512]{1,0:T(8,128)S(1)}, f32[64,512]{1,0:T(8,128)S(1)}, u32[]{:S(2)}, u32[]{:S(2)}) collective-permute-start(f32[64,512]{1,0:T(8,128)S(1)} %sum_second_axis.1.x.a), channel_id=1, source_target_pairs={{0,32},{1,33},{2,34},{3,35},{4,36},{5,37},{6,38},{7,39},{8,40},{9,... | collective-permute-start | bytes 393224 | tf_op jit(solution)/shard_map/ppermute | solution.py:251
  39.7 3.6 %collective-permute-start.12 = (f32[64,512]{1,0:T(8,128)S(1)}, f32[64,512]{1,0:T(8,128)S(1)}, u32[]{:S(2)}, u32[]{:S(2)}) collective-permute-start(f32[64,512]{1,0:T(8,128)S(1)} %sum_second_axis.1.x.a), channel_id=1, source_target_pairs={{0,64},{1,65},{2,66},{3,67},{4,68},{5,69},{6,70},{7,71},{8,72},{9,... | collective-permute-start | bytes 393224 | tf_op jit(solution)/shard_map/ppermute | solution.py:251
  43.3 1.0 %collective-permute-start.11 = (f32[64,512]{1,0:T(8,128)S(1)}, f32[64,512]{1,0:T(8,128)S(1)}, u32[]{:S(2)}, u32[]{:S(2)}) collective-permute-start(f32[64,512]{1,0:T(8,128)S(1)} %sum_second_axis.1.x.a), channel_id=1, source_target_pairs={{0,96},{1,97},{2,98},{3,99},{4,100},{5,101},{6,102},{7,103},{8,104... | collective-permute-start | bytes 393224 | tf_op jit(solution)/shard_map/ppermute | solution.py:251
  44.3 1.2 %collective-permute-done.13.d = f32[64,512]{1,0:T(8,128)S(1)} collective-permute-done((f32[64,512]{1,0:T(8,128)S(1)}, f32[64,512]{1,0:T(8,128)S(1)}, u32[]{:S(2)}, u32[]{:S(2)}) %collective-permute-start.13) | collective-permute-done | bytes 131104 | tf_op jit(solution)/shard_map/ppermute | solution.py:251
  45.5 2.1 %collective-permute-done.12.c = f32[64,512]{1,0:T(8,128)S(1)} collective-permute-done((f32[64,512]{1,0:T(8,128)S(1)}, f32[64,512]{1,0:T(8,128)S(1)}, u32[]{:S(2)}, u32[]{:S(2)}) %collective-permute-start.12) | collective-permute-done | bytes 131104 | tf_op jit(solution)/shard_map/ppermute | solution.py:251
  47.6 0.6 collective-permute-done.11.b
  48.3 0.3 gram.1.refs_0_
  48.6 0.1 collective-permute-start.14
  48.7 1.2 %collective-permute-done.14.refs_1_ = f32[64,256]{1,0:T(8,128)S(1)} collective-permute-done((f32[64,256]{1,0:T(8,128)S(1)}, f32[64,256]{1,0:T(8,128)S(1)}, u32[]{:S(2)}, u32[]{:S(2)}) %collective-permute-start.14) | collective-permute-done | bytes 65568 | tf_op jit(solution)/shard_map/ppermute | solution.py:251
  50.0 1.1 %collective-permute-start.15 = (f32[64,256]{1,0:T(8,128)S(1)}, f32[64,256]{1,0:T(8,128)S(1)}, u32[]{:S(2)}, u32[]{:S(2)}) collective-permute-start(f32[64,256]{1,0:T(8,128)S(1)} %get-tuple-element.44.refs_0_), channel_id=1, source_target_pairs={{0,2},{1,5},{2,4},{3,7},{4,6},{5,1},{6,0},{7,3},{8,10},{9,13},{10,... | collective-permute-start | bytes 196616 | tf_op jit(solution)/shard_map/ppermute | solution.py:251
  51.0 2.2 %collective-permute-start.16 = (f32[32,256]{1,0:T(8,128)S(1)}, f32[32,256]{1,0:T(8,128)S(1)}, u32[]{:S(2)}, u32[]{:S(2)}) collective-permute-start(f32[32,256]{1,0:T(8,128)S(1)} %get-tuple-element.45), channel_id=1, source_target_pairs={{0,6},{1,7},{2,0},{3,1},{4,2},{5,3},{6,4},{7,5},{8,14},{9,15},{10,... | collective-permute-start | bytes 98312 | tf_op jit(solution)/shard_map/ppermute | solution.py:251
  53.3 2.0 %collective-permute-done.16.half = f32[32,256]{1,0:T(8,128)S(1)} collective-permute-done((f32[32,256]{1,0:T(8,128)S(1)}, f32[32,256]{1,0:T(8,128)S(1)}, u32[]{:S(2)}, u32[]{:S(2)}) %collective-permute-start.16) | collective-permute-done | bytes 32800 | tf_op jit(solution)/shard_map/ppermute | solution.py:251
  55.2 0.5 collective-permute-done.15.whole
  55.7 0.1 collective-permute-start.17
  55.8 1.2 %collective-permute-done.17.refs_2_ = f32[64,256]{1,0:T(8,128)S(1)} collective-permute-done((f32[64,256]{1,0:T(8,128)S(1)}, f32[64,256]{1,0:T(8,128)S(1)}, u32[]{:S(2)}, u32[]{:S(2)}) %collective-permute-start.17) | collective-permute-done | bytes 65568 | tf_op jit(solution)/shard_map/ppermute | solution.py:251
  57.1 1.5 %collective-permute-start.18 = (f32[64,256]{1,0:T(8,128)S(1)}, f32[64,256]{1,0:T(8,128)S(1)}, u32[]{:S(2)}, u32[]{:S(2)}) collective-permute-start(f32[64,256]{1,0:T(8,128)S(1)} %get-tuple-element.46), channel_id=1, source_target_pairs={{0,8},{1,17},{2,10},{3,19},{4,12},{5,21},{6,14},{7,23},{8,16},{9,2... | collective-permute-start | bytes 196616 | tf_op jit(solution)/shard_map/ppermute | solution.py:251
  58.6 1.8 %collective-permute-start.19 = (f32[32,256]{1,0:T(8,128)S(1)}, f32[32,256]{1,0:T(8,128)S(1)}, u32[]{:S(2)}, u32[]{:S(2)}) collective-permute-start(f32[32,256]{1,0:T(8,128)S(1)} %get-tuple-element.47), channel_id=1, source_target_pairs={{0,24},{1,25},{2,26},{3,27},{4,28},{5,29},{6,30},{7,31},{8,0},{9,1... | collective-permute-start | bytes 98312 | tf_op jit(solution)/shard_map/ppermute | solution.py:251
  60.4 2.1 %collective-permute-done.19.half = f32[32,256]{1,0:T(8,128)S(1)} collective-permute-done((f32[32,256]{1,0:T(8,128)S(1)}, f32[32,256]{1,0:T(8,128)S(1)}, u32[]{:S(2)}, u32[]{:S(2)}) %collective-permute-start.19) | collective-permute-done | bytes 32800 | tf_op jit(solution)/shard_map/ppermute | solution.py:251
  62.5 0.3 collective-permute-done.18.whole
  62.8 0.1 collective-permute-start.20
  62.9 0.7 %copy.6 = f32[64,512]{1,0:T(8,128)} custom-call(f32[64,512]{1,0:T(8,128)S(1)} %sum_second_axis.1.x.a), custom_call_target="tpu_custom_call" | custom-call | tf_op jit(solution)/shard_map/copy/pallas_call | solution.py:210
  63.6 0.6 collective-permute-done.20
  64.1 0.6 add_add_fusion
  (7 shorter events, 0.1 us)
Async XLA Ops:
  6.6 4.1 %collective-permute-start = (f32[4,4,8,2048]{3,2,1,0:T(8,128)S(1)}, f32[4,4,8,2048]{3,2,1,0:T(8,128)S(1)}, u32[]{:S(2)}, u32[]{:S(2)}) collective-permute-start(f32[4,4,8,2048]{3,2,1,0:T(8,128)S(1)} %get-tuple-element.26), channel_id=1, source_target_pairs={{0,1},{1,0},{2,3},{3,2},{4,5},{5,4},{6,7},{7,6},{8,9},{9,8},{10,11... | collective-permute-start | bytes 3145736 | tf_op jit(solution)/shard_map/ppermute | solution.py:251
  10.1 5.9 %collective-permute-start.4 = (f32[4,4,8,2048]{3,2,1,0:T(8,128)S(1)}, f32[4,4,8,2048]{3,2,1,0:T(8,128)S(1)}, u32[]{:S(2)}, u32[]{:S(2)}) collective-permute-start(f32[4,4,8,2048]{3,2,1,0:T(8,128)S(1)} %get-tuple-element.35), channel_id=1, source_target_pairs={{0,1},{1,0},{2,3},{3,2},{4,5},{5,4},{6,7},{7,6},{8,9},{9,8},{10,11... | collective-permute-start | bytes 3145736 | tf_op jit(solution)/shard_map/ppermute | solution.py:251
  10.8 8.6 %collective-permute-start.1 = (f32[4,8,2048]{2,1,0:T(8,128)S(1)}, f32[4,8,2048]{2,1,0:T(8,128)S(1)}, u32[]{:S(2)}, u32[]{:S(2)}) collective-permute-start(f32[4,8,2048]{2,1,0:T(8,128)S(1)} %get-tuple-element.28), channel_id=1, source_target_pairs={{0,8},{1,3},{2,10},{3,5},{4,12},{5,7},{6,14},{7,1},{8,16},{9,11},{... | collective-permute-start | bytes 786440 | tf_op jit(solution)/shard_map/ppermute | solution.py:251
  12.5 7.9 %collective-permute-start.2 = (f32[4,8,2048]{2,1,0:T(8,128)S(1)}, f32[4,8,2048]{2,1,0:T(8,128)S(1)}, u32[]{:S(2)}, u32[]{:S(2)}) collective-permute-start(f32[4,8,2048]{2,1,0:T(8,128)S(1)} %get-tuple-element.29), channel_id=1, source_target_pairs={{0,24},{1,7},{2,26},{3,1},{4,28},{5,3},{6,30},{7,5},{8,0},{9,15},{... | collective-permute-start | bytes 786440 | tf_op jit(solution)/shard_map/ppermute | solution.py:251
  14.1 8.3 %collective-permute-start.3 = (f32[4,8,2048]{2,1,0:T(8,128)S(1)}, f32[4,8,2048]{2,1,0:T(8,128)S(1)}, u32[]{:S(2)}, u32[]{:S(2)}) collective-permute-start(f32[4,8,2048]{2,1,0:T(8,128)S(1)} %get-tuple-element.30), channel_id=1, source_target_pairs={{0,16},{1,5},{2,18},{3,7},{4,20},{5,1},{6,22},{7,3},{8,24},{9,13},... | collective-permute-start | bytes 786440 | tf_op jit(solution)/shard_map/ppermute | solution.py:251
  16.1 9.0 %collective-permute-start.5 = (f32[4,8,2048]{2,1,0:T(8,128)S(1)}, f32[4,8,2048]{2,1,0:T(8,128)S(1)}, u32[]{:S(2)}, u32[]{:S(2)}) collective-permute-start(f32[4,8,2048]{2,1,0:T(8,128)S(1)} %get-tuple-element.37), channel_id=1, source_target_pairs={{0,8},{1,3},{2,10},{3,5},{4,12},{5,7},{6,14},{7,1},{8,16},{9,11},{... | collective-permute-start | bytes 786440 | tf_op jit(solution)/shard_map/ppermute | solution.py:251
  16.8 8.4 %collective-permute-start.6 = (f32[4,8,2048]{2,1,0:T(8,128)S(1)}, f32[4,8,2048]{2,1,0:T(8,128)S(1)}, u32[]{:S(2)}, u32[]{:S(2)}) collective-permute-start(f32[4,8,2048]{2,1,0:T(8,128)S(1)} %get-tuple-element.38), channel_id=1, source_target_pairs={{0,24},{1,7},{2,26},{3,1},{4,28},{5,3},{6,30},{7,5},{8,0},{9,15},{... | collective-permute-start | bytes 786440 | tf_op jit(solution)/shard_map/ppermute | solution.py:251
  19.4 8.5 %collective-permute-start.7 = (f32[4,8,2048]{2,1,0:T(8,128)S(1)}, f32[4,8,2048]{2,1,0:T(8,128)S(1)}, u32[]{:S(2)}, u32[]{:S(2)}) collective-permute-start(f32[4,8,2048]{2,1,0:T(8,128)S(1)} %get-tuple-element.39), channel_id=1, source_target_pairs={{0,16},{1,5},{2,18},{3,7},{4,20},{5,1},{6,22},{7,3},{8,24},{9,13},... | collective-permute-start | bytes 786440 | tf_op jit(solution)/shard_map/ppermute | solution.py:251
  28.1 6.2 %collective-permute-start.8 = (f32[8,4096]{1,0:T(8,128)S(1)}, f32[8,4096]{1,0:T(8,128)S(1)}, u32[]{:S(2)}, u32[]{:S(2)}) collective-permute-start(f32[8,4096]{1,0:T(8,128)S(1)} %get-tuple-element.41), channel_id=1, source_target_pairs={{0,2},{1,9},{2,4},{3,11},{4,6},{5,13},{6,0},{7,15},{8,10},{9,17},{... | collective-permute-start | bytes 393224 | tf_op jit(solution)/shard_map/ppermute | solution.py:251
  29.7 7.2 %collective-permute-start.9 = (f32[8,4096]{1,0:T(8,128)S(1)}, f32[8,4096]{1,0:T(8,128)S(1)}, u32[]{:S(2)}, u32[]{:S(2)}) collective-permute-start(f32[8,4096]{1,0:T(8,128)S(1)} %get-tuple-element.42), channel_id=1, source_target_pairs={{0,4},{1,17},{2,6},{3,19},{4,0},{5,21},{6,2},{7,23},{8,12},{9,25},... | collective-permute-start | bytes 393224 | tf_op jit(solution)/shard_map/ppermute | solution.py:251
  32.6 5.0 %collective-permute-start.10 = (f32[8,4096]{1,0:T(8,128)S(1)}, f32[8,4096]{1,0:T(8,128)S(1)}, u32[]{:S(2)}, u32[]{:S(2)}) collective-permute-start(f32[8,4096]{1,0:T(8,128)S(1)} %get-tuple-element.43), channel_id=1, source_target_pairs={{0,6},{1,25},{2,0},{3,27},{4,2},{5,29},{6,4},{7,31},{8,14},{9,1},{... | collective-permute-start | bytes 393224 | tf_op jit(solution)/shard_map/ppermute | solution.py:251
  37.7 7.8 %collective-permute-start.13 = (f32[64,512]{1,0:T(8,128)S(1)}, f32[64,512]{1,0:T(8,128)S(1)}, u32[]{:S(2)}, u32[]{:S(2)}) collective-permute-start(f32[64,512]{1,0:T(8,128)S(1)} %sum_second_axis.1.x.a), channel_id=1, source_target_pairs={{0,32},{1,33},{2,34},{3,35},{4,36},{5,37},{6,38},{7,39},{8,40},{9,... | collective-permute-start | bytes 393224 | tf_op jit(solution)/shard_map/ppermute | solution.py:251
  39.7 7.9 %collective-permute-start.12 = (f32[64,512]{1,0:T(8,128)S(1)}, f32[64,512]{1,0:T(8,128)S(1)}, u32[]{:S(2)}, u32[]{:S(2)}) collective-permute-start(f32[64,512]{1,0:T(8,128)S(1)} %sum_second_axis.1.x.a), channel_id=1, source_target_pairs={{0,64},{1,65},{2,66},{3,67},{4,68},{5,69},{6,70},{7,71},{8,72},{9,... | collective-permute-start | bytes 393224 | tf_op jit(solution)/shard_map/ppermute | solution.py:251
  43.3 5.0 %collective-permute-start.11 = (f32[64,512]{1,0:T(8,128)S(1)}, f32[64,512]{1,0:T(8,128)S(1)}, u32[]{:S(2)}, u32[]{:S(2)}) collective-permute-start(f32[64,512]{1,0:T(8,128)S(1)} %sum_second_axis.1.x.a), channel_id=1, source_target_pairs={{0,96},{1,97},{2,98},{3,99},{4,100},{5,101},{6,102},{7,103},{8,104... | collective-permute-start | bytes 393224 | tf_op jit(solution)/shard_map/ppermute | solution.py:251
  48.6 1.3 %collective-permute-start.14 = (f32[64,256]{1,0:T(8,128)S(1)}, f32[64,256]{1,0:T(8,128)S(1)}, u32[]{:S(2)}, u32[]{:S(2)}) collective-permute-start(f32[64,256]{1,0:T(8,128)S(1)} %gram.1.refs_0_), channel_id=1, source_target_pairs={{0,1},{1,0},{2,3},{3,2},{4,5},{5,4},{6,7},{7,6},{8,9},{9,8},{10,11... | collective-permute-start | bytes 196616 | tf_op jit(solution)/shard_map/ppermute | solution.py:251
  50.0 5.7 %collective-permute-start.15 = (f32[64,256]{1,0:T(8,128)S(1)}, f32[64,256]{1,0:T(8,128)S(1)}, u32[]{:S(2)}, u32[]{:S(2)}) collective-permute-start(f32[64,256]{1,0:T(8,128)S(1)} %get-tuple-element.44.refs_0_), channel_id=1, source_target_pairs={{0,2},{1,5},{2,4},{3,7},{4,6},{5,1},{6,0},{7,3},{8,10},{9,13},{10,... | collective-permute-start | bytes 196616 | tf_op jit(solution)/shard_map/ppermute | solution.py:251
  51.0 4.2 %collective-permute-start.16 = (f32[32,256]{1,0:T(8,128)S(1)}, f32[32,256]{1,0:T(8,128)S(1)}, u32[]{:S(2)}, u32[]{:S(2)}) collective-permute-start(f32[32,256]{1,0:T(8,128)S(1)} %get-tuple-element.45), channel_id=1, source_target_pairs={{0,6},{1,7},{2,0},{3,1},{4,2},{5,3},{6,4},{7,5},{8,14},{9,15},{10,... | collective-permute-start | bytes 98312 | tf_op jit(solution)/shard_map/ppermute | solution.py:251
  55.7 1.3 %collective-permute-start.17 = (f32[64,256]{1,0:T(8,128)S(1)}, f32[64,256]{1,0:T(8,128)S(1)}, u32[]{:S(2)}, u32[]{:S(2)}) collective-permute-start(f32[64,256]{1,0:T(8,128)S(1)} %hear.2.refs_1_), channel_id=1, source_target_pairs={{0,1},{1,0},{2,3},{3,2},{4,5},{5,4},{6,7},{7,6},{8,9},{9,8},{10,11... | collective-permute-start | bytes 196616 | tf_op jit(solution)/shard_map/ppermute | solution.py:251
  57.1 5.7 %collective-permute-start.18 = (f32[64,256]{1,0:T(8,128)S(1)}, f32[64,256]{1,0:T(8,128)S(1)}, u32[]{:S(2)}, u32[]{:S(2)}) collective-permute-start(f32[64,256]{1,0:T(8,128)S(1)} %get-tuple-element.46), channel_id=1, source_target_pairs={{0,8},{1,17},{2,10},{3,19},{4,12},{5,21},{6,14},{7,23},{8,16},{9,2... | collective-permute-start | bytes 196616 | tf_op jit(solution)/shard_map/ppermute | solution.py:251
  58.6 3.9 %collective-permute-start.19 = (f32[32,256]{1,0:T(8,128)S(1)}, f32[32,256]{1,0:T(8,128)S(1)}, u32[]{:S(2)}, u32[]{:S(2)}) collective-permute-start(f32[32,256]{1,0:T(8,128)S(1)} %get-tuple-element.47), channel_id=1, source_target_pairs={{0,24},{1,25},{2,26},{3,27},{4,28},{5,29},{6,30},{7,31},{8,0},{9,1... | collective-permute-start | bytes 98312 | tf_op jit(solution)/shard_map/ppermute | solution.py:251
  62.8 1.3 %collective-permute-start.20 = (f32[64,256]{1,0:T(8,128)S(1)}, f32[64,256]{1,0:T(8,128)S(1)}, u32[]{:S(2)}, u32[]{:S(2)}) collective-permute-start(f32[64,256]{1,0:T(8,128)S(1)} %hear.3), channel_id=1, source_target_pairs={{0,1},{1,0},{2,3},{3,2},{4,5},{5,4},{6,7},{7,6},{8,9},{9,8},{10,11... | collective-permute-start | bytes 196616 | tf_op jit(solution)/shard_map/ppermute | solution.py:251
